TPU v7x, 256 devices: a whole 4x4x8 slice. The times are simulated.
256 devices in a mesh: dom: 16 (over x, y), depth: 16 (over z, core).
Axes of the slice: x: 4, y: 4, z: 8, core: 2. Of those that a mesh axis runs over, the one named last changes fastest.
Arguments:
- head: float32 [16, 1024, 512], P('depth', 'dom'), may hold values from -1.5 to 0.3
- water_prev: float32 [16, 1024, 512], P('depth', 'dom'), may hold values from 0.05 to 0.4
- alpha: float32 [16, 1024, 512], P('depth', 'dom'), may hold values from 0.3 to 3
- shape_n: float32 [16, 1024, 512], P('depth', 'dom'), may hold values from 1.3 to 3
- theta_r: float32 [16, 1024, 512], P('depth', 'dom'), may hold values from 0.02 to 0.1
- theta_s: float32 [16, 1024, 512], P('depth', 'dom'), may hold values from 0.35 to 0.5
- sat_cond: float32 [16, 1024, 512], P('depth', 'dom'), may hold values from 0.5 to 5
- refine: int32 [1024], P('dom'), may hold values from 0 to 8
- destination: int32 [1024], P('dom'), may hold values from 0 to 1023, as said below
- neighbours: int32 [1024, 4, 4], P('dom'), may hold values from -1 to 1023, as said below
Outputs:
- new_head: float32 [16, 1024, 512], P('depth', 'dom')
- residual: float32 [16, 1024, 512], P('depth', 'dom')
Inputs may be any that keep to these rules, and one draw needn't show every extreme that they name: destination is a permutation of the 1024 positions, position p on device p // 64. The blocks of each device go to exactly 8 other devices, exactly 4 to each; its other blocks stay on it. neighbours[p, f] lists the new positions beyond lateral face f of new block p: all four entries -1 where there is no neighbour; one block in entry 0 and -1 in the rest for a face of equal size; or four finer blocks, entry (a // 4) * 2 + b // 4 for face cell (a, b). Every listed block lies at most 16 positions from p, some at exactly 16.
All inputs are finite; a program needn't handle non-finite values.
Results may differ from a plain program's by a relative error of at most 0.0003.
Values sent between devices are 32-bit elements; how exact they have to be, the bound alone decides.
No kernel may reach another device: no remote copies, remote signals or barrier semaphores. Data moves between devices by JAX's collectives and lax.ppermute only.
A program may use at most 128 MiB of HBM per device.

v0:
```python
import jax
import jax.numpy as jnp
import numpy as np
from jax import lax
from jax.sharding import PartitionSpec as P

inv_step = 4.0
exact = lax.Precision.HIGHEST


def with_halo(x, sides, width):
    for axis, dim in sides:
        peers, length = (lax.axis_size(axis), x.shape[dim])
        up = [(i, (i + 1) % peers) for i in range(peers - 1)]
        down = [(j, i) for i, j in up]
        last = lax.slice_in_dim(x, length - width, length, axis=dim)
        initial = lax.slice_in_dim(x, 0, width, axis=dim)
        before = lax.ppermute(last, axis, up)
        after = lax.ppermute(initial, axis, down)
        x = jnp.concatenate([before, x, after], axis=dim)
    return x


def axis_table(stride, bit, smooth):
    table = np.zeros((512, 512), np.float32)
    for cell in range(512):
        fine = cell // stride % 8
        base = cell - fine * stride
        half = fine // 2
        if smooth:
            if fine % 2 == 0:
                table[base + max(4 * bit + half - 1, 0) * stride, cell] += 0.25
                table[base + (4 * bit + half) * stride, cell] += 0.75
            else:
                table[base + (4 * bit + half) * stride, cell] += 0.75
                table[base + min(4 * bit + half + 1, 7) * stride, cell] += 0.25
        else:
            table[base + (4 * bit + half) * stride, cell] = 1.0
    return table


def face_cells(face):
    listed = []
    for first in range(8):
        for second in range(8):
            if face == 0:
                listed.append(first * 8 + second)
            elif face == 1:
                listed.append(448 + first * 8 + second)
            elif face == 2:
                listed.append(first * 64 + second)
            else:
                listed.append(first * 64 + 56 + second)
    return listed


def plane_cells(level_k):
    return [first * 64 + second * 8 + level_k for first in range(8) for second in range(8)]


def take_faces(offset_k):
    table = np.zeros((512, 512), np.float32)
    for face in range(4):
        for spot, cell in enumerate(face_cells(face)):
            table[cell, face * 128 + offset_k + spot] = 1.0
    return table


def take_plane(level_k, offset_k):
    table = np.zeros((512, 128), np.float32)
    for spot, cell in enumerate(plane_cells(level_k)):
        table[cell, offset_k + spot] = 1.0
    return table


def put_cells(listed):
    table = np.zeros((64, 512), np.float32)
    for spot, cell in enumerate(listed):
        table[spot, cell] = 1.0
    return table


def quarter_tables():
    table = np.zeros((4, 4, 128, 128), np.float32)
    for part_k in range(2):
        for first in range(8):
            for second in range(8):
                quarter = first // 4 * 2 + second // 4
                for pair in range(4):
                    source = (
                        part_k * 64
                        + (2 * (first % 4) + pair // 2) * 8
                        + 2 * (second % 4)
                        + pair % 2
                    )
                    table[pair, quarter, source, part_k * 64 + first * 8 + second] = 1.0
    return table


def interior_mask(stride, upward):
    cells = np.arange(512)
    index = cells // stride % 8
    return index < 7 if upward else index > 0


def select(values, table):
    return jnp.einsum("...c,cd->...d", values, jnp.asarray(table), precision=exact)


def adapt(fields, flags, smooth):
    octant = jnp.maximum(flags - 1, 0)
    current = fields
    for stride, bits in ((64, octant // 4), (8, octant // 2 % 2), (1, octant % 2)):
        first = select(current, axis_table(stride, 0, smooth))
        second = select(current, axis_table(stride, 1, smooth))
        current = jnp.where((bits == 1).reshape(1, -1, 1), second, first)
    return jnp.where((flags == 0).reshape(1, -1, 1), fields, current)


def closure(head_cell, cell_alpha, cell_shape, cell_resid, cell_sat, cell_cond):
    expo = 1.0 - 1.0 / cell_shape
    ratio = jnp.power(cell_alpha * jnp.maximum(-head_cell, 0.0), cell_shape)
    saturation = jnp.power(1.0 + ratio, -expo)
    water = cell_resid + (cell_sat - cell_resid) * saturation
    inner = 1.0 - jnp.power(ratio / (1.0 + ratio), expo)
    conduct = cell_cond * jnp.sqrt(saturation) * inner * inner
    return (water, conduct)


def ghost_values(wide, table_nb):
    rows = wide.reshape(-1, 128)
    safe = jnp.maximum(table_nb, 0)
    opposite = jnp.array([1, 0, 3, 2], jnp.int32).reshape(1, 4, 1)
    picked = rows[safe * 4 + opposite]
    conform = picked[:, :, 0]
    tables = quarter_tables()
    terms = [
        jnp.einsum("bfex,exy->bfy", picked, jnp.asarray(tables[pair]), precision=exact)
        for pair in range(4)
    ]
    hanging = 0.25 * (terms[0] + terms[1] + terms[2] + terms[3])
    count = jnp.sum((table_nb >= 0).astype(jnp.int32), axis=2)
    value = jnp.where((count == 4)[:, :, None], hanging, conform)
    present = (count > 0).astype(jnp.float32)
    return (value, present)


def moved_by(values, stride, upward):
    blocks = values.shape[0]
    empty = jnp.zeros((blocks, stride), values.dtype)
    if upward:
        return jnp.concatenate([values[:, stride:], empty], axis=1)
    return jnp.concatenate([empty, values[:, : 512 - stride]], axis=1)


def balance(
    head_cell,
    water,
    conduct,
    prior,
    cell_alpha,
    cell_resid,
    cell_sat,
    lat_value,
    lat_on,
    below,
    above,
    low_on,
    high_on,
):
    plans = []
    for face, stride, upward in ((0, 64, False), (1, 64, True), (2, 8, False), (3, 8, True)):
        cells_table = put_cells(face_cells(face))
        plans.append(
            (
                select(lat_value[:, face, :64], cells_table),
                select(lat_value[:, face, 64:], cells_table),
                lat_on[:, face : face + 1],
                stride,
                upward,
                0.0,
            )
        )
    low_table = put_cells(plane_cells(0))
    high_table = put_cells(plane_cells(7))
    plans.append(
        (select(below[:, :64], low_table), select(below[:, 64:], low_table), low_on, 1, False, -1.0)
    )
    plans.append(
        (
            select(above[:, :64], high_table),
            select(above[:, 64:], high_table),
            high_on,
            1,
            True,
            1.0,
        )
    )
    flux = jnp.zeros_like(head_cell)
    total = jnp.zeros_like(head_cell)
    for ghost_h, ghost_k, plane_on, stride, upward, lift in plans:
        inside = jnp.asarray(interior_mask(stride, upward)).reshape(1, 512)
        near_h = jnp.where(inside, moved_by(head_cell, stride, upward), ghost_h)
        near_k = jnp.where(inside, moved_by(conduct, stride, upward), ghost_k)
        near_on = jnp.where(inside, 1.0, plane_on * jnp.ones_like(head_cell))
        face_k = near_on * 0.5 * (conduct + near_k)
        flux = flux + face_k * (near_h - head_cell + lift)
        total = total + face_k
    resid = inv_step * (water - prior) - flux
    diagonal = inv_step * (cell_sat - cell_resid) * cell_alpha + total
    return (resid, diagonal)


def relocate(stacked, destination):
    fields, blocks, cells = stacked.shape
    peers = lax.axis_size("dom")
    rank_me = lax.axis_index("dom")
    room = blocks // 16
    owner = destination // blocks
    spot = destination % blocks
    remote = owner != rank_me
    picked = ((owner[:, None] == jnp.arange(peers)[None, :]) & remote[:, None]).astype(jnp.int32)
    order = jnp.sum(jnp.cumsum(picked, axis=0) * picked, axis=1) - 1
    slot = jnp.where(remote, owner * room + order, peers * room)
    packed = (
        jnp.zeros((fields, peers * room + 1, cells), stacked.dtype)
        .at[:, slot]
        .set(stacked)[:, : peers * room]
    )
    places = jnp.full((1, peers * room + 1), -1, jnp.int32).at[0, slot].set(spot)[:, : peers * room]
    packed, places = (
        lax.all_to_all(packed, "dom", split_axis=1, concat_axis=1, tiled=True),
        lax.all_to_all(places, "dom", split_axis=1, concat_axis=1, tiled=True),
    )
    target = jnp.concatenate(
        [jnp.where(remote, blocks, spot), jnp.where(places[0] >= 0, places[0], blocks)]
    )
    values = jnp.concatenate([stacked, packed], axis=1)
    return (
        jnp.zeros((fields, blocks + 1, cells), stacked.dtype).at[:, target].set(values)[:, :blocks]
    )


def evaluate(
    head_cell,
    prior,
    cell_alpha,
    cell_shape,
    cell_resid,
    cell_sat,
    cell_cond,
    local_nb,
    low_on,
    high_on,
    reach,
):
    water, conduct = closure(head_cell, cell_alpha, cell_shape, cell_resid, cell_sat, cell_cond)
    faces = select(head_cell, take_faces(0)) + select(conduct, take_faces(64))
    wide = with_halo(faces, (("dom", 0),), reach)
    lat_value, lat_on = ghost_values(wide, local_nb)
    bottom = select(head_cell, take_plane(0, 0)) + select(conduct, take_plane(0, 64))
    top = select(head_cell, take_plane(7, 0)) + select(conduct, take_plane(7, 64))
    tall = with_halo(jnp.stack([bottom, top]), (("depth", 0),), 1)
    return balance(
        head_cell,
        water,
        conduct,
        prior,
        cell_alpha,
        cell_resid,
        cell_sat,
        lat_value,
        lat_on,
        tall[0],
        tall[3],
        low_on,
        high_on,
    )


def on_device(
    head, water_prev, alpha, shape_n, theta_r, theta_s, sat_cond, refine, destination, neighbours
):
    blocks = head.shape[1]
    smooth_part = adapt(jnp.concatenate([head, water_prev], axis=0), refine, True)
    plain_part = adapt(
        jnp.concatenate([alpha, shape_n, theta_r, theta_s, sat_cond], axis=0), refine, False
    )
    settled = relocate(jnp.concatenate([smooth_part, plain_part], axis=0), destination)
    start, prior, cell_alpha, cell_shape, cell_resid, cell_sat, cell_cond = [
        settled[number] for number in range(7)
    ]
    level = lax.axis_index("depth")
    low_on = (level > 0).astype(jnp.float32)
    high_on = (level < lax.axis_size("depth") - 1).astype(jnp.float32)
    reach = blocks // 4
    offset = lax.axis_index("dom") * blocks - reach
    local_nb = jnp.where(neighbours >= 0, neighbours - offset, -1)
    resid, diagonal = evaluate(
        start,
        prior,
        cell_alpha,
        cell_shape,
        cell_resid,
        cell_sat,
        cell_cond,
        local_nb,
        low_on,
        high_on,
        reach,
    )
    new_head = start - resid / diagonal
    final, unused = evaluate(
        new_head,
        prior,
        cell_alpha,
        cell_shape,
        cell_resid,
        cell_sat,
        cell_cond,
        local_nb,
        low_on,
        high_on,
        reach,
    )
    return (new_head[None], final[None])


def solution(mesh):
    placed = (
        P("depth", "dom", None),
        P("depth", "dom", None),
        P("depth", "dom", None),
        P("depth", "dom", None),
        P("depth", "dom", None),
        P("depth", "dom", None),
        P("depth", "dom", None),
        P("dom"),
        P("dom"),
        P("dom", None, None),
    )
    return jax.shard_map(
        on_device,
        mesh=mesh,
        in_specs=placed,
        out_specs=(P("depth", "dom", None), P("depth", "dom", None)),
        check_vma=False,
    )
```

profile of v0, /device:TPU:99, one launch (start us, length us, event | category | flops | bytes accessed | tf_op | source)
XLA Modules:
  0.0 139.3 jit_solution(13650349103853694307)
XLA Ops:
  0.6 0.8 select_bitcast_fusion
  1.8 0.8 scatter_custom_fusion
  3.3 6.9 %all-to-all-start = ((s32[1,16,4]{2,0,1:T(1,128)}), s32[1,16,4]{2,0,1:T(1,128)S(1)}, u32[]{:S(2)}, u32[]{:S(2)}) async-start(s32[1,16,4]{2,0,1:T(1,128)} %bitcast.2), calls=%async_computation | async-start | bytes 16384 | tf_op jit(solution)/shard_map/all_to_all | solution.py:233
  10.9 0.9 constant_dynamic-update-slice_fusion.6
  11.8 1.0 constant_dynamic-update-slice_fusion.1
  12.8 0.9 constant_dynamic-update-slice_fusion.5
  13.7 0.9 constant_dynamic-update-slice_fusion.4
  14.6 0.9 constant_dynamic-update-slice_fusion.3
  15.6 0.9 constant_dynamic-update-slice_fusion.2
  16.5 1.2 fusion.132
  17.8 1.3 convolution_select_fusion.2
  19.1 1.2 fusion.133
  20.3 1.3 convolution_select_fusion.1
  21.6 1.2 fusion.134
  22.9 0.7 fusion.129
  23.7 0.7 convolution_select_fusion.5
  25.2 0.7 convolution_select_fusion.4
  26.6 1.3 fusion
  27.9 0.7 fusion.1
  30.1 2.6 %scatter_fusion = f32[7,65,512]{2,0,1:T(8,128)S(1)} fusion(f32[7,65,512]{2,0,1:T(8,128)S(1)} %broadcast.217.clone, s32[64]{0:T(128)S(1)} %compare_select_fusion.3, f32[64,7,512]{2,1,0:T(8,128)S(1)} %copy.110), kind=kCustom, calls=%fused_computation.3 | custom fusion | bytes 2752768 | tf_op jit(solution)/shard_map/scatter | solution.py:228
  32.7 1.1 slice.286
  33.8 6.7 %all-to-all-start.1 = ((f32[7,64,512]{2,0,1:T(8,128)}), f32[7,64,512]{2,0,1:T(8,128)S(1)}, u32[]{:S(2)}, u32[]{:S(2)}) async-start(f32[7,64,512]{2,0,1:T(8,128)} %slice.286), calls=%async_computation.1 | async-start | bytes 2097152 | tf_op jit(solution)/shard_map/all_to_all | solution.py:232
  42.7 11.2 %all-to-all-done.1 = f32[7,64,512]{2,0,1:T(8,128)S(1)} async-done(((f32[7,64,512]{2,0,1:T(8,128)}), f32[7,64,512]{2,0,1:T(8,128)S(1)}, u32[]{:S(2)}, u32[]{:S(2)}) %all-to-all-start.1) | async-done | bytes 917536 | tf_op jit(solution)/shard_map/all_to_all | solution.py:232
  54.7 1.1 copy.112
  55.9 4.6 %scatter_fusion.1 = f32[7,65,512]{2,0,1:T(8,128)S(1)} fusion(f32[7,65,512]{2,0,1:T(8,128)S(1)} %broadcast.217, s32[128]{0:T(128)S(1)} %fusion.110, f32[128,7,512]{2,1,0:T(8,128)S(1)} %copy.112), kind=kCustom, calls=%fused_computation.4 | custom fusion | bytes 5505536 | tf_op jit(solution)/shard_map/scatter | solution.py:240
  60.5 1.4 fusion.114
  61.9 0.8 multiply_multiply_fusion.1
  62.6 0.9 fusion.122
  63.5 0.9 fusion.124
  64.4 0.9 fusion.127
  65.4 0.8 fusion.135
  66.1 0.8 convolution_add_fusion.1
  66.9 2.2 %collective-permute-start = (f32[16,512]{1,0:T(8,128)S(1)}, f32[16,512]{1,0:T(8,128)S(1)}, u32[]{:S(2)}, u32[]{:S(2)}) collective-permute-start(f32[16,512]{1,0:T(8,128)S(1)} %get-tuple-element.37), channel_id=1, source_target_pairs={{0,16},{16,32},{32,48},{48,64},{64,80},{80,96},{96,112},{112,128},... | collective-permute-start | bytes 98312 | tf_op jit(solution)/shard_map/ppermute | solution.py:18
  69.1 5.2 %collective-permute-start.1 = (f32[16,512]{1,0:T(8,128)S(1)}, f32[16,512]{1,0:T(8,128)S(1)}, u32[]{:S(2)}, u32[]{:S(2)}) collective-permute-start(f32[16,512]{1,0:T(8,128)S(1)} %get-tuple-element.38), channel_id=1, source_target_pairs={{16,0},{32,16},{48,32},{64,48},{80,64},{96,80},{112,96},{128,112},... | collective-permute-start | bytes 98312 | tf_op jit(solution)/shard_map/ppermute | solution.py:19
  74.6 0.9 fusion.82
  75.5 8.3 %collective-permute-start.2 = (f32[1,64,128]{2,1,0:T(8,128)}, f32[1,64,128]{2,1,0:T(8,128)}, u32[]{:S(2)}, u32[]{:S(2)}) collective-permute-start(f32[1,64,128]{2,1,0:T(8,128)} %fusion.82), channel_id=1, source_target_pairs={{0,1},{1,2},{2,3},{3,4},{4,5},{5,6},{6,7},{7,8},{8,9},{9,10},{10,1... | collective-permute-start | bytes 98312 | tf_op jit(solution)/shard_map/ppermute | solution.py:18
  84.1 0.9 fusion.81
  85.0 2.1 %collective-permute-start.3 = (f32[1,64,128]{2,1,0:T(8,128)}, f32[1,64,128]{2,1,0:T(8,128)}, u32[]{:S(2)}, u32[]{:S(2)}) collective-permute-start(f32[1,64,128]{2,1,0:T(8,128)} %fusion.81), channel_id=1, source_target_pairs={{1,0},{2,1},{3,2},{4,3},{5,4},{6,5},{7,6},{8,7},{9,8},{10,9},{11,1... | collective-permute-start | bytes 98312 | tf_op jit(solution)/shard_map/ppermute | solution.py:19
  87.2 2.8 %gather_fusion = f32[1024,128]{1,0:T(8,128)S(1)} fusion(f32[384,128]{1,0:T(8,128)S(1)} %reshape.135, s32[1024]{0:T(1024)S(1)} %broadcast_clamp_fusion), kind=kCustom, calls=%fused_computation | custom fusion | bytes 1052672 | tf_op jit(solution)/shard_map/gather | solution.py:134
  90.2 1.7 %convolution_bitcast_fusion.4 = f32[64,4,128]{2,0,1:T(8,128)S(1)} fusion(f32[4,128,128,1]{2,1,0,3:T(8,128)} %constant.309, f32[64,4,4,128]{3,2,1,0:T(4,128)S(1)} %bitcast.312), kind=kOutput, calls=%fused_computation.18 | convolution fusion | flops 201326592 | bytes 917504 | tf_op jit(solution)/shard_map/bfex,exy->bfy/dot_general | solution.py:138
  96.2 1.1 fusion.27
  97.3 1.0 fusion.30
  98.4 1.1 fusion.32
  99.5 1.0 fusion.35
  101.0 1.4 %multiply_multiply_fusion = (f32[64,512]{1,0:T(8,128)S(1)}, f32[64,512]{1,0:T(8,128)S(1)}) fusion(f32[1,64,512]{2,0,1:T(1,128)S(1)} %copy-done.19, f32[1,64,512]{2,0,1:T(1,128)S(1)} %copy-done.11, f32[1,64,512]{2,0,1:T(1,128)S(1)} %copy-done.14, f32[64,512]{1,0:T(8,128)S(1)} %get-tuple-element.3, f32[64,512]{1,0:T(8,128)S(1)} %fusion.32, ...), kind=kOutput, calls=%fused_computation.144 | convolution fusion | flops 26476544 | bytes 2916864 | tf_op jit(solution)/shard_map/...c,cd->...d/dot_general | solution.py:107
  102.4 0.8 fusion.138
  103.2 0.8 fusion.116
  103.9 0.8 fusion.118
  104.7 0.8 fusion.115
  105.4 0.8 fusion.117
  106.6 0.8 fusion.120
  107.6 0.8 convolution_add_fusion
  108.4 1.9 %collective-permute-start.4 = (f32[16,512]{1,0:T(8,128)S(1)}, f32[16,512]{1,0:T(8,128)S(1)}, u32[]{:S(2)}, u32[]{:S(2)}) collective-permute-start(f32[16,512]{1,0:T(8,128)S(1)} %get-tuple-element.23), channel_id=1, source_target_pairs={{0,16},{16,32},{32,48},{48,64},{64,80},{80,96},{96,112},{112,128},... | collective-permute-start | bytes 98312 | tf_op jit(solution)/shard_map/ppermute | solution.py:18
  110.3 5.5 %collective-permute-start.5 = (f32[16,512]{1,0:T(8,128)S(1)}, f32[16,512]{1,0:T(8,128)S(1)}, u32[]{:S(2)}, u32[]{:S(2)}) collective-permute-start(f32[16,512]{1,0:T(8,128)S(1)} %get-tuple-element.24), channel_id=1, source_target_pairs={{16,0},{32,16},{48,32},{64,48},{80,64},{96,80},{112,96},{128,112},... | collective-permute-start | bytes 98312 | tf_op jit(solution)/shard_map/ppermute | solution.py:19
  115.8 0.9 fusion.80
  116.7 5.4 %collective-permute-start.6 = (f32[1,64,128]{2,1,0:T(8,128)}, f32[1,64,128]{2,1,0:T(8,128)}, u32[]{:S(2)}, u32[]{:S(2)}) collective-permute-start(f32[1,64,128]{2,1,0:T(8,128)} %fusion.80), channel_id=1, source_target_pairs={{0,1},{1,2},{2,3},{3,4},{4,5},{5,6},{6,7},{7,8},{8,9},{9,10},{10,1... | collective-permute-start | bytes 98312 | tf_op jit(solution)/shard_map/ppermute | solution.py:18
  122.1 0.9 fusion.79
  123.0 2.2 %collective-permute-start.7 = (f32[1,64,128]{2,1,0:T(8,128)}, f32[1,64,128]{2,1,0:T(8,128)}, u32[]{:S(2)}, u32[]{:S(2)}) collective-permute-start(f32[1,64,128]{2,1,0:T(8,128)} %fusion.79), channel_id=1, source_target_pairs={{1,0},{2,1},{3,2},{4,3},{5,4},{6,5},{7,6},{8,7},{9,8},{10,9},{11,1... | collective-permute-start | bytes 98312 | tf_op jit(solution)/shard_map/ppermute | solution.py:19
  125.3 2.8 %gather_fusion.1 = f32[1024,128]{1,0:T(8,128)S(1)} fusion(f32[384,128]{1,0:T(8,128)S(1)} %reshape.136, s32[1024]{0:T(1024)S(1)} %broadcast_clamp_fusion), kind=kCustom, calls=%fused_computation.1 | custom fusion | bytes 1052672 | tf_op jit(solution)/shard_map/gather | solution.py:134
  133.2 1.0 fusion.63
  134.3 1.1 fusion.61
  135.7 1.0 fusion.68
  136.7 1.1 fusion.66
  137.9 1.4 %fusion.45 = f32[1,64,512]{2,1,0:T(8,128)} fusion(f32[64,512]{1,0:T(8,128)S(1)} %fusion.66, f32[64,512]{1,0:T(8,128)S(1)} %fusion.61, f32[64,512]{1,0:T(8,128)S(1)} %fusion.57, f32[64,512]{1,0:T(8,128)S(1)} %fusion.53, f32[64,512]{1,0:T(8,128)S(1)} %fusion.49, f32[64,512]{1,0:T(8,128)S(1)} %fusion.46, f32[64,512]{1,0:T(8,128)S(1)} %get-tuple-element.55, ...), kind=kOutput, calls=%fused_computation.91 | convolution fusion | flops 25952256 | bytes 2130944 | tf_op jit(solution)/shard_map/...c,cd->...d/dot_general | solution.py:107
  (268 shorter events, 18.5 us)
Async XLA Ops:
  0.6 15.9 %copy-start.44 = (f32[512,512,1]{1,0,2:T(8,128)S(1)}, f32[512,512,1]{1,0,2:T(8,128)}, u32[]{:S(2)}) copy-start(f32[512,512,1]{1,0,2:T(8,128)} %constant.300) | copy-start | bytes 3145732
  3.3 30.5 %all-to-all-start = ((s32[1,16,4]{2,0,1:T(1,128)}), s32[1,16,4]{2,0,1:T(1,128)S(1)}, u32[]{:S(2)}, u32[]{:S(2)}) async-start(s32[1,16,4]{2,0,1:T(1,128)} %bitcast.2), calls=%async_computation | async-start | bytes 16384 | tf_op jit(solution)/shard_map/all_to_all | solution.py:233
  11.8 6.0 %copy-start.27 = (f32[512,512,1]{1,0,2:T(8,128)S(1)}, f32[512,512,1]{1,0,2:T(8,128)}, u32[]{:S(2)}) copy-start(f32[512,512,1]{1,0,2:T(8,128)} %constant.301) | copy-start | bytes 3145732
  30.0 2.7 %copy-start.75 = (pred[512]{0:T(512)(128)(4,1)S(1)}, pred[512]{0:T(512)(128)(4,1)}, u32[]{:S(2)}) copy-start(pred[512]{0:T(512)(128)(4,1)} %constant.232.clone) | copy-start | bytes 1540
  32.7 7.7 %copy-start.74 = (pred[512]{0:T(512)(128)(4,1)S(1)}, pred[512]{0:T(512)(128)(4,1)}, u32[]{:S(2)}) copy-start(pred[512]{0:T(512)(128)(4,1)} %constant.233.clone) | copy-start | bytes 1540
  33.8 20.1 %all-to-all-start.1 = ((f32[7,64,512]{2,0,1:T(8,128)}), f32[7,64,512]{2,0,1:T(8,128)S(1)}, u32[]{:S(2)}, u32[]{:S(2)}) async-start(f32[7,64,512]{2,0,1:T(8,128)} %slice.286), calls=%async_computation.1 | async-start | bytes 2097152 | tf_op jit(solution)/shard_map/all_to_all | solution.py:232
  61.9 3.4 %copy-start.10 = (f32[1,64,512]{2,0,1:T(1,128)}, f32[1,64,512]{2,0,1:T(1,128)S(1)}, u32[]{:S(2)}) copy-start(f32[1,64,512]{2,0,1:T(1,128)S(1)} %get-tuple-element.9) | copy-start | bytes 393220
  61.9 3.4 %copy-start.13 = (f32[1,64,512]{2,0,1:T(1,128)}, f32[1,64,512]{2,0,1:T(1,128)S(1)}, u32[]{:S(2)}) copy-start(f32[1,64,512]{2,0,1:T(1,128)S(1)} %get-tuple-element.10) | copy-start | bytes 393220
  61.9 3.4 %copy-start.18 = (f32[1,64,512]{2,0,1:T(1,128)}, f32[1,64,512]{2,0,1:T(1,128)S(1)}, u32[]{:S(2)}) copy-start(f32[1,64,512]{2,0,1:T(1,128)S(1)} %get-tuple-element.14) | copy-start | bytes 393220
  61.9 3.4 %copy-start.1 = (f32[512,512]{1,0:T(8,128)S(1)}, f32[512,512]{1,0:T(8,128)}, u32[]{:S(2)}) copy-start(f32[512,512]{1,0:T(8,128)} %constant.211.clone) | copy-start | bytes 3145732
  63.5 2.6 %copy-start.2 = (f32[512,512]{1,0:T(8,128)S(1)}, f32[512,512]{1,0:T(8,128)}, u32[]{:S(2)}) copy-start(f32[512,512]{1,0:T(8,128)} %constant.212.clone) | copy-start | bytes 3145732
  64.4 9.9 %copy-start.48 = (f32[512,128]{1,0:T(8,128)S(1)}, f32[512,128]{1,0:T(8,128)}, u32[]{:S(2)}) copy-start(f32[512,128]{1,0:T(8,128)} %constant.220.clone) | copy-start | bytes 786436
  65.3 9.3 %copy-start.35 = (f32[512,128]{1,0:T(8,128)S(1)}, f32[512,128]{1,0:T(8,128)}, u32[]{:S(2)}) copy-start(f32[512,128]{1,0:T(8,128)} %constant.221.clone) | copy-start | bytes 786436
  65.3 18.5 %copy-start.46 = (f32[512,128]{1,0:T(8,128)S(1)}, f32[512,128]{1,0:T(8,128)}, u32[]{:S(2)}) copy-start(f32[512,128]{1,0:T(8,128)} %constant.218.clone) | copy-start | bytes 786436
  65.4 18.7 %copy-start.33 = (f32[512,128]{1,0:T(8,128)S(1)}, f32[512,128]{1,0:T(8,128)}, u32[]{:S(2)}) copy-start(f32[512,128]{1,0:T(8,128)} %constant.219.clone) | copy-start | bytes 786436
  66.9 20.2 %collective-permute-start = (f32[16,512]{1,0:T(8,128)S(1)}, f32[16,512]{1,0:T(8,128)S(1)}, u32[]{:S(2)}, u32[]{:S(2)}) collective-permute-start(f32[16,512]{1,0:T(8,128)S(1)} %get-tuple-element.37), channel_id=1, source_target_pairs={{0,16},{16,32},{32,48},{48,64},{64,80},{80,96},{96,112},{112,128},... | collective-permute-start | bytes 98312 | tf_op jit(solution)/shard_map/ppermute | solution.py:18
  69.1 18.0 %collective-permute-start.1 = (f32[16,512]{1,0:T(8,128)S(1)}, f32[16,512]{1,0:T(8,128)S(1)}, u32[]{:S(2)}, u32[]{:S(2)}) collective-permute-start(f32[16,512]{1,0:T(8,128)S(1)} %get-tuple-element.38), channel_id=1, source_target_pairs={{16,0},{32,16},{48,32},{64,48},{80,64},{96,80},{112,96},{128,112},... | collective-permute-start | bytes 98312 | tf_op jit(solution)/shard_map/ppermute | solution.py:19
  75.5 20.7 %collective-permute-start.2 = (f32[1,64,128]{2,1,0:T(8,128)}, f32[1,64,128]{2,1,0:T(8,128)}, u32[]{:S(2)}, u32[]{:S(2)}) collective-permute-start(f32[1,64,128]{2,1,0:T(8,128)} %fusion.82), channel_id=1, source_target_pairs={{0,1},{1,2},{2,3},{3,4},{4,5},{5,6},{6,7},{7,8},{8,9},{9,10},{10,1... | collective-permute-start | bytes 98312 | tf_op jit(solution)/shard_map/ppermute | solution.py:18
  85.0 13.4 %collective-permute-start.3 = (f32[1,64,128]{2,1,0:T(8,128)}, f32[1,64,128]{2,1,0:T(8,128)}, u32[]{:S(2)}, u32[]{:S(2)}) collective-permute-start(f32[1,64,128]{2,1,0:T(8,128)} %fusion.81), channel_id=1, source_target_pairs={{1,0},{2,1},{3,2},{4,3},{5,4},{6,5},{7,6},{8,7},{9,8},{10,9},{11,1... | collective-permute-start | bytes 98312 | tf_op jit(solution)/shard_map/ppermute | solution.py:19
  87.2 4.6 %copy-start.30 = (f32[4,128,128,1]{2,1,0,3:T(8,128)S(1)}, f32[4,128,128,1]{2,1,0,3:T(8,128)}, u32[]{:S(2)}) copy-start(f32[4,128,128,1]{2,1,0,3:T(8,128)} %constant.308) | copy-start | bytes 786436
  90.0 2.5 %copy-start.28 = (f32[4,128,128,1]{2,1,0,3:T(8,128)S(1)}, f32[4,128,128,1]{2,1,0,3:T(8,128)}, u32[]{:S(2)}) copy-start(f32[4,128,128,1]{2,1,0,3:T(8,128)} %constant.307) | copy-start | bytes 786436
  90.0 3.3 %copy-start.51 = (f32[4,128,128,1]{2,1,0,3:T(8,128)S(1)}, f32[4,128,128,1]{2,1,0,3:T(8,128)}, u32[]{:S(2)}) copy-start(f32[4,128,128,1]{2,1,0,3:T(8,128)} %constant.306) | copy-start | bytes 786436
  90.1 3.3 %copy-start.87 = (pred[64,4]{0,1:T(4,128)(4,1)S(1)}, pred[64,4]{0,1:T(4,128)(4,1)}, u32[]{:S(2)}) copy-start(pred[64,4]{0,1:T(4,128)(4,1)} %get-tuple-element.49) | copy-start | bytes 772
  91.9 2.6 %copy-start.70 = (f32[64,448]{1,0:T(8,128)S(1)}, f32[64,448]{1,0:T(8,128)}, u32[]{:S(2)}) copy-start(f32[64,448]{1,0:T(8,128)} %get-tuple-element.30) | copy-start | bytes 344068
  94.5 2.9 %copy-start.68 = (f32[64,511]{1,0:T(8,128)S(1)}, f32[64,511]{1,0:T(8,128)}, u32[]{:S(2)}) copy-start(f32[64,511]{1,0:T(8,128)} %get-tuple-element.39) | copy-start | bytes 392452
  94.8 3.6 %copy-start.3 = (f32[64,512]{1,0:T(8,128)S(1)}, f32[64,512]{1,0:T(8,128)}, u32[]{:S(2)}) copy-start(f32[64,512]{1,0:T(8,128)} %constant.227.clone) | copy-start | bytes 393220
  94.8 3.6 %copy-start.62 = (f32[64,511]{1,0:T(8,128)S(1)}, f32[64,511]{1,0:T(8,128)}, u32[]{:S(2)}) copy-start(f32[64,511]{1,0:T(8,128)} %get-tuple-element.61) | copy-start | bytes 392452
  95.1 4.3 %copy-start.67 = (f32[64,511]{1,0:T(8,128)S(1)}, f32[64,511]{1,0:T(8,128)}, u32[]{:S(2)}) copy-start(f32[64,511]{1,0:T(8,128)} %get-tuple-element.40) | copy-start | bytes 392452
  95.5 5.1 %copy-start.16 = (f32[64,512]{1,0:T(8,128)S(1)}, f32[64,512]{1,0:T(8,128)}, u32[]{:S(2)}) copy-start(f32[64,512]{1,0:T(8,128)} %constant.222.clone) | copy-start | bytes 393220
  95.5 5.1 %copy-start.57 = (f32[64,448]{1,0:T(8,128)S(1)}, f32[64,448]{1,0:T(8,128)}, u32[]{:S(2)}) copy-start(f32[64,448]{1,0:T(8,128)} %get-tuple-element.58) | copy-start | bytes 344068
  95.5 5.1 %copy-start.85 = (pred[512]{0:T(512)(128)(4,1)S(1)}, pred[512]{0:T(512)(128)(4,1)}, u32[]{:S(2)}) copy-start(pred[512]{0:T(512)(128)(4,1)} %constant.228.clone) | copy-start | bytes 1540
  95.5 5.1 %copy-start.95 = (f32[64]{0:T(128)S(1)}, f32[64]{0:T(128)}, u32[]{:S(2)}) copy-start(f32[64]{0:T(128)} %get-tuple-element.45) | copy-start | bytes 772
  95.8 5.1 %copy-start.11 = (f32[1,64,512]{2,0,1:T(1,128)S(1)}, f32[1,64,512]{2,0,1:T(1,128)}, u32[]{:S(2)}) copy-start(f32[1,64,512]{2,0,1:T(1,128)} %copy-done.10) | copy-start | bytes 393220
  95.9 5.1 %copy-start.14 = (f32[1,64,512]{2,0,1:T(1,128)S(1)}, f32[1,64,512]{2,0,1:T(1,128)}, u32[]{:S(2)}) copy-start(f32[1,64,512]{2,0,1:T(1,128)} %copy-done.13) | copy-start | bytes 393220
  95.9 5.1 %copy-start.19 = (f32[1,64,512]{2,0,1:T(1,128)S(1)}, f32[1,64,512]{2,0,1:T(1,128)}, u32[]{:S(2)}) copy-start(f32[1,64,512]{2,0,1:T(1,128)} %copy-done.18) | copy-start | bytes 393220
  95.9 5.1 %copy-start.20 = (f32[1,64,512]{2,0,1:T(1,128)S(1)}, f32[1,64,512]{2,0,1:T(1,128)}, u32[]{:S(2)}) copy-start(f32[1,64,512]{2,0,1:T(1,128)} %get-tuple-element.8) | copy-start | bytes 393220
  95.9 5.1 %copy-start.22 = (f32[1,64,512]{2,0,1:T(1,128)S(1)}, f32[1,64,512]{2,0,1:T(1,128)}, u32[]{:S(2)}) copy-start(f32[1,64,512]{2,0,1:T(1,128)} %get-tuple-element.11) | copy-start | bytes 393220
  95.9 5.1 %copy-start.24 = (f32[1,64,512]{2,0,1:T(1,128)S(1)}, f32[1,64,512]{2,0,1:T(1,128)}, u32[]{:S(2)}) copy-start(f32[1,64,512]{2,0,1:T(1,128)} %get-tuple-element.12) | copy-start | bytes 393220
  95.9 5.1 %copy-start.56 = (f32[64,448]{1,0:T(8,128)S(1)}, f32[64,448]{1,0:T(8,128)}, u32[]{:S(2)}) copy-start(f32[64,448]{1,0:T(8,128)} %get-tuple-element.29) | copy-start | bytes 344068
  102.4 35.4 %copy-start = (f32[64,512]{1,0:T(8,128)}, f32[64,512]{1,0:T(8,128)S(1)}, u32[]{:S(2)}) copy-start(f32[64,512]{1,0:T(8,128)S(1)} %get-tuple-element.56) | copy-start | bytes 393220
  102.4 3.8 %copy-start.49 = (f32[512,128]{1,0:T(8,128)S(1)}, f32[512,128]{1,0:T(8,128)}, u32[]{:S(2)}) copy-start(f32[512,128]{1,0:T(8,128)} %constant.220.clone) | copy-start | bytes 786436
  103.2 4.2 %copy-start.47 = (f32[512,128]{1,0:T(8,128)S(1)}, f32[512,128]{1,0:T(8,128)}, u32[]{:S(2)}) copy-start(f32[512,128]{1,0:T(8,128)} %constant.218.clone) | copy-start | bytes 786436
  106.2 9.6 %copy-start.36 = (f32[512,128]{1,0:T(8,128)S(1)}, f32[512,128]{1,0:T(8,128)}, u32[]{:S(2)}) copy-start(f32[512,128]{1,0:T(8,128)} %constant.221.clone) | copy-start | bytes 786436
  106.5 15.7 %copy-start.34 = (f32[512,128]{1,0:T(8,128)S(1)}, f32[512,128]{1,0:T(8,128)}, u32[]{:S(2)}) copy-start(f32[512,128]{1,0:T(8,128)} %constant.219.clone) | copy-start | bytes 786436
  108.4 16.8 %collective-permute-start.4 = (f32[16,512]{1,0:T(8,128)S(1)}, f32[16,512]{1,0:T(8,128)S(1)}, u32[]{:S(2)}, u32[]{:S(2)}) collective-permute-start(f32[16,512]{1,0:T(8,128)S(1)} %get-tuple-element.23), channel_id=1, source_target_pairs={{0,16},{16,32},{32,48},{48,64},{64,80},{80,96},{96,112},{112,128},... | collective-permute-start | bytes 98312 | tf_op jit(solution)/shard_map/ppermute | solution.py:18
  110.3 14.9 %collective-permute-start.5 = (f32[16,512]{1,0:T(8,128)S(1)}, f32[16,512]{1,0:T(8,128)S(1)}, u32[]{:S(2)}, u32[]{:S(2)}) collective-permute-start(f32[16,512]{1,0:T(8,128)S(1)} %get-tuple-element.24), channel_id=1, source_target_pairs={{16,0},{32,16},{48,32},{64,48},{80,64},{96,80},{112,96},{128,112},... | collective-permute-start | bytes 98312 | tf_op jit(solution)/shard_map/ppermute | solution.py:19
  116.7 16.5 %collective-permute-start.6 = (f32[1,64,128]{2,1,0:T(8,128)}, f32[1,64,128]{2,1,0:T(8,128)}, u32[]{:S(2)}, u32[]{:S(2)}) collective-permute-start(f32[1,64,128]{2,1,0:T(8,128)} %fusion.80), channel_id=1, source_target_pairs={{0,1},{1,2},{2,3},{3,4},{4,5},{5,6},{6,7},{7,8},{8,9},{9,10},{10,1... | collective-permute-start | bytes 98312 | tf_op jit(solution)/shard_map/ppermute | solution.py:18
  123.0 12.6 %collective-permute-start.7 = (f32[1,64,128]{2,1,0:T(8,128)}, f32[1,64,128]{2,1,0:T(8,128)}, u32[]{:S(2)}, u32[]{:S(2)}) collective-permute-start(f32[1,64,128]{2,1,0:T(8,128)} %fusion.79), channel_id=1, source_target_pairs={{1,0},{2,1},{3,2},{4,3},{5,4},{6,5},{7,6},{8,7},{9,8},{10,9},{11,1... | collective-permute-start | bytes 98312 | tf_op jit(solution)/shard_map/ppermute | solution.py:19
  125.3 2.9 %copy-start.32 = (f32[4,128,128,1]{2,1,0,3:T(8,128)S(1)}, f32[4,128,128,1]{2,1,0,3:T(8,128)}, u32[]{:S(2)}) copy-start(f32[4,128,128,1]{2,1,0,3:T(8,128)} %constant.309) | copy-start | bytes 786436
  125.3 3.5 %copy-start.31 = (f32[4,128,128,1]{2,1,0,3:T(8,128)S(1)}, f32[4,128,128,1]{2,1,0,3:T(8,128)}, u32[]{:S(2)}) copy-start(f32[4,128,128,1]{2,1,0,3:T(8,128)} %constant.308) | copy-start | bytes 786436
  128.9 2.6 %copy-start.7 = (f32[64,512]{1,0:T(8,128)S(1)}, f32[64,512]{1,0:T(8,128)}, u32[]{:S(2)}) copy-start(f32[64,512]{1,0:T(8,128)} %constant.224.clone) | copy-start | bytes 393220
  128.9 2.6 %copy-start.54 = (f32[64,504]{1,0:T(8,128)S(1)}, f32[64,504]{1,0:T(8,128)}, u32[]{:S(2)}) copy-start(f32[64,504]{1,0:T(8,128)} %get-tuple-element.21) | copy-start | bytes 387076
  128.9 2.6 %copy-start.82 = (pred[512]{0:T(512)(128)(4,1)S(1)}, pred[512]{0:T(512)(128)(4,1)}, u32[]{:S(2)}) copy-start(pred[512]{0:T(512)(128)(4,1)} %constant.230.clone) | copy-start | bytes 1540
  131.5 2.8 %copy-start.58 = (f32[64,511]{1,0:T(8,128)S(1)}, f32[64,511]{1,0:T(8,128)}, u32[]{:S(2)}) copy-start(f32[64,511]{1,0:T(8,128)} %get-tuple-element.25) | copy-start | bytes 392452
  131.8 3.6 %copy-start.17 = (f32[64,512]{1,0:T(8,128)S(1)}, f32[64,512]{1,0:T(8,128)}, u32[]{:S(2)}) copy-start(f32[64,512]{1,0:T(8,128)} %constant.222.clone) | copy-start | bytes 393220
  131.8 3.6 %copy-start.86 = (pred[512]{0:T(512)(128)(4,1)S(1)}, pred[512]{0:T(512)(128)(4,1)}, u32[]{:S(2)}) copy-start(pred[512]{0:T(512)(128)(4,1)} %constant.228.clone) | copy-start | bytes 1540
  132.4 4.2 %copy-start.55 = (f32[64,511]{1,0:T(8,128)S(1)}, f32[64,511]{1,0:T(8,128)}, u32[]{:S(2)}) copy-start(f32[64,511]{1,0:T(8,128)} %get-tuple-element.26) | copy-start | bytes 392452
  132.8 5.0 %copy-start.12 = (f32[1,64,512]{2,0,1:T(1,128)S(1)}, f32[1,64,512]{2,0,1:T(1,128)}, u32[]{:S(2)}) copy-start(f32[1,64,512]{2,0,1:T(1,128)} %copy-done.10) | copy-start | bytes 393220
  132.8 5.0 %copy-start.15 = (f32[1,64,512]{2,0,1:T(1,128)S(1)}, f32[1,64,512]{2,0,1:T(1,128)}, u32[]{:S(2)}) copy-start(f32[1,64,512]{2,0,1:T(1,128)} %copy-done.13) | copy-start | bytes 393220
  132.8 5.0 %copy-start.21 = (f32[1,64,512]{2,0,1:T(1,128)S(1)}, f32[1,64,512]{2,0,1:T(1,128)}, u32[]{:S(2)}) copy-start(f32[1,64,512]{2,0,1:T(1,128)} %get-tuple-element.8) | copy-start | bytes 393220
  132.8 5.0 %copy-start.23 = (f32[1,64,512]{2,0,1:T(1,128)S(1)}, f32[1,64,512]{2,0,1:T(1,128)}, u32[]{:S(2)}) copy-start(f32[1,64,512]{2,0,1:T(1,128)} %get-tuple-element.11) | copy-start | bytes 393220
  132.9 5.0 %copy-start.25 = (f32[1,64,512]{2,0,1:T(1,128)S(1)}, f32[1,64,512]{2,0,1:T(1,128)}, u32[]{:S(2)}) copy-start(f32[1,64,512]{2,0,1:T(1,128)} %get-tuple-element.12) | copy-start | bytes 393220
  132.9 5.0 %copy-start.72 = (f32[64,448]{1,0:T(8,128)S(1)}, f32[64,448]{1,0:T(8,128)}, u32[]{:S(2)}) copy-start(f32[64,448]{1,0:T(8,128)} %get-tuple-element.15) | copy-start | bytes 344068
  132.9 5.0 %copy-start.96 = (f32[64]{0:T(128)S(1)}, f32[64]{0:T(128)}, u32[]{:S(2)}) copy-start(f32[64]{0:T(128)} %get-tuple-element.45) | copy-start | bytes 772
  (44 other events, 81.1 us)
where the time goes:
time: 140 us; the launch traced here: 139 us
  starting transfers between devices  46.4 us (33%)
  matrix products  41.1 us (29%)
  local copies, waits for them, and re-layouts  33.5 us (24%)
  waiting for transfers between devices  11.2 us (8%)
  other arithmetic  4.27 us (3%)
  between operations  2.78 us (2%)
    dot_general x48, matrix products, select(): jnp.einsum('...c,cd->...d', values, jnp.asarray(table), precision=exact)  34.8 us
    ppermute x4, starting transfers between devices, with_halo(): before = lax.ppermute(last, axis, up)  17.8 us
    ppermute x4, starting transfers between devices, with_halo(): after = lax.ppermute(initial, axis, down)  15 us
    all_to_all x1, waiting for transfers between devices, relocate(): lax.all_to_all(packed, 'dom', split_axis=1, concat_axis=1, tiled=True)  11.2 us
    all_to_all x1, starting transfers between devices, relocate(): lax.all_to_all(places, 'dom', split_axis=1, concat_axis=1, tiled=True)  6.92 us
    all_to_all x1, starting transfers between devices, relocate(): lax.all_to_all(packed, 'dom', split_axis=1, concat_axis=1, tiled=True)  6.67 us
    slice x9, local copies, waits for them, and re-layouts, moved_by(): return jnp.concatenate([empty, values[:, :512 - stride]], axis=1)  6.55 us
    dot_general x8, matrix products, ghost_values(): jnp.einsum('bfex,exy->bfy', picked, jnp.asarray(tables[pair]), precision=...  6.32 us
  transfers between devices with their start and end apart: 10, of which 1 were waited for; matrix products, arithmetic and copies ran while one was open for 36% of the time, Pallas kernels for 0%

commit v1 on v0

v1 whole, which is shorter than its diff:
```python
import jax
import jax.numpy as jnp
from jax import lax
from jax.experimental import pallas as pl
from jax.experimental.pallas import tpu as pltpu
from jax.sharding import PartitionSpec as P

peers = 16
blocks = 64
fields = 6
room = 4
reach = 16
rows = fields * 4
chunk = room * rows + 8
vmem = 48 * 1024 * 1024
f32 = jnp.float32


def lane_take(x, index):
    numbers = lax.GatherDimensionNumbers((), (1,), (1,), (0,), (0,))
    return lax.gather(x, index[..., None], numbers, (1, 1), mode=lax.GatherScatterMode.PROMISE_IN_BOUNDS)


def row_take(x, index):
    numbers = lax.GatherDimensionNumbers((), (0,), (0,), (1,), (1,))
    return lax.gather(x, index[..., None], numbers, (1, 1), mode=lax.GatherScatterMode.PROMISE_IN_BOUNDS)


def iota(shape, axis):
    return lax.broadcasted_iota(jnp.int32, shape, axis)


def turn(x, shift, axis=None):
    axis = x.ndim - 1 if axis is None else axis
    shift = shift % x.shape[axis]
    if shift == 0:
        return x
    if x.ndim == 2:
        return pltpu.roll(x, shift, axis)
    flat = pltpu.roll(x.reshape(-1, x.shape[-1]), shift, 1)
    return flat.reshape(x.shape)


def pack_kernel(*refs):
    sources, (send, own, stay), (work, flags, count) = refs[:9], refs[9:12], refs[12:15]
    held, sems = refs[15:24], refs[24]
    copies = [pltpu.make_async_copy(source, ref, sems.at[n]) for n, (source, ref) in enumerate(zip(sources, held))]
    for copy in copies:
        copy.start()
    refine, destination, head, prior, alpha, shape_n, resid, sat, cond = held
    me = lax.axis_index("dom")
    for copy in copies:
        copy.wait()
    for peer in range(peers):
        count[peer] = 0
    for block in range(blocks):
        flags[pl.ds(block, 1), :] = jnp.full((1, 128), refine[block], jnp.int32)
    lane = iota((blocks, 128), 1)
    half, fine_y, fine_z = (lane >> 6) & 1, (lane >> 3) & 7, lane & 7
    flag = flags[...]
    octant = jnp.maximum(flag - 1, 0)
    kept = flag == 0
    bit_x, bit_y, bit_z = (octant >> 2) & 1, (octant >> 1) & 1, octant & 1
    up_x = bit_x == 1

    def get(ref):
        return [ref[0, :, 128 * c : 128 * c + 128] for c in range(4)]

    plain_y, plain_z = 4 * bit_y + (fine_y >> 1), 4 * bit_z + (fine_z >> 1)
    inner = plain_y * 8 + plain_z
    plain_index = [jnp.where(kept, lane, parity * 64 + inner) for parity in range(2)]

    def plain(v):
        chosen = [
            jnp.where(up_x, v[2], v[0]),
            jnp.where(kept, v[1], jnp.where(up_x, v[2], v[0])),
            jnp.where(kept, v[2], jnp.where(up_x, v[3], v[1])),
            jnp.where(kept | up_x, v[3], v[1]),
        ]
        return [lane_take(chosen[c], plain_index[c % 2]) for c in range(4)]

    side_y = jnp.clip(plain_y + 2 * (fine_y & 1) - 1, 0, 7)
    side_z = jnp.clip(plain_z + 2 * (fine_z & 1) - 1, 0, 7)
    near_y = half * 64 + plain_y * 8 + fine_z
    far_y = half * 64 + side_y * 8 + fine_z
    near_z = (lane & 120) + plain_z
    far_z = (lane & 120) + side_z
    lower = lane < 64

    def smooth(v):
        r = [turn(x, 64) for x in v]
        base = [jnp.where(up_x, v[2 + c], v[c]) for c in range(2)]
        base_r = [jnp.where(up_x, r[2 + c], r[c]) for c in range(2)]
        near = [
            jnp.where(lower, base[0], base_r[0]),
            jnp.where(lower, base_r[0], base[0]),
            jnp.where(lower, base[1], base_r[1]),
            jnp.where(lower, base_r[1], base[1]),
        ]
        far = [
            jnp.where(lower, jnp.where(up_x, r[1], v[0]), base[0]),
            jnp.where(lower, base[0], jnp.where(up_x, r[3], r[1])),
            jnp.where(lower, base_r[0], base[1]),
            jnp.where(lower, base[1], jnp.where(up_x, v[3], r[2])),
        ]
        result = []
        for c in range(4):
            x = 0.75 * near[c] + 0.25 * far[c]
            x = 0.75 * lane_take(x, near_y) + 0.25 * lane_take(x, far_y)
            x = 0.75 * lane_take(x, near_z) + 0.25 * lane_take(x, far_z)
            result.append(jnp.where(kept, v[c], x))
        return result

    low = get(resid)
    span = [high - bottom for high, bottom in zip(get(sat), low)]
    moved = [
        smooth(get(head)),
        [a - b for a, b in zip(plain(low), smooth(get(prior)))],
        plain(get(alpha)),
        plain(get(shape_n)),
        plain(get(cond)),
        plain(span),
    ]
    for f in range(fields):
        for c in range(4):
            own[pl.ds((f * 4 + c) * blocks, blocks), :] = moved[f][c]
            for g in range(blocks // 8):
                part = moved[f][c][8 * g : 8 * g + 8]
                work[pl.ds(8 * g * rows + f * 4 + c, 8, stride=rows), :] = part

    for peer in range(peers):
        send[pl.ds(peer * chunk + room * rows, 8), :] = jnp.full((8, 128), -1.0, f32)

    for block in range(blocks):
        target = destination[block]
        owner = target >> 6
        used = count[owner] & (room - 1)
        count[owner] = used + 1
        spot = jnp.full((1, 128), target & 63, jnp.int32).astype(f32)
        start = pl.multiple_of(owner * chunk + used * rows, 8)
        send[pl.ds(start, rows), :] = work[block * rows : block * rows + rows, :]
        send[pl.ds(owner * chunk + room * rows + used, 1), :] = spot
        stay[block : block + 1, :] = jnp.where(owner == me, spot, -1.0)
    send[pl.ds(pl.multiple_of(me * chunk + room * rows, 8), 8), :] = jnp.full((8, 128), -1.0, f32)


def find(places):
    hit = places == (iota((blocks, 128), 1) & 63).astype(f32)
    row = jnp.sum(jnp.where(hit, iota((blocks, 128), 0), 0), axis=0, keepdims=True)
    has = jnp.sum(jnp.where(hit, 1, 0), axis=0, keepdims=True) > 0
    return row + (iota((1, 128), 1) & 64), has


def settle_kernel(own, stay, out):
    index, _ = find(stay[...])
    index = jnp.broadcast_to(index, (128, 128))
    for f in range(fields):
        for c in range(2):
            lo = own[(f * 4 + c) * blocks : (f * 4 + c + 1) * blocks, :]
            hi = own[(f * 4 + c + 2) * blocks : (f * 4 + c + 3) * blocks, :]
            cells = jnp.concatenate([lo, hi], axis=0).T
            out[f, 128 * c : 128 * c + 128, :] = lane_take(cells, index)


def closure(head, less, alpha, shape_n, cond, span):
    expo = 1.0 - 1.0 / shape_n
    log_t = shape_n * jnp.log(alpha * jnp.maximum(-head, 0.0))
    log_s = jnp.log(1.0 + jnp.exp(log_t))
    root = jnp.exp(-0.5 * expo * log_s)
    inner = 1.0 - jnp.exp(expo * (log_t - log_s))
    return cond * root * inner * inner, 4.0 * (less + span * root * root)


def cube(x):
    return x.reshape(4, 8, 8, 128)


def face_tiles(x):
    y0, y7 = x[:, 0], x[:, 7]
    return [
        x[0],
        turn(x[3], 64),
        jnp.concatenate([y0, turn(y0, 64)], axis=0),
        jnp.concatenate([y7, turn(y7, 64)], axis=0),
    ]


def pack_faces(tiles_h, tiles_k, first):
    group = iota((8, 8, 128), 2) >> 4
    packed = None
    for f in range(4):
        for q, tiles in enumerate((tiles_h, tiles_k)):
            part = turn(tiles[f], (2 * f + q) * reach - first)
            packed = part if packed is None else jnp.where(group == 2 * f + q, part, packed)
    return packed.reshape(64, 128)


def emit(head_ref, cond_ref, right, left, up, down):
    tiles_h, tiles_k = face_tiles(cube(head_ref[...])), face_tiles(cube(cond_ref[...]))
    right[...] = pack_faces(tiles_h, tiles_k, blocks - reach)
    left[...] = pack_faces(tiles_h, tiles_k, 0)
    for q, ref in enumerate((head_ref, cond_ref)):
        up[32 * q : 32 * q + 32, :] = ref[pl.ds(7, 32, stride=8), :]
        down[32 * q : 32 * q + 32, :] = ref[pl.ds(0, 32, stride=8), :]


def arrive_kernel(recv, settled, state, cond_out, water_out, right, left, up, down):
    def slots(start):
        return [recv[pl.ds(start(o), peers, stride=chunk), :] for o in range(room)]

    places = jnp.concatenate(slots(lambda o: room * rows + o), axis=0)
    index, has = find(places)
    index = jnp.broadcast_to(index, (128, 128))
    for f in range(fields):
        for c in range(2):
            parts = slots(lambda o: o * rows + f * 4 + c) + slots(lambda o: o * rows + f * 4 + c + 2)
            cells = jnp.concatenate(parts, axis=0).T
            span = slice(128 * c, 128 * c + 128)
            state[f, span, :] = jnp.where(has, lane_take(cells, index), settled[f, span, :])
    cond, water = closure(*[state[f] for f in range(fields)])
    cond_out[...] = cond
    water_out[...] = water
    emit(state.at[0], cond_out, right, left, up, down)


class Table:
    def __init__(self, near):
        position = near[...] - lax.axis_index("dom") * blocks
        spot = jnp.where(position < 0, position + 80, jnp.where(position >= blocks, position + reach, position))
        present = near[...] >= 0
        spot = jnp.where(present, spot, 0)
        lower = iota((8, 128), 1) < 64
        front = iota((8, 128), 0) < 4

        def row(f, e):
            return jnp.broadcast_to(spot[4 * f + e : 4 * f + e + 1], (8, 128))

        def on(f, e):
            return jnp.broadcast_to(present[4 * f + e : 4 * f + e + 1].astype(jnp.int32), (8, 128)) == 1

        self.lower = lower
        self.one_x = jnp.where(lower, row(0, 0), row(1, 0))
        self.four_x = [
            jnp.where(
                lower,
                jnp.where(front, row(0, 2 * s), row(0, 2 * s + 1)),
                jnp.where(front, row(1, 2 * s), row(1, 2 * s + 1)),
            )
            for s in range(2)
        ]
        self.hang_x = (lower & on(0, 3)) | (~lower & on(1, 3))
        self.on_x = (lower & on(0, 0)) | (~lower & on(1, 0))
        self.one_y = [row(f, 0) for f in (2, 3)]
        self.four_y = [
            jnp.where(
                lower,
                jnp.where(front, row(f, 0), row(f, 1)),
                jnp.where(front, row(f, 2), row(f, 3)),
            )
            for f in (2, 3)
        ]
        self.hang_y = [on(f, 3) for f in (2, 3)]
        self.on_y = [on(f, 0) for f in (2, 3)]


def quarters(tile):
    pick = (iota((8, 128), 0) & 3) * 2
    result = []
    for a in range(4):
        pair = tile[2 * a] + tile[2 * a + 1]
        pair = 0.25 * (pair + turn(pair, 7, 0))
        result.append(row_take(pair, pick))
    return result


def ghosts(x, left, right, q, table):
    lane = iota((8, 8, 128), 2)
    tiles = []
    for f, tile in enumerate(face_tiles(x)):
        g = 2 * f + q
        after = jnp.where(lane < 80, turn(left, 64 - g * reach), turn(right, 80 - g * reach))
        tiles.append(jnp.where(lane < 64, tile, after))
    coarse = [quarters(tile) for tile in tiles]
    low = table.lower
    face_x = []
    for a in range(8):
        one = jnp.where(low, lane_take(tiles[1][a], table.one_x), lane_take(tiles[0][a], table.one_x))
        index = table.four_x[a // 4]
        four = jnp.where(low, lane_take(coarse[1][a % 4], index), lane_take(coarse[0][a % 4], index))
        face_x.append(jnp.where(table.hang_x, four, one))
    face_y = []
    for side, source in ((0, 3), (1, 2)):
        made = []
        for a in range(4):
            index = table.one_y[side]
            one = jnp.where(low, lane_take(tiles[source][a], index), lane_take(tiles[source][a + 4], index))
            four = lane_take(coarse[source][a], table.four_y[side])
            made.append(jnp.where(table.hang_y[side], four, one))
        face_y.append(jnp.stack(made))
    return jnp.stack(face_x), face_y[0], face_y[1]


def balance(head, cond, left, right, below, above, near, planes):
    table = Table(near)
    level = lax.axis_index("depth")
    left, right = left[...].reshape(8, 8, 128), right[...].reshape(8, 8, 128)
    ghost_h = ghosts(head, left, right, 0, table)
    ghost_k = ghosts(cond, left, right, 1, table)
    for q in range(2):
        planes[2 * q, pl.ds(0, 32, stride=8), :] = below[32 * q : 32 * q + 32, :]
        planes[2 * q + 1, pl.ds(7, 32, stride=8), :] = above[32 * q : 32 * q + 32, :]
    level_k = iota((4, 8, 8, 128), 2)
    low = iota((8, 8, 128), 2) < 64

    def neighbours(x, ghost, q):
        around, y2, y3 = ghost
        x0, x3 = turn(x[0], 64), turn(x[3], 64)
        return [
            jnp.concatenate([jnp.where(low, around, x3)[None], x[:3]], axis=0),
            jnp.concatenate([x[1:], jnp.where(low, x0, around)[None]], axis=0),
            jnp.concatenate([y2[:, None], x[:, :7]], axis=1),
            jnp.concatenate([x[:, 1:], y3[:, None]], axis=1),
            jnp.where(level_k == 0, cube(planes[2 * q]), cube(turn(x.reshape(256, 128), 1, 0))),
            jnp.where(level_k == 7, cube(planes[2 * q + 1]), cube(turn(x.reshape(256, 128), 255, 0))),
        ]

    slab = iota((4, 8, 8, 128), 0)
    row_j = iota((4, 8, 8, 128), 1)
    lower = iota((4, 8, 8, 128), 3) < 64
    off_x, off_y = ~table.on_x, [~on for on in table.on_y]
    closed = [
        (slab == 0) & lower & off_x,
        (slab == 3) & ~lower & off_x,
        (row_j == 0) & off_y[0],
        (row_j == 7) & off_y[1],
        (level_k == 0) & (level == 0),
        (level_k == 7) & (level == lax.axis_size("depth") - 1),
    ]
    flux = total = None
    pairs = zip(neighbours(head, ghost_h, 0), neighbours(cond, ghost_k, 1), closed)
    for direction, (near_h, near_k, shut) in enumerate(pairs):
        face_k = jnp.where(shut, 0.0, cond + near_k)
        lift = (0.0, 0.0, 0.0, 0.0, -1.0, 1.0)[direction]
        part = jnp.where(shut, 0.0, face_k * (near_h - head + lift))
        flux = part if flux is None else flux + part
        total = face_k if total is None else total + face_k
    return 0.5 * flux, 0.5 * total


def newton_kernel(
    state, cond, water, left, right, below, above, near, head_out, cond_out, water_out, to_right, to_left, up, down, planes
):
    head = cube(state[0])
    flux, total = balance(head, cube(cond[...]), left, right, below, above, near, planes)
    resid = cube(water[...]) - flux
    diagonal = 4.0 * cube(state[5]) * cube(state[2]) + total
    head_out[...] = (head - resid / diagonal).reshape(256, 128)
    new_cond, new_water = closure(head_out[...], *[state[f] for f in range(1, fields)])
    cond_out[...] = new_cond
    water_out[...] = new_water
    emit(head_out, cond_out, to_right, to_left, up, down)


def leave(ref, cells):
    for c in range(2):
        turned = cells[128 * c : 128 * c + 128].T
        ref[0, :, 128 * c : 128 * c + 128] = turned[:blocks]
        ref[0, :, 128 * c + 256 : 128 * c + 384] = turned[blocks:]


def residual_kernel(head, cond, water, left, right, below, above, near, head_out, resid_out, planes):
    flux, _ = balance(cube(head[...]), cube(cond[...]), left, right, below, above, near, planes)
    leave(resid_out, water[...] - flux.reshape(256, 128))
    leave(head_out, head[...])


def shape(*dims):
    return jax.ShapeDtypeStruct(dims, f32)


def call(kernel, outs, scratch, *operands, source=pltpu.VMEM, limit=vmem):
    whole = pl.BlockSpec(memory_space=pltpu.VMEM)
    return pl.pallas_call(
        kernel,
        out_shape=outs,
        in_specs=[pl.BlockSpec(memory_space=source)] * len(operands),
        out_specs=[whole] * len(outs),
        scratch_shapes=scratch,
        compiler_params=pltpu.CompilerParams(vmem_limit_bytes=limit),
    )(*operands)


def exchange(to_right, to_left, up, down):
    def shifted(x, axis, step):
        size = lax.axis_size(axis)
        return lax.ppermute(x, axis, [(i, (i + step) % size) for i in range(size)])

    return (
        shifted(to_right, "dom", 1),
        shifted(to_left, "dom", -1),
        shifted(up, "depth", 1),
        shifted(down, "depth", -1),
    )


def on_device(head, water_prev, alpha, shape_n, theta_r, theta_s, sat_cond, refine, destination, neighbours):
    send, own, stay = call(
        pack_kernel,
        [shape(peers * chunk, 128), shape(rows * blocks, 128), shape(blocks, 128)],
        [pltpu.VMEM((blocks * rows, 128), f32), pltpu.VMEM((blocks, 128), jnp.int32), pltpu.SMEM((peers,), jnp.int32)]
        + [pltpu.SMEM((blocks,), jnp.int32)] * 2
        + [pltpu.VMEM((1, blocks, 512), f32)] * 7
        + [pltpu.SemaphoreType.DMA((9,))],
        refine, destination, head, water_prev, alpha, shape_n, theta_r, theta_s, sat_cond,
        source=pltpu.HBM,
        limit=64 * 1024 * 1024,
    )
    recv = lax.all_to_all(send.reshape(peers, chunk, 128), "dom", 0, 0, tiled=True)
    (settled,) = call(settle_kernel, [shape(fields, 256, 128)], [], own, stay)
    near = neighbours.reshape(blocks, 16).T
    near = jnp.concatenate([near, near], axis=1)
    cells, halo = shape(256, 128), [shape(64, 128)] * 4
    state, cond, water, *outgoing = call(
        arrive_kernel,
        [shape(fields, 256, 128), cells, cells] + halo,
        [],
        recv.reshape(peers * chunk, 128), settled,
    )
    planes = [pltpu.VMEM((4, 256, 128), f32)]
    new_head, cond, water, *outgoing = call(
        newton_kernel, [cells] * 3 + halo, planes, state, cond, water, *exchange(*outgoing), near
    )
    final = shape(1, blocks, 512)
    return tuple(
        call(residual_kernel, [final, final], planes, new_head, cond, water, *exchange(*outgoing), near)
    )


def solution(mesh):
    cells = P("depth", "dom", None)
    return jax.shard_map(
        on_device,
        mesh=mesh,
        in_specs=(cells,) * 7 + (P("dom"), P("dom"), P("dom", None, None)),
        out_specs=(cells, cells),
        check_vma=False,
    )
```

time: 140 us -> 54.2 us (0.39)
  the two profiles are of different devices: /device:TPU:99 before, /device:TPU:97 now
where the time goes in v1:
time: 54.2 us; the launch traced here: 54 us
  starting transfers between devices  23.2 us (43%)
  waiting for transfers between devices  21.9 us (40%)
  Pallas kernels  8.08 us (15%)
  between operations  0.73 us (1%)
    ppermute x8, starting transfers between devices, shifted(): return lax.ppermute(x, axis, [(i, (i + step) % size) for i in range(size)])  16.3 us
    all_to_all x1, waiting for transfers between devices, on_device(): lax.all_to_all(send.reshape(peers, chunk, 128), 'dom', 0, 0, tiled=True)  12.8 us
    ppermute x8, waiting for transfers between devices, shifted(): return lax.ppermute(x, axis, [(i, (i + step) % size) for i in range(size)])  9.01 us
    pallas_call x5, Pallas kernels, call(): pl.pallas_call(kernel, out_shape=outs, in_specs=[pl.BlockSpec(memory_spac...  8.08 us
    all_to_all x1, starting transfers between devices, on_device(): lax.all_to_all(send.reshape(peers, chunk, 128), 'dom', 0, 0, tiled=True)  6.9 us
  transfers between devices with their start and end apart: 9, of which 6 were waited for; matrix products, arithmetic and copies ran while one was open for 0% of the time, Pallas kernels for 1%

profile of v1, /device:TPU:97, one launch (start us, length us, event | category | flops | bytes accessed | tf_op | source)
XLA Modules:
  0.0 54.0 jit_solution(17820464619920789348)
XLA Ops:
  0.6 4.3 %shard_map.113 = (f32[1664,128]{1,0:T(8,128)}, f32[1536,128]{1,0:T(8,128)}, f32[64,128]{1,0:T(8,128)}) custom-call(s32[64]{0:T(128)} %refs_0_.1, s32[64]{0:T(128)} %refs_1_.1, f32[1,64,512]{2,1,0:T(8,128)} %refs_2_.1, f32[1,64,512]{2,1,0:T(8,128)} %refs_3_.1, f32[1,64,512]{2,1,0:T(8,128)} %refs_4_.1, f32[1,64,512]{2,1,0:T(8,128)} %refs_5_.1, ...), custom_call_target="tpu_custom_call" | custom-call | tf_op jit(solution)/shard_map/pallas_call | solution.py:383
  4.9 0.0 copy-start
  4.9 0.0 copy-start.1
  4.9 6.9 %all-to-all-start = ((f32[16,104,128]{2,1,0:T(8,128)}), f32[16,104,128]{2,1,0:T(8,128)S(1)}, u32[]{:S(2)}, u32[]{:S(2)}) async-start(f32[16,104,128]{2,1,0:T(8,128)} %bitcast.6), calls=%async_computation | async-start | bytes 1703936 | tf_op jit(solution)/shard_map/all_to_all | solution.py:418
  11.8 0.0 copy-done
  11.9 0.0 copy-done.1
  11.9 0.5 shard_map.114.settled
  12.4 12.8 %all-to-all-done = f32[16,104,128]{2,1,0:T(8,128)S(1)} async-done(((f32[16,104,128]{2,1,0:T(8,128)}), f32[16,104,128]{2,1,0:T(8,128)S(1)}, u32[]{:S(2)}, u32[]{:S(2)}) %all-to-all-start) | async-done | bytes 852000 | tf_op jit(solution)/shard_map/all_to_all | solution.py:418
  25.2 0.8 %shard_map.115 = (f32[6,256,128]{2,1,0:T(8,128)S(1)}, f32[256,128]{1,0:T(8,128)S(1)}, f32[256,128]{1,0:T(8,128)S(1)}, f32[64,128]{1,0:T(8,128)S(1)}, f32[64,128]...) custom-call(f32[1664,128]{1,0:T(8,128)S(1)} %bitcast.5, f32[6,256,128]{2,1,0:T(8,128)S(1)} %shard_map.114.settled), custom_call_target="tpu_custom_call" | custom-call | tf_op jit(solution)/shard_map/pallas_call | solution.py:383
  26.1 0.0 copy-start.2
  26.1 0.4 collective-permute-start
  26.4 4.5 %collective-permute-start.1 = (f32[64,128]{1,0:T(8,128)S(1)}, f32[64,128]{1,0:T(8,128)S(1)}, u32[]{:S(2)}, u32[]{:S(2)}) collective-permute-start(f32[64,128]{1,0:T(8,128)S(1)} %get-tuple-element.26), channel_id=1, source_target_pairs={{0,240},{16,0},{32,16},{48,32},{64,48},{80,64},{96,80},{112,96},{1... | collective-permute-start | bytes 98312 | tf_op jit(solution)/shard_map/ppermute | solution.py:396
  30.9 6.1 %collective-permute-start.2 = (f32[64,128]{1,0:T(8,128)S(1)}, f32[64,128]{1,0:T(8,128)S(1)}, u32[]{:S(2)}, u32[]{:S(2)}) collective-permute-start(f32[64,128]{1,0:T(8,128)S(1)} %get-tuple-element.27), channel_id=1, source_target_pairs={{0,1},{1,2},{2,3},{3,4},{4,5},{5,6},{6,7},{7,8},{8,9},{9,10},{10,1... | collective-permute-start | bytes 98312 | tf_op jit(solution)/shard_map/ppermute | solution.py:396
  37.0 0.0 collective-permute-start.3
  37.0 0.0 copy-done.2
  37.0 0.1 pad_add_fusion.near
  37.1 0.0 collective-permute-done.left
  37.1 0.0 collective-permute-done.1.right
  37.1 0.9 %collective-permute-done.2.below = f32[64,128]{1,0:T(8,128)S(1)} collective-permute-done((f32[64,128]{1,0:T(8,128)S(1)}, f32[64,128]{1,0:T(8,128)S(1)}, u32[]{:S(2)}, u32[]{:S(2)}) %collective-permute-start.2) | collective-permute-done | bytes 32800 | tf_op jit(solution)/shard_map/ppermute | solution.py:396
  38.0 3.5 %collective-permute-done.3.above = f32[64,128]{1,0:T(8,128)S(1)} collective-permute-done((f32[64,128]{1,0:T(8,128)S(1)}, f32[64,128]{1,0:T(8,128)S(1)}, u32[]{:S(2)}, u32[]{:S(2)}) %collective-permute-start.3) | collective-permute-done | bytes 32800 | tf_op jit(solution)/shard_map/ppermute | solution.py:396
  41.5 1.0 %shard_map.116 = (f32[256,128]{1,0:T(8,128)S(1)}, f32[256,128]{1,0:T(8,128)S(1)}, f32[256,128]{1,0:T(8,128)S(1)}, f32[64,128]{1,0:T(8,128)S(1)}, f32[64,128]{1,0...) custom-call(f32[6,256,128]{2,1,0:T(8,128)S(1)} %get-tuple-element.22.state, ...), custom_call_target="tpu_custom_call" | custom-call | tf_op jit(solution)/shard_map/pallas_call | solution.py:383
  42.6 0.1 collective-permute-start.4
  42.7 4.8 %collective-permute-start.5 = (f32[64,128]{1,0:T(8,128)S(1)}, f32[64,128]{1,0:T(8,128)S(1)}, u32[]{:S(2)}, u32[]{:S(2)}) collective-permute-start(f32[64,128]{1,0:T(8,128)S(1)} %get-tuple-element.33), channel_id=1, source_target_pairs={{0,240},{16,0},{32,16},{48,32},{64,48},{80,64},{96,80},{112,96},{1... | collective-permute-start | bytes 98312 | tf_op jit(solution)/shard_map/ppermute | solution.py:396
  47.5 0.6 %collective-permute-start.6 = (f32[64,128]{1,0:T(8,128)S(1)}, f32[64,128]{1,0:T(8,128)S(1)}, u32[]{:S(2)}, u32[]{:S(2)}) collective-permute-start(f32[64,128]{1,0:T(8,128)S(1)} %get-tuple-element.34), channel_id=1, source_target_pairs={{0,1},{1,2},{2,3},{3,4},{4,5},{5,6},{6,7},{7,8},{8,9},{9,10},{10,1... | collective-permute-start | bytes 98312 | tf_op jit(solution)/shard_map/ppermute | solution.py:396
  48.0 0.0 collective-permute-start.7
  48.0 0.7 %collective-permute-done.4.left = f32[64,128]{1,0:T(8,128)S(1)} collective-permute-done((f32[64,128]{1,0:T(8,128)S(1)}, f32[64,128]{1,0:T(8,128)S(1)}, u32[]{:S(2)}, u32[]{:S(2)}) %collective-permute-start.4) | collective-permute-done | bytes 32800 | tf_op jit(solution)/shard_map/ppermute | solution.py:396
  48.8 0.0 collective-permute-done.5.right
  48.8 0.3 collective-permute-done.6.below
  49.0 3.5 %collective-permute-done.7.above = f32[64,128]{1,0:T(8,128)S(1)} collective-permute-done((f32[64,128]{1,0:T(8,128)S(1)}, f32[64,128]{1,0:T(8,128)S(1)}, u32[]{:S(2)}, u32[]{:S(2)}) %collective-permute-start.7) | collective-permute-done | bytes 32800 | tf_op jit(solution)/shard_map/ppermute | solution.py:396
  52.6 1.4 %shard_map.117 = (f32[1,64,512]{2,1,0:T(8,128)}, f32[1,64,512]{2,1,0:T(8,128)}) custom-call(f32[256,128]{1,0:T(8,128)S(1)} %get-tuple-element.29.head, f32[256,128]{1,0:T(8,128)S(1)} %get-tuple-element.30.cond, f32[256,128]{1,0:T(8,128)S(1)} %get-tuple-element.31.water, f32[64,128]{1,0:T(8,128)S(1)} %collective-permute-done.4.left, ...), custom_call_target="tpu_custom_call" | custom-call | tf_op jit(solution)/shard_map/pallas_call | solution.py:383
Async XLA Ops:
  4.9 6.9 %copy-start = (f32[1536,128]{1,0:T(8,128)S(1)}, f32[1536,128]{1,0:T(8,128)}, u32[]{:S(2)}) copy-start(f32[1536,128]{1,0:T(8,128)} %get-tuple-element.20.own) | copy-start | bytes 2359300
  4.9 6.9 %copy-start.1 = (f32[64,128]{1,0:T(8,128)S(1)}, f32[64,128]{1,0:T(8,128)}, u32[]{:S(2)}) copy-start(f32[64,128]{1,0:T(8,128)} %get-tuple-element.21.stay) | copy-start | bytes 98308
  4.9 20.3 %all-to-all-start = ((f32[16,104,128]{2,1,0:T(8,128)}), f32[16,104,128]{2,1,0:T(8,128)S(1)}, u32[]{:S(2)}, u32[]{:S(2)}) async-start(f32[16,104,128]{2,1,0:T(8,128)} %bitcast.6), calls=%async_computation | async-start | bytes 1703936 | tf_op jit(solution)/shard_map/all_to_all | solution.py:418
  26.1 10.9 %copy-start.2 = (s32[64,4,4]{0,2,1:T(4,128)S(1)}, s32[64,4,4]{0,2,1:T(4,128)}, u32[]{:S(2)}) copy-start(s32[64,4,4]{0,2,1:T(4,128)} %param.19) | copy-start | bytes 12292
  26.1 11.0 %collective-permute-start = (f32[64,128]{1,0:T(8,128)S(1)}, f32[64,128]{1,0:T(8,128)S(1)}, u32[]{:S(2)}, u32[]{:S(2)}) collective-permute-start(f32[64,128]{1,0:T(8,128)S(1)} %get-tuple-element.25), channel_id=1, source_target_pairs={{0,16},{16,32},{32,48},{48,64},{64,80},{80,96},{96,112},{112,128},... | collective-permute-start | bytes 98312 | tf_op jit(solution)/shard_map/ppermute | solution.py:396
  26.4 10.6 %collective-permute-start.1 = (f32[64,128]{1,0:T(8,128)S(1)}, f32[64,128]{1,0:T(8,128)S(1)}, u32[]{:S(2)}, u32[]{:S(2)}) collective-permute-start(f32[64,128]{1,0:T(8,128)S(1)} %get-tuple-element.26), channel_id=1, source_target_pairs={{0,240},{16,0},{32,16},{48,32},{64,48},{80,64},{96,80},{112,96},{1... | collective-permute-start | bytes 98312 | tf_op jit(solution)/shard_map/ppermute | solution.py:396
  30.9 7.1 %collective-permute-start.2 = (f32[64,128]{1,0:T(8,128)S(1)}, f32[64,128]{1,0:T(8,128)S(1)}, u32[]{:S(2)}, u32[]{:S(2)}) collective-permute-start(f32[64,128]{1,0:T(8,128)S(1)} %get-tuple-element.27), channel_id=1, source_target_pairs={{0,1},{1,2},{2,3},{3,4},{4,5},{5,6},{6,7},{7,8},{8,9},{9,10},{10,1... | collective-permute-start | bytes 98312 | tf_op jit(solution)/shard_map/ppermute | solution.py:396
  37.0 4.6 %collective-permute-start.3 = (f32[64,128]{1,0:T(8,128)S(1)}, f32[64,128]{1,0:T(8,128)S(1)}, u32[]{:S(2)}, u32[]{:S(2)}) collective-permute-start(f32[64,128]{1,0:T(8,128)S(1)} %get-tuple-element.28), channel_id=1, source_target_pairs={{0,15},{1,0},{2,1},{3,2},{4,3},{5,4},{6,5},{7,6},{8,7},{9,8},{10,9... | collective-permute-start | bytes 98312 | tf_op jit(solution)/shard_map/ppermute | solution.py:396
  42.6 6.2 %collective-permute-start.4 = (f32[64,128]{1,0:T(8,128)S(1)}, f32[64,128]{1,0:T(8,128)S(1)}, u32[]{:S(2)}, u32[]{:S(2)}) collective-permute-start(f32[64,128]{1,0:T(8,128)S(1)} %get-tuple-element.32), channel_id=1, source_target_pairs={{0,16},{16,32},{32,48},{48,64},{64,80},{80,96},{96,112},{112,128},... | collective-permute-start | bytes 98312 | tf_op jit(solution)/shard_map/ppermute | solution.py:396
  42.7 6.1 %collective-permute-start.5 = (f32[64,128]{1,0:T(8,128)S(1)}, f32[64,128]{1,0:T(8,128)S(1)}, u32[]{:S(2)}, u32[]{:S(2)}) collective-permute-start(f32[64,128]{1,0:T(8,128)S(1)} %get-tuple-element.33), channel_id=1, source_target_pairs={{0,240},{16,0},{32,16},{48,32},{64,48},{80,64},{96,80},{112,96},{1... | collective-permute-start | bytes 98312 | tf_op jit(solution)/shard_map/ppermute | solution.py:396
  47.5 1.6 %collective-permute-start.6 = (f32[64,128]{1,0:T(8,128)S(1)}, f32[64,128]{1,0:T(8,128)S(1)}, u32[]{:S(2)}, u32[]{:S(2)}) collective-permute-start(f32[64,128]{1,0:T(8,128)S(1)} %get-tuple-element.34), channel_id=1, source_target_pairs={{0,1},{1,2},{2,3},{3,4},{4,5},{5,6},{6,7},{7,8},{8,9},{9,10},{10,1... | collective-permute-start | bytes 98312 | tf_op jit(solution)/shard_map/ppermute | solution.py:396
  48.0 4.6 %collective-permute-start.7 = (f32[64,128]{1,0:T(8,128)S(1)}, f32[64,128]{1,0:T(8,128)S(1)}, u32[]{:S(2)}, u32[]{:S(2)}) collective-permute-start(f32[64,128]{1,0:T(8,128)S(1)} %get-tuple-element.35), channel_id=1, source_target_pairs={{0,15},{1,0},{2,1},{3,2},{4,3},{5,4},{6,5},{7,6},{8,7},{9,8},{10,9... | collective-permute-start | bytes 98312 | tf_op jit(solution)/shard_map/ppermute | solution.py:396

commit v2 on v1

--- a/solution.py
+++ b/solution.py
@@ -11,6 +11,7 @@
 room = 4
 reach = 16
 rows = fields * 4
+late, early = 16, 8
 chunk = room * rows + 8
 vmem = 48 * 1024 * 1024
 f32 = jnp.float32
@@ -42,17 +43,24 @@
 
 
 def pack_kernel(*refs):
-    sources, (send, own, stay), (work, flags, count) = refs[:9], refs[9:12], refs[12:15]
-    held, sems = refs[15:24], refs[24]
-    copies = [pltpu.make_async_copy(source, ref, sems.at[n]) for n, (source, ref) in enumerate(zip(sources, held))]
-    for copy in copies:
+    sources, targets, refs = refs[:9], refs[9:12], refs[12:]
+    held, (own, send, stay), refs = refs[:9], refs[9:12], refs[12:]
+    work_late, work_early, flags, count, slot_early, sems_in, sems_out = refs
+    arriving = [pltpu.make_async_copy(source, ref, sems_in.at[n]) for n, (source, ref) in enumerate(zip(sources, held))]
+    for copy in arriving:
         copy.start()
-    refine, destination, head, prior, alpha, shape_n, resid, sat, cond = held
+    leaving = []
+
+    def depart(source, target):
+        copy = pltpu.make_async_copy(source, target, sems_out.at[len(leaving)])
+        copy.start()
+        leaving.append(copy)
+
+    refine, destination = held[:2]
     me = lax.axis_index("dom")
-    for copy in copies:
-        copy.wait()
     for peer in range(peers):
         count[peer] = 0
+    arriving[0].wait()
     for block in range(blocks):
         flags[pl.ds(block, 1), :] = jnp.full((1, 128), refine[block], jnp.int32)
     lane = iota((blocks, 128), 1)
@@ -63,8 +71,9 @@
     bit_x, bit_y, bit_z = (octant >> 2) & 1, (octant >> 1) & 1, octant & 1
     up_x = bit_x == 1
 
-    def get(ref):
-        return [ref[0, :, 128 * c : 128 * c + 128] for c in range(4)]
+    def get(n):
+        arriving[n].wait()
+        return [held[n][0, :, 128 * c : 128 * c + 128] for c in range(4)]
 
     plain_y, plain_z = 4 * bit_y + (fine_y >> 1), 4 * bit_z + (fine_z >> 1)
     inner = plain_y * 8 + plain_z
@@ -111,37 +120,44 @@
             result.append(jnp.where(kept, v[c], x))
         return result
 
-    low = get(resid)
-    span = [high - bottom for high, bottom in zip(get(sat), low)]
-    moved = [
-        smooth(get(head)),
-        [a - b for a, b in zip(plain(low), smooth(get(prior)))],
-        plain(get(alpha)),
-        plain(get(shape_n)),
-        plain(get(cond)),
-        plain(span),
-    ]
-    for f in range(fields):
+    def keep(f, values, work, size, first):
         for c in range(4):
-            own[pl.ds((f * 4 + c) * blocks, blocks), :] = moved[f][c]
+            own[f * 4 + c] = values[c]
             for g in range(blocks // 8):
-                part = moved[f][c][8 * g : 8 * g + 8]
-                work[pl.ds(8 * g * rows + f * 4 + c, 8, stride=rows), :] = part
-
+                work[pl.ds(8 * g * size + (f - first) * 4 + c, 8, stride=size), :] = values[c][8 * g : 8 * g + 8]
+        depart(own.at[4 * f : 4 * f + 4], targets[0].at[4 * f : 4 * f + 4])
+
+    for n, f in ((2, 2), (3, 3), (4, 4)):
+        keep(f, plain(get(n)), work_late, late, 2)
+    high, low = get(5), get(6)
+    keep(5, plain([x - y for x, y in zip(high, low)]), work_late, late, 2)
+
+    arriving[1].wait()
     for peer in range(peers):
-        send[pl.ds(peer * chunk + room * rows, 8), :] = jnp.full((8, 128), -1.0, f32)
-
+        send[peer, rows * room :, :] = jnp.full((8, 128), -1.0, f32)
     for block in range(blocks):
         target = destination[block]
         owner = target >> 6
         used = count[owner] & (room - 1)
         count[owner] = used + 1
         spot = jnp.full((1, 128), target & 63, jnp.int32).astype(f32)
-        start = pl.multiple_of(owner * chunk + used * rows, 8)
-        send[pl.ds(start, rows), :] = work[block * rows : block * rows + rows, :]
-        send[pl.ds(owner * chunk + room * rows + used, 1), :] = spot
+        slot_early[block] = room * late + used * early
+        start = pl.ds(pl.multiple_of(used * late, 8), late)
+        send[owner, start, :] = work_late[block * late : block * late + late, :]
+        send[owner, pl.ds(room * rows + used, 1), :] = spot
         stay[block : block + 1, :] = jnp.where(owner == me, spot, -1.0)
-    send[pl.ds(pl.multiple_of(me * chunk + room * rows, 8), 8), :] = jnp.full((8, 128), -1.0, f32)
+    send[me, rows * room :, :] = jnp.full((8, 128), -1.0, f32)
+    depart(send.at[:, : room * late], targets[1].at[:, : room * late])
+    depart(stay, targets[2])
+
+    keep(0, smooth(get(7)), work_early, early, 0)
+    keep(1, [x - y for x, y in zip(plain(low), smooth(get(8)))], work_early, early, 0)
+    for block in range(blocks):
+        start = pl.ds(pl.multiple_of(slot_early[block], 8), early)
+        send[destination[block] >> 6, start, :] = work_early[block * early : block * early + early, :]
+    depart(send.at[:, room * late :], targets[1].at[:, room * late :])
+    for copy in leaving:
+        copy.wait()
 
 
 def find(places):
@@ -156,9 +172,7 @@
     index = jnp.broadcast_to(index, (128, 128))
     for f in range(fields):
         for c in range(2):
-            lo = own[(f * 4 + c) * blocks : (f * 4 + c + 1) * blocks, :]
-            hi = own[(f * 4 + c + 2) * blocks : (f * 4 + c + 3) * blocks, :]
-            cells = jnp.concatenate([lo, hi], axis=0).T
+            cells = jnp.concatenate([own[f * 4 + c], own[f * 4 + c + 2]], axis=0).T
             out[f, 128 * c : 128 * c + 128, :] = lane_take(cells, index)
 
 
@@ -195,16 +209,23 @@
     return packed.reshape(64, 128)
 
 
-def emit(head_ref, cond_ref, right, left, up, down):
+def even(axis):
+    return lax.axis_index(axis) % 2 == 0
+
+
+def emit(head_ref, cond_ref, near, far, core, chip):
     tiles_h, tiles_k = face_tiles(cube(head_ref[...])), face_tiles(cube(cond_ref[...]))
-    right[...] = pack_faces(tiles_h, tiles_k, blocks - reach)
-    left[...] = pack_faces(tiles_h, tiles_k, 0)
+    right = pack_faces(tiles_h, tiles_k, blocks - reach)
+    left = pack_faces(tiles_h, tiles_k, 0)
+    near[...] = jnp.where(even("dom"), right, left)
+    far[...] = jnp.where(even("dom"), left, right)
     for q, ref in enumerate((head_ref, cond_ref)):
-        up[32 * q : 32 * q + 32, :] = ref[pl.ds(7, 32, stride=8), :]
-        down[32 * q : 32 * q + 32, :] = ref[pl.ds(0, 32, stride=8), :]
-
-
-def arrive_kernel(recv, settled, state, cond_out, water_out, right, left, up, down):
+        top, bottom = ref[pl.ds(7, 32, stride=8), :], ref[pl.ds(0, 32, stride=8), :]
+        core[32 * q : 32 * q + 32, :] = jnp.where(even("depth"), top, bottom)
+        chip[32 * q : 32 * q + 32, :] = jnp.where(even("depth"), bottom, top)
+
+
+def arrive_kernel(recv, settled, state, cond_out, water_out, *outgoing):
     def slots(start):
         return [recv[pl.ds(start(o), peers, stride=chunk), :] for o in range(room)]
 
@@ -213,14 +234,19 @@
     index = jnp.broadcast_to(index, (128, 128))
     for f in range(fields):
         for c in range(2):
-            parts = slots(lambda o: o * rows + f * 4 + c) + slots(lambda o: o * rows + f * 4 + c + 2)
+            parts = []
+            for r in (c, c + 2):
+                if f < 2:
+                    parts += slots(lambda o: room * late + o * early + f * 4 + r)
+                else:
+                    parts += slots(lambda o: o * late + (f - 2) * 4 + r)
             cells = jnp.concatenate(parts, axis=0).T
             span = slice(128 * c, 128 * c + 128)
             state[f, span, :] = jnp.where(has, lane_take(cells, index), settled[f, span, :])
     cond, water = closure(*[state[f] for f in range(fields)])
     cond_out[...] = cond
     water_out[...] = water
-    emit(state.at[0], cond_out, right, left, up, down)
+    emit(state.at[0], cond_out, *outgoing)
 
 
 class Table:
@@ -300,10 +326,13 @@
     return jnp.stack(face_x), face_y[0], face_y[1]
 
 
-def balance(head, cond, left, right, below, above, near, planes):
+def balance(head, cond, near_in, far_in, core, chip, near, planes):
     table = Table(near)
     level = lax.axis_index("depth")
-    left, right = left[...].reshape(8, 8, 128), right[...].reshape(8, 8, 128)
+    left = jnp.where(even("dom"), far_in[...], near_in[...]).reshape(8, 8, 128)
+    right = jnp.where(even("dom"), near_in[...], far_in[...]).reshape(8, 8, 128)
+    below = jnp.where(even("depth"), chip[...], core[...])
+    above = jnp.where(even("depth"), core[...], chip[...])
     ghost_h = ghosts(head, left, right, 0, table)
     ghost_k = ghosts(cond, left, right, 1, table)
     for q in range(2):
@@ -348,17 +377,17 @@
 
 
 def newton_kernel(
-    state, cond, water, left, right, below, above, near, head_out, cond_out, water_out, to_right, to_left, up, down, planes
+    state, cond, water, near_in, far_in, core, chip, table, head_out, cond_out, water_out, near, far, to_core, to_chip, planes
 ):
     head = cube(state[0])
-    flux, total = balance(head, cube(cond[...]), left, right, below, above, near, planes)
+    flux, total = balance(head, cube(cond[...]), near_in, far_in, core, chip, table, planes)
     resid = cube(water[...]) - flux
     diagonal = 4.0 * cube(state[5]) * cube(state[2]) + total
     head_out[...] = (head - resid / diagonal).reshape(256, 128)
     new_cond, new_water = closure(head_out[...], *[state[f] for f in range(1, fields)])
     cond_out[...] = new_cond
     water_out[...] = new_water
-    emit(head_out, cond_out, to_right, to_left, up, down)
+    emit(head_out, cond_out, near, far, to_core, to_chip)
 
 
 def leave(ref, cells):
@@ -368,8 +397,8 @@
         ref[0, :, 128 * c + 256 : 128 * c + 384] = turned[blocks:]
 
 
-def residual_kernel(head, cond, water, left, right, below, above, near, head_out, resid_out, planes):
-    flux, _ = balance(cube(head[...]), cube(cond[...]), left, right, below, above, near, planes)
+def residual_kernel(head, cond, water, near_in, far_in, core, chip, table, head_out, resid_out, planes):
+    flux, _ = balance(cube(head[...]), cube(cond[...]), near_in, far_in, core, chip, table, planes)
     leave(resid_out, water[...] - flux.reshape(256, 128))
     leave(head_out, head[...])
 
@@ -378,44 +407,58 @@
     return jax.ShapeDtypeStruct(dims, f32)
 
 
-def call(kernel, outs, scratch, *operands, source=pltpu.VMEM, limit=vmem):
-    whole = pl.BlockSpec(memory_space=pltpu.VMEM)
+def call(kernel, outs, scratch, *operands, space=pltpu.VMEM, limit=vmem):
+    whole = pl.BlockSpec(memory_space=space)
     return pl.pallas_call(
         kernel,
         out_shape=outs,
-        in_specs=[pl.BlockSpec(memory_space=source)] * len(operands),
+        in_specs=[whole] * len(operands),
         out_specs=[whole] * len(outs),
         scratch_shapes=scratch,
         compiler_params=pltpu.CompilerParams(vmem_limit_bytes=limit),
     )(*operands)
 
 
-def exchange(to_right, to_left, up, down):
-    def shifted(x, axis, step):
-        size = lax.axis_size(axis)
-        return lax.ppermute(x, axis, [(i, (i + step) % size) for i in range(size)])
-
-    return (
-        shifted(to_right, "dom", 1),
-        shifted(to_left, "dom", -1),
-        shifted(up, "depth", 1),
-        shifted(down, "depth", -1),
-    )
+def exchange(near, far, core, chip):
+    lateral, columns = lax.axis_size("dom"), lax.axis_size("depth")
+
+    def swap(x, partner):
+        places = [(t, d) for t in range(lateral) for d in range(columns)]
+        pairs = []
+        for t, d in places:
+            u, e = partner(t, d)
+            pairs.append((t * columns + d, u * columns + e))
+        return lax.ppermute(x, ("dom", "depth"), pairs)
+
+    def far_of(t, d):
+        u = ((t + 1) ^ 1) - 1
+        return (u, d) if 0 <= u < lateral else (t, d ^ 1)
+
+    def chip_of(t, d):
+        e = ((d + 1) ^ 1) - 1
+        return (t, e) if 0 <= e < columns else (t ^ 1, d)
+
+    far = swap(far, far_of)
+    near = swap(near, lambda t, d: (t ^ 1, d))
+    chip = swap(chip, chip_of)
+    core = swap(core, lambda t, d: (t, d ^ 1))
+    return near, far, core, chip
+
+
+def pack(head, water_prev, alpha, shape_n, theta_r, theta_s, sat_cond, refine, destination):
+    outs = [shape(rows, blocks, 128), shape(peers, chunk, 128), shape(blocks, 128)]
+    scratch = [pltpu.SMEM((blocks,), jnp.int32)] * 2 + [pltpu.VMEM((1, blocks, 512), f32)] * 7
+    scratch += [pltpu.VMEM(out.shape, f32) for out in outs]
+    scratch += [pltpu.VMEM((blocks * late, 128), f32), pltpu.VMEM((blocks * early, 128), f32)]
+    scratch += [pltpu.VMEM((blocks, 128), jnp.int32), pltpu.SMEM((peers,), jnp.int32), pltpu.SMEM((blocks,), jnp.int32)]
+    scratch += [pltpu.SemaphoreType.DMA((9,))] * 2
+    operands = (refine, destination, alpha, shape_n, sat_cond, theta_s, theta_r, head, water_prev)
+    return call(pack_kernel, outs, scratch, *operands, space=pltpu.HBM, limit=64 * 1024 * 1024)
 
 
 def on_device(head, water_prev, alpha, shape_n, theta_r, theta_s, sat_cond, refine, destination, neighbours):
-    send, own, stay = call(
-        pack_kernel,
-        [shape(peers * chunk, 128), shape(rows * blocks, 128), shape(blocks, 128)],
-        [pltpu.VMEM((blocks * rows, 128), f32), pltpu.VMEM((blocks, 128), jnp.int32), pltpu.SMEM((peers,), jnp.int32)]
-        + [pltpu.SMEM((blocks,), jnp.int32)] * 2
-        + [pltpu.VMEM((1, blocks, 512), f32)] * 7
-        + [pltpu.SemaphoreType.DMA((9,))],
-        refine, destination, head, water_prev, alpha, shape_n, theta_r, theta_s, sat_cond,
-        source=pltpu.HBM,
-        limit=64 * 1024 * 1024,
-    )
-    recv = lax.all_to_all(send.reshape(peers, chunk, 128), "dom", 0, 0, tiled=True)
+    own, send, stay = pack(head, water_prev, alpha, shape_n, theta_r, theta_s, sat_cond, refine, destination)
+    recv = lax.all_to_all(send, "dom", 0, 0, tiled=True)
     (settled,) = call(settle_kernel, [shape(fields, 256, 128)], [], own, stay)
     near = neighbours.reshape(blocks, 16).T
     near = jnp.concatenate([near, near], axis=1)

time: 54.2 us -> 45.1 us (0.83)
  the two profiles are of different devices: /device:TPU:97 before, /device:TPU:99 now
where the time goes in v2:
time: 45.1 us; the launch traced here: 44.9 us
  starting transfers between devices  21.5 us (48%)
  waiting for transfers between devices  14.6 us (32%)
  Pallas kernels  7.97 us (18%)
  between operations  0.72 us (2%)
    ppermute x8, starting transfers between devices, swap(): return lax.ppermute(x, ('dom', 'depth'), pairs)  14.4 us
    all_to_all x1, waiting for transfers between devices, on_device(): recv = lax.all_to_all(send, 'dom', 0, 0, tiled=True)  11.3 us
    pallas_call x5, Pallas kernels, call(): pl.pallas_call(kernel, out_shape=outs, in_specs=[whole] * len(operands),...  7.97 us
    all_to_all x1, starting transfers between devices, on_device(): recv = lax.all_to_all(send, 'dom', 0, 0, tiled=True)  7.06 us
    ppermute x8, waiting for transfers between devices, swap(): return lax.ppermute(x, ('dom', 'depth'), pairs)  3.32 us
  transfers between devices with their start and end apart: 9, of which 3 were waited for; matrix products, arithmetic and copies ran while one was open for 0% of the time, Pallas kernels for 1%

profile of v2, /device:TPU:99, one launch (start us, length us, event | category | flops | bytes accessed | tf_op | source)
XLA Modules:
  0.0 44.9 jit_solution(15493272483996635005)
XLA Ops:
  0.6 4.2 %shard_map.113 = (f32[24,64,128]{2,1,0:T(8,128)}, f32[16,104,128]{2,1,0:T(8,128)}, f32[64,128]{1,0:T(8,128)}) custom-call(s32[64]{0:T(128)} %refs_0_.1, s32[64]{0:T(128)} %refs_1_.1, f32[1,64,512]{2,1,0:T(8,128)} %refs_2_.1, f32[1,64,512]{2,1,0:T(8,128)} %refs_3_.1, f32[1,64,512]{2,1,0:T(8,128)} %refs_4_.1, f32[1,64,512]{2,1,0:T(8,128)} %refs_5_.1, ...), custom_call_target="tpu_custom_call" | custom-call | tf_op jit(solution)/shard_map/pallas_call | solution.py:412
  4.8 0.0 copy-start
  4.8 0.0 copy-start.1
  4.8 7.1 %all-to-all-start = ((f32[16,104,128]{2,1,0:T(8,128)}), f32[16,104,128]{2,1,0:T(8,128)S(1)}, u32[]{:S(2)}, u32[]{:S(2)}) async-start(f32[16,104,128]{2,1,0:T(8,128)} %get-tuple-element.19), calls=%async_computation | async-start | bytes 1703936 | tf_op jit(solution)/shard_map/all_to_all | solution.py:461
  11.9 0.0 copy-done
  11.9 0.0 copy-done.1
  11.9 0.5 %shard_map.114.settled = f32[6,256,128]{2,1,0:T(8,128)S(1)} custom-call(f32[24,64,128]{2,1,0:T(8,128)S(1)} %copy-done, f32[64,128]{1,0:T(8,128)S(1)} %copy-done.1), custom_call_target="tpu_custom_call" | custom-call | tf_op jit(solution)/shard_map/pallas_call | solution.py:412
  12.5 11.3 %all-to-all-done = f32[16,104,128]{2,1,0:T(8,128)S(1)} async-done(((f32[16,104,128]{2,1,0:T(8,128)}), f32[16,104,128]{2,1,0:T(8,128)S(1)}, u32[]{:S(2)}, u32[]{:S(2)}) %all-to-all-start) | async-done | bytes 852000 | tf_op jit(solution)/shard_map/all_to_all | solution.py:461
  23.7 0.8 %shard_map.115 = (f32[6,256,128]{2,1,0:T(8,128)S(1)}, f32[256,128]{1,0:T(8,128)S(1)}, f32[256,128]{1,0:T(8,128)S(1)}, f32[64,128]{1,0:T(8,128)S(1)}, f32[64,128]...) custom-call(f32[1664,128]{1,0:T(8,128)S(1)} %bitcast.4, f32[6,256,128]{2,1,0:T(8,128)S(1)} %shard_map.114.settled), custom_call_target="tpu_custom_call" | custom-call | tf_op jit(solution)/shard_map/pallas_call | solution.py:412
  24.6 0.0 copy-start.2
  24.6 0.4 collective-permute-start
  25.0 2.9 %collective-permute-start.1 = (f32[64,128]{1,0:T(8,128)S(1)}, f32[64,128]{1,0:T(8,128)S(1)}, u32[]{:S(2)}, u32[]{:S(2)}) collective-permute-start(f32[64,128]{1,0:T(8,128)S(1)} %get-tuple-element.26), channel_id=1, source_target_pairs={{0,1},{1,0},{2,3},{3,2},{4,5},{5,4},{6,7},{7,6},{8,9},{9,8},{10,11... | collective-permute-start | bytes 98312 | tf_op jit(solution)/shard_map/ppermute | solution.py:431
  27.9 2.4 %collective-permute-start.2 = (f32[64,128]{1,0:T(8,128)S(1)}, f32[64,128]{1,0:T(8,128)S(1)}, u32[]{:S(2)}, u32[]{:S(2)}) collective-permute-start(f32[64,128]{1,0:T(8,128)S(1)} %get-tuple-element.27), channel_id=1, source_target_pairs={{0,1},{1,0},{2,3},{3,2},{4,5},{5,4},{6,7},{7,6},{8,9},{9,8},{10,11... | collective-permute-start | bytes 98312 | tf_op jit(solution)/shard_map/ppermute | solution.py:431
  30.3 2.7 %collective-permute-start.3 = (f32[64,128]{1,0:T(8,128)S(1)}, f32[64,128]{1,0:T(8,128)S(1)}, u32[]{:S(2)}, u32[]{:S(2)}) collective-permute-start(f32[64,128]{1,0:T(8,128)S(1)} %get-tuple-element.28), channel_id=1, source_target_pairs={{0,16},{1,2},{2,1},{3,4},{4,3},{5,6},{6,5},{7,8},{8,7},{9,10},{10,... | collective-permute-start | bytes 98312 | tf_op jit(solution)/shard_map/ppermute | solution.py:431
  33.0 0.0 copy-done.2
  33.0 0.1 pad_add_fusion.table
  33.1 0.0 collective-permute-done.near_in
  33.1 0.0 collective-permute-done.1.far_in
  33.1 0.0 collective-permute-done.2.core
  33.1 1.7 %collective-permute-done.3.chip = f32[64,128]{1,0:T(8,128)S(1)} collective-permute-done((f32[64,128]{1,0:T(8,128)S(1)}, f32[64,128]{1,0:T(8,128)S(1)}, u32[]{:S(2)}, u32[]{:S(2)}) %collective-permute-start.3) | collective-permute-done | bytes 32800 | tf_op jit(solution)/shard_map/ppermute | solution.py:431
  34.8 1.0 %shard_map.116 = (f32[256,128]{1,0:T(8,128)S(1)}, f32[256,128]{1,0:T(8,128)S(1)}, f32[256,128]{1,0:T(8,128)S(1)}, f32[64,128]{1,0:T(8,128)S(1)}, f32[64,128]{1,0...) custom-call(f32[6,256,128]{2,1,0:T(8,128)S(1)} %get-tuple-element.22.state, ...), custom_call_target="tpu_custom_call" | custom-call | tf_op jit(solution)/shard_map/pallas_call | solution.py:412
  35.9 0.1 collective-permute-start.4
  36.0 2.6 %collective-permute-start.5 = (f32[64,128]{1,0:T(8,128)S(1)}, f32[64,128]{1,0:T(8,128)S(1)}, u32[]{:S(2)}, u32[]{:S(2)}) collective-permute-start(f32[64,128]{1,0:T(8,128)S(1)} %get-tuple-element.33), channel_id=1, source_target_pairs={{0,1},{1,0},{2,3},{3,2},{4,5},{5,4},{6,7},{7,6},{8,9},{9,8},{10,11... | collective-permute-start | bytes 98312 | tf_op jit(solution)/shard_map/ppermute | solution.py:431
  38.6 0.0 collective-permute-start.6
  38.6 3.3 %collective-permute-start.7 = (f32[64,128]{1,0:T(8,128)S(1)}, f32[64,128]{1,0:T(8,128)S(1)}, u32[]{:S(2)}, u32[]{:S(2)}) collective-permute-start(f32[64,128]{1,0:T(8,128)S(1)} %get-tuple-element.35), channel_id=1, source_target_pairs={{0,16},{1,2},{2,1},{3,4},{4,3},{5,6},{6,5},{7,8},{8,7},{9,10},{10,... | collective-permute-start | bytes 98312 | tf_op jit(solution)/shard_map/ppermute | solution.py:431
  41.9 0.0 collective-permute-done.4.near_in
  41.9 0.0 collective-permute-done.5.far_in
  41.9 0.0 collective-permute-done.6.core
  41.9 1.6 %collective-permute-done.7.chip = f32[64,128]{1,0:T(8,128)S(1)} collective-permute-done((f32[64,128]{1,0:T(8,128)S(1)}, f32[64,128]{1,0:T(8,128)S(1)}, u32[]{:S(2)}, u32[]{:S(2)}) %collective-permute-start.7) | collective-permute-done | bytes 32800 | tf_op jit(solution)/shard_map/ppermute | solution.py:431
  43.5 1.4 %shard_map.117 = (f32[1,64,512]{2,1,0:T(8,128)}, f32[1,64,512]{2,1,0:T(8,128)}) custom-call(f32[256,128]{1,0:T(8,128)S(1)} %get-tuple-element.29.head, f32[256,128]{1,0:T(8,128)S(1)} %get-tuple-element.30.cond, f32[256,128]{1,0:T(8,128)S(1)} %get-tuple-element.31.water, f32[64,128]{1,0:T(8,128)S(1)} %collective-permute-done.4.near_in, ...), custom_call_target="tpu_custom_call" | custom-call | tf_op jit(solution)/shard_map/pallas_call | solution.py:412
Async XLA Ops:
  4.8 7.1 %copy-start = (f32[24,64,128]{2,1,0:T(8,128)S(1)}, f32[24,64,128]{2,1,0:T(8,128)}, u32[]{:S(2)}) copy-start(f32[24,64,128]{2,1,0:T(8,128)} %get-tuple-element.20.own) | copy-start | bytes 2359300
  4.8 7.1 %copy-start.1 = (f32[64,128]{1,0:T(8,128)S(1)}, f32[64,128]{1,0:T(8,128)}, u32[]{:S(2)}) copy-start(f32[64,128]{1,0:T(8,128)} %get-tuple-element.21.stay) | copy-start | bytes 98308
  4.8 18.9 %all-to-all-start = ((f32[16,104,128]{2,1,0:T(8,128)}), f32[16,104,128]{2,1,0:T(8,128)S(1)}, u32[]{:S(2)}, u32[]{:S(2)}) async-start(f32[16,104,128]{2,1,0:T(8,128)} %get-tuple-element.19), calls=%async_computation | async-start | bytes 1703936 | tf_op jit(solution)/shard_map/all_to_all | solution.py:461
  24.6 8.4 %copy-start.2 = (s32[64,4,4]{0,2,1:T(4,128)S(1)}, s32[64,4,4]{0,2,1:T(4,128)}, u32[]{:S(2)}) copy-start(s32[64,4,4]{0,2,1:T(4,128)} %param.19) | copy-start | bytes 12292
  24.6 8.5 %collective-permute-start = (f32[64,128]{1,0:T(8,128)S(1)}, f32[64,128]{1,0:T(8,128)S(1)}, u32[]{:S(2)}, u32[]{:S(2)}) collective-permute-start(f32[64,128]{1,0:T(8,128)S(1)} %get-tuple-element.25), channel_id=1, source_target_pairs={{0,16},{1,17},{2,18},{3,19},{4,20},{5,21},{6,22},{7,23},{8,24},{9,... | collective-permute-start | bytes 98312 | tf_op jit(solution)/shard_map/ppermute | solution.py:431
  25.0 8.1 %collective-permute-start.1 = (f32[64,128]{1,0:T(8,128)S(1)}, f32[64,128]{1,0:T(8,128)S(1)}, u32[]{:S(2)}, u32[]{:S(2)}) collective-permute-start(f32[64,128]{1,0:T(8,128)S(1)} %get-tuple-element.26), channel_id=1, source_target_pairs={{0,1},{1,0},{2,3},{3,2},{4,5},{5,4},{6,7},{7,6},{8,9},{9,8},{10,11... | collective-permute-start | bytes 98312 | tf_op jit(solution)/shard_map/ppermute | solution.py:431
  27.9 5.2 %collective-permute-start.2 = (f32[64,128]{1,0:T(8,128)S(1)}, f32[64,128]{1,0:T(8,128)S(1)}, u32[]{:S(2)}, u32[]{:S(2)}) collective-permute-start(f32[64,128]{1,0:T(8,128)S(1)} %get-tuple-element.27), channel_id=1, source_target_pairs={{0,1},{1,0},{2,3},{3,2},{4,5},{5,4},{6,7},{7,6},{8,9},{9,8},{10,11... | collective-permute-start | bytes 98312 | tf_op jit(solution)/shard_map/ppermute | solution.py:431
  30.3 4.6 %collective-permute-start.3 = (f32[64,128]{1,0:T(8,128)S(1)}, f32[64,128]{1,0:T(8,128)S(1)}, u32[]{:S(2)}, u32[]{:S(2)}) collective-permute-start(f32[64,128]{1,0:T(8,128)S(1)} %get-tuple-element.28), channel_id=1, source_target_pairs={{0,16},{1,2},{2,1},{3,4},{4,3},{5,6},{6,5},{7,8},{8,7},{9,10},{10,... | collective-permute-start | bytes 98312 | tf_op jit(solution)/shard_map/ppermute | solution.py:431
  35.9 6.0 %collective-permute-start.4 = (f32[64,128]{1,0:T(8,128)S(1)}, f32[64,128]{1,0:T(8,128)S(1)}, u32[]{:S(2)}, u32[]{:S(2)}) collective-permute-start(f32[64,128]{1,0:T(8,128)S(1)} %get-tuple-element.32), channel_id=1, source_target_pairs={{0,16},{1,17},{2,18},{3,19},{4,20},{5,21},{6,22},{7,23},{8,24},{9,... | collective-permute-start | bytes 98312 | tf_op jit(solution)/shard_map/ppermute | solution.py:431
  36.0 5.9 %collective-permute-start.5 = (f32[64,128]{1,0:T(8,128)S(1)}, f32[64,128]{1,0:T(8,128)S(1)}, u32[]{:S(2)}, u32[]{:S(2)}) collective-permute-start(f32[64,128]{1,0:T(8,128)S(1)} %get-tuple-element.33), channel_id=1, source_target_pairs={{0,1},{1,0},{2,3},{3,2},{4,5},{5,4},{6,7},{7,6},{8,9},{9,8},{10,11... | collective-permute-start | bytes 98312 | tf_op jit(solution)/shard_map/ppermute | solution.py:431
  38.6 3.3 %collective-permute-start.6 = (f32[64,128]{1,0:T(8,128)S(1)}, f32[64,128]{1,0:T(8,128)S(1)}, u32[]{:S(2)}, u32[]{:S(2)}) collective-permute-start(f32[64,128]{1,0:T(8,128)S(1)} %get-tuple-element.34), channel_id=1, source_target_pairs={{0,1},{1,0},{2,3},{3,2},{4,5},{5,4},{6,7},{7,6},{8,9},{9,8},{10,11... | collective-permute-start | bytes 98312 | tf_op jit(solution)/shard_map/ppermute | solution.py:431
  38.6 4.9 %collective-permute-start.7 = (f32[64,128]{1,0:T(8,128)S(1)}, f32[64,128]{1,0:T(8,128)S(1)}, u32[]{:S(2)}, u32[]{:S(2)}) collective-permute-start(f32[64,128]{1,0:T(8,128)S(1)} %get-tuple-element.35), channel_id=1, source_target_pairs={{0,16},{1,2},{2,1},{3,4},{4,3},{5,6},{6,5},{7,8},{8,7},{9,10},{10,... | collective-permute-start | bytes 98312 | tf_op jit(solution)/shard_map/ppermute | solution.py:431

commit v3 on v2

--- a/solution.py
+++ b/solution.py
@@ -27,6 +27,10 @@
     return lax.gather(x, index[..., None], numbers, (1, 1), mode=lax.GatherScatterMode.PROMISE_IN_BOUNDS)
 
 
+def seat(device):
+    return peers - 1 - ((device & 3) * 4 + (device >> 2))
+
+
 def iota(shape, axis):
     return lax.broadcasted_iota(jnp.int32, shape, axis)
 
@@ -42,10 +46,23 @@
     return flat.reshape(x.shape)
 
 
+def plane_weights(bit_y, bit_z):
+    source, fine = iota((128, 128), 0), iota((128, 128), 1)
+
+    def line(bit, shift):
+        coarse, index = (source >> shift) & 7, (fine >> shift) & 7
+        near = 4 * bit + (index >> 1)
+        far = jnp.clip(near + 2 * (index & 1) - 1, 0, 7)
+        return jnp.where(coarse == near, 0.75, 0.0) + jnp.where(coarse == far, 0.25, 0.0)
+
+    weight = line(bit_y, 3) * line(bit_z, 0)
+    return jnp.where((source >> 6) == (fine >> 6), weight, 0.0).astype(jnp.bfloat16)
+
+
 def pack_kernel(*refs):
     sources, targets, refs = refs[:9], refs[9:12], refs[12:]
     held, (own, send, stay), refs = refs[:9], refs[9:12], refs[12:]
-    work_late, work_early, flags, count, slot_early, sems_in, sems_out = refs
+    work_late, work_early, weights, flags, count, slot_early, sems_in, sems_out = refs
     arriving = [pltpu.make_async_copy(source, ref, sems_in.at[n]) for n, (source, ref) in enumerate(zip(sources, held))]
     for copy in arriving:
         copy.start()
@@ -56,6 +73,10 @@
         copy.start()
         leaving.append(copy)
 
+    for bits in range(4):
+        table = plane_weights(bits // 2, bits % 2)
+        for n in range(2):
+            weights[128 * n : 128 * n + 128, 128 * bits : 128 * bits + 128] = table
     refine, destination = held[:2]
     me = lax.axis_index("dom")
     for peer in range(peers):
@@ -88,12 +109,6 @@
         ]
         return [lane_take(chosen[c], plain_index[c % 2]) for c in range(4)]
 
-    side_y = jnp.clip(plain_y + 2 * (fine_y & 1) - 1, 0, 7)
-    side_z = jnp.clip(plain_z + 2 * (fine_z & 1) - 1, 0, 7)
-    near_y = half * 64 + plain_y * 8 + fine_z
-    far_y = half * 64 + side_y * 8 + fine_z
-    near_z = (lane & 120) + plain_z
-    far_z = (lane & 120) + side_z
     lower = lane < 64
 
     def smooth(v):
@@ -112,12 +127,18 @@
             jnp.where(lower, base_r[0], base[1]),
             jnp.where(lower, base[1], jnp.where(up_x, v[3], r[2])),
         ]
+        x = jnp.concatenate([0.75 * near[c] + 0.25 * far[c] for c in range(4)], axis=0)
+        high = x.astype(jnp.bfloat16)
+        x = x - high.astype(f32)
+        middle = x.astype(jnp.bfloat16)
+        x = (x - middle.astype(f32)).astype(jnp.bfloat16)
+        y = jnp.dot(jnp.concatenate([high, middle], axis=1), weights[...], preferred_element_type=f32)
+        y = y + jnp.dot(x, weights[:128, :], preferred_element_type=f32)
         result = []
         for c in range(4):
-            x = 0.75 * near[c] + 0.25 * far[c]
-            x = 0.75 * lane_take(x, near_y) + 0.25 * lane_take(x, far_y)
-            x = 0.75 * lane_take(x, near_z) + 0.25 * lane_take(x, far_z)
-            result.append(jnp.where(kept, v[c], x))
+            parts = [y[blocks * c : blocks * (c + 1), 128 * n : 128 * n + 128] for n in range(4)]
+            parts = [jnp.where(bit_z == 1, parts[n + 1], parts[n]) for n in (0, 2)]
+            result.append(jnp.where(kept, v[c], jnp.where(bit_y == 1, parts[1], parts[0])))
         return result
 
     def keep(f, values, work, size, first):
@@ -138,15 +159,16 @@
     for block in range(blocks):
         target = destination[block]
         owner = target >> 6
+        place = seat(owner)
         used = count[owner] & (room - 1)
         count[owner] = used + 1
         spot = jnp.full((1, 128), target & 63, jnp.int32).astype(f32)
         slot_early[block] = room * late + used * early
         start = pl.ds(pl.multiple_of(used * late, 8), late)
-        send[owner, start, :] = work_late[block * late : block * late + late, :]
-        send[owner, pl.ds(room * rows + used, 1), :] = spot
+        send[place, start, :] = work_late[block * late : block * late + late, :]
+        send[place, pl.ds(room * rows + used, 1), :] = spot
         stay[block : block + 1, :] = jnp.where(owner == me, spot, -1.0)
-    send[me, rows * room :, :] = jnp.full((8, 128), -1.0, f32)
+    send[seat(me), rows * room :, :] = jnp.full((8, 128), -1.0, f32)
     depart(send.at[:, : room * late], targets[1].at[:, : room * late])
     depart(stay, targets[2])
 
@@ -154,7 +176,7 @@
     keep(1, [x - y for x, y in zip(plain(low), smooth(get(8)))], work_early, early, 0)
     for block in range(blocks):
         start = pl.ds(pl.multiple_of(slot_early[block], 8), early)
-        send[destination[block] >> 6, start, :] = work_early[block * early : block * early + early, :]
+        send[seat(destination[block] >> 6), start, :] = work_early[block * early : block * early + early, :]
     depart(send.at[:, room * late :], targets[1].at[:, room * late :])
     for copy in leaving:
         copy.wait()
@@ -225,7 +247,7 @@
         chip[32 * q : 32 * q + 32, :] = jnp.where(even("depth"), bottom, top)
 
 
-def arrive_kernel(recv, settled, state, cond_out, water_out, *outgoing):
+def arrive_kernel(recv, settled, head_out, state, cond_out, water_out, *outgoing):
     def slots(start):
         return [recv[pl.ds(start(o), peers, stride=chunk), :] for o in range(room)]
 
@@ -243,6 +265,7 @@
             cells = jnp.concatenate(parts, axis=0).T
             span = slice(128 * c, 128 * c + 128)
             state[f, span, :] = jnp.where(has, lane_take(cells, index), settled[f, span, :])
+    head_out[...] = state[0]
     cond, water = closure(*[state[f] for f in range(fields)])
     cond_out[...] = cond
     water_out[...] = water
@@ -326,68 +349,82 @@
     return jnp.stack(face_x), face_y[0], face_y[1]
 
 
-def balance(head, cond, near_in, far_in, core, chip, near, planes):
+def inside_kernel(head_ref, cond_ref, flux_out, total_out, *head_out):
+    head, cond = cube(head_ref[...]), cube(cond_ref[...])
+    lower = iota((8, 8, 128), 2) < 64
+    level_k = iota((256, 128), 0) & 7
+
+    def pair(k, other_k, h, other_h):
+        face_k = k + other_k
+        return face_k * (other_h - h), face_k
+
+    def spread(below, above, sign):
+        return [above[0]] + [above[n] + sign * below[n - 1] for n in range(1, len(above))] + [sign * below[-1]]
+
+    steps = [pair(cond[n], cond[n + 1], head[n], head[n + 1]) for n in range(3)]
+    cross = [jnp.where(lower, x, 0.0) for x in pair(cond[3], turn(cond[0], 64), head[3], turn(head[0], 64))]
+    up_h, up_k = turn(head_ref[...], 255, 0), turn(cond_ref[...], 255, 0)
+    rise = pair(cond_ref[...], up_k, head_ref[...], up_h + 1.0)
+    rise = [jnp.where(level_k < 7, x, 0.0) for x in rise]
+    along = pair(cond[:, :7], cond[:, 1:], head[:, :7], head[:, 1:])
+    for q, (out, sign) in enumerate(((flux_out, -1.0), (total_out, 1.0))):
+        x = spread([step[q] for step in steps], [step[q] for step in steps], sign)
+        x[3] = x[3] + cross[q]
+        x[0] = x[0] + sign * turn(cross[q], 64)
+        empty = jnp.zeros((4, 1, 8, 128), f32)
+        y = jnp.concatenate([along[q], empty], axis=1) + sign * jnp.concatenate([empty, along[q]], axis=1)
+        z = rise[q] + sign * turn(rise[q], 1, 0)
+        out[...] = (jnp.stack(x) + y).reshape(256, 128) + z
+    for ref in head_out:
+        leave(ref, head_ref[...])
+
+
+def balance(head_ref, cond_ref, flux_in, total_in, near_in, far_in, core, chip, near, planes):
     table = Table(near)
     level = lax.axis_index("depth")
+    head, cond = cube(head_ref[...]), cube(cond_ref[...])
     left = jnp.where(even("dom"), far_in[...], near_in[...]).reshape(8, 8, 128)
     right = jnp.where(even("dom"), near_in[...], far_in[...]).reshape(8, 8, 128)
+    around_h, *sides_h = ghosts(head, left, right, 0, table)
+    around_k, *sides_k = ghosts(cond, left, right, 1, table)
+    lower = iota((8, 8, 128), 2) < 64
+
+    def term(on, k, other_k, h, other_h):
+        face_k = jnp.where(on, k + other_k, 0.0)
+        return jnp.where(on, face_k * (other_h - h), 0.0), face_k
+
+    edge_k, edge_h = jnp.where(lower, cond[0], cond[3]), jnp.where(lower, head[0], head[3])
+    x = term(table.on_x, edge_k, around_k, edge_h, around_h)
+    y = [term(table.on_y[n], cond[:, j], sides_k[n], head[:, j], sides_h[n]) for n, j in ((0, 0), (1, 7))]
     below = jnp.where(even("depth"), chip[...], core[...])
     above = jnp.where(even("depth"), core[...], chip[...])
-    ghost_h = ghosts(head, left, right, 0, table)
-    ghost_k = ghosts(cond, left, right, 1, table)
-    for q in range(2):
-        planes[2 * q, pl.ds(0, 32, stride=8), :] = below[32 * q : 32 * q + 32, :]
-        planes[2 * q + 1, pl.ds(7, 32, stride=8), :] = above[32 * q : 32 * q + 32, :]
+    last = lax.axis_size("depth") - 1
+    for n, (plane, k, on, lift) in enumerate(((below, 0, level > 0, -1.0), (above, 7, level < last, 1.0))):
+        own_h, own_k = head_ref[pl.ds(k, 32, stride=8), :], cond_ref[pl.ds(k, 32, stride=8), :]
+        for q, value in enumerate(term(on, own_k, plane[32:], own_h, plane[:32] + lift)):
+            planes[2 * n + q, pl.ds(k, 32, stride=8), :] = value
     level_k = iota((4, 8, 8, 128), 2)
-    low = iota((8, 8, 128), 2) < 64
-
-    def neighbours(x, ghost, q):
-        around, y2, y3 = ghost
-        x0, x3 = turn(x[0], 64), turn(x[3], 64)
-        return [
-            jnp.concatenate([jnp.where(low, around, x3)[None], x[:3]], axis=0),
-            jnp.concatenate([x[1:], jnp.where(low, x0, around)[None]], axis=0),
-            jnp.concatenate([y2[:, None], x[:, :7]], axis=1),
-            jnp.concatenate([x[:, 1:], y3[:, None]], axis=1),
-            jnp.where(level_k == 0, cube(planes[2 * q]), cube(turn(x.reshape(256, 128), 1, 0))),
-            jnp.where(level_k == 7, cube(planes[2 * q + 1]), cube(turn(x.reshape(256, 128), 255, 0))),
-        ]
-
-    slab = iota((4, 8, 8, 128), 0)
-    row_j = iota((4, 8, 8, 128), 1)
-    lower = iota((4, 8, 8, 128), 3) < 64
-    off_x, off_y = ~table.on_x, [~on for on in table.on_y]
-    closed = [
-        (slab == 0) & lower & off_x,
-        (slab == 3) & ~lower & off_x,
-        (row_j == 0) & off_y[0],
-        (row_j == 7) & off_y[1],
-        (level_k == 0) & (level == 0),
-        (level_k == 7) & (level == lax.axis_size("depth") - 1),
-    ]
-    flux = total = None
-    pairs = zip(neighbours(head, ghost_h, 0), neighbours(cond, ghost_k, 1), closed)
-    for direction, (near_h, near_k, shut) in enumerate(pairs):
-        face_k = jnp.where(shut, 0.0, cond + near_k)
-        lift = (0.0, 0.0, 0.0, 0.0, -1.0, 1.0)[direction]
-        part = jnp.where(shut, 0.0, face_k * (near_h - head + lift))
-        flux = part if flux is None else flux + part
-        total = face_k if total is None else total + face_k
-    return 0.5 * flux, 0.5 * total
-
-
-def newton_kernel(
-    state, cond, water, near_in, far_in, core, chip, table, head_out, cond_out, water_out, near, far, to_core, to_chip, planes
-):
-    head = cube(state[0])
-    flux, total = balance(head, cube(cond[...]), near_in, far_in, core, chip, table, planes)
+    sums = []
+    for q, ref in enumerate((flux_in, total_in)):
+        z = jnp.where(level_k == 0, cube(planes[q]), jnp.where(level_k == 7, cube(planes[2 + q]), 0.0))
+        total = cube(ref[...]) + z
+        slabs = [total[0] + jnp.where(lower, x[q], 0.0), total[1], total[2], total[3] + jnp.where(lower, 0.0, x[q])]
+        total = jnp.stack(slabs)
+        rows_j = [total[:, :1] + y[0][q][:, None], total[:, 1:7], total[:, 7:] + y[1][q][:, None]]
+        sums.append(0.5 * jnp.concatenate(rows_j, axis=1))
+    return sums
+
+
+def newton_kernel(state, cond, water, flux, total, *refs):
+    (near_in, far_in, core, chip, table), (head_out, cond_out, water_out, *outgoing), planes = refs[:5], refs[5:12], refs[12]
+    flux, total = balance(state.at[0], cond, flux, total, near_in, far_in, core, chip, table, planes)
     resid = cube(water[...]) - flux
     diagonal = 4.0 * cube(state[5]) * cube(state[2]) + total
-    head_out[...] = (head - resid / diagonal).reshape(256, 128)
+    head_out[...] = (cube(state[0]) - resid / diagonal).reshape(256, 128)
     new_cond, new_water = closure(head_out[...], *[state[f] for f in range(1, fields)])
     cond_out[...] = new_cond
     water_out[...] = new_water
-    emit(head_out, cond_out, near, far, to_core, to_chip)
+    emit(head_out, cond_out, *outgoing)
 
 
 def leave(ref, cells):
@@ -397,10 +434,9 @@
         ref[0, :, 128 * c + 256 : 128 * c + 384] = turned[blocks:]
 
 
-def residual_kernel(head, cond, water, near_in, far_in, core, chip, table, head_out, resid_out, planes):
-    flux, _ = balance(cube(head[...]), cube(cond[...]), near_in, far_in, core, chip, table, planes)
+def residual_kernel(head, cond, water, flux, total, near_in, far_in, core, chip, table, resid_out, planes):
+    flux, _ = balance(head, cond, flux, total, near_in, far_in, core, chip, table, planes)
     leave(resid_out, water[...] - flux.reshape(256, 128))
-    leave(head_out, head[...])
 
 
 def shape(*dims):
@@ -450,6 +486,7 @@
     scratch = [pltpu.SMEM((blocks,), jnp.int32)] * 2 + [pltpu.VMEM((1, blocks, 512), f32)] * 7
     scratch += [pltpu.VMEM(out.shape, f32) for out in outs]
     scratch += [pltpu.VMEM((blocks * late, 128), f32), pltpu.VMEM((blocks * early, 128), f32)]
+    scratch += [pltpu.VMEM((256, 512), jnp.bfloat16)]
     scratch += [pltpu.VMEM((blocks, 128), jnp.int32), pltpu.SMEM((peers,), jnp.int32), pltpu.SMEM((blocks,), jnp.int32)]
     scratch += [pltpu.SemaphoreType.DMA((9,))] * 2
     operands = (refine, destination, alpha, shape_n, sat_cond, theta_s, theta_r, head, water_prev)
@@ -458,25 +495,28 @@
 
 def on_device(head, water_prev, alpha, shape_n, theta_r, theta_s, sat_cond, refine, destination, neighbours):
     own, send, stay = pack(head, water_prev, alpha, shape_n, theta_r, theta_s, sat_cond, refine, destination)
-    recv = lax.all_to_all(send, "dom", 0, 0, tiled=True)
+    recv = lax.all_to_all(send, "dom", 0, 0, tiled=True, axis_index_groups=[sorted(range(peers), key=seat)])
     (settled,) = call(settle_kernel, [shape(fields, 256, 128)], [], own, stay)
     near = neighbours.reshape(blocks, 16).T
     near = jnp.concatenate([near, near], axis=1)
     cells, halo = shape(256, 128), [shape(64, 128)] * 4
-    state, cond, water, *outgoing = call(
+    head, state, cond, water, *outgoing = call(
         arrive_kernel,
-        [shape(fields, 256, 128), cells, cells] + halo,
+        [cells, shape(fields, 256, 128), cells, cells] + halo,
         [],
         recv.reshape(peers * chunk, 128), settled,
     )
+    incoming = exchange(*outgoing)
+    sums = call(inside_kernel, [cells, cells], [], head, cond)
     planes = [pltpu.VMEM((4, 256, 128), f32)]
-    new_head, cond, water, *outgoing = call(
-        newton_kernel, [cells] * 3 + halo, planes, state, cond, water, *exchange(*outgoing), near
+    head, cond, water, *outgoing = call(
+        newton_kernel, [cells] * 3 + halo, planes, state, cond, water, *sums, *incoming, near
     )
+    incoming = exchange(*outgoing)
     final = shape(1, blocks, 512)
-    return tuple(
-        call(residual_kernel, [final, final], planes, new_head, cond, water, *exchange(*outgoing), near)
-    )
+    *sums, new_head = call(inside_kernel, [cells, cells, final], [], head, cond)
+    (residual,) = call(residual_kernel, [final], planes, head, cond, water, *sums, *incoming, near)
+    return new_head, residual
 
 
 def solution(mesh):

time: 45.1 us -> 42.2 us (0.936)
  starting transfers between devices: 21.5 us -> 19.6 us
  waiting for transfers between devices: 14.6 us -> 13.2 us
    ppermute x8, starting transfers between devices: 14.4 us -> 11.6 us  [swap(): return lax.ppermute(x, ('dom', 'depth'), pairs)]
    ppermute x8, waiting for transfers between devices: 3.32 us -> 2.26 us  [swap(): return lax.ppermute(x, ('dom', 'depth'), pairs)]
    all_to_all x1, starting transfers between devices: 7.06 us -> 7.94 us  [on_device(): lax.all_to_all(send, 'dom', 0, 0, tiled=True, axis_index_groups=[sorted(r...]
    pallas_call x5 -> x7, Pallas kernels: 7.97 us -> 8.41 us  [call(): pl.pallas_call(kernel, out_shape=outs, in_specs=[whole] * len(operands),...]
  transfers between devices with their start and end apart: 9 -> 9, of which waited for: 3 -> 3; matrix products, arithmetic and copies ran while one was open for 0% -> 0% of each run, Pallas kernels for 1% -> 4%
where the time goes in v3:
time: 42.2 us; the launch traced here: 42 us
  starting transfers between devices  19.6 us (46%)
  waiting for transfers between devices  13.2 us (31%)
  Pallas kernels  8.41 us (20%)
  between operations  0.75 us (2%)
    ppermute x8, starting transfers between devices, swap(): return lax.ppermute(x, ('dom', 'depth'), pairs)  11.6 us
    all_to_all x1, waiting for transfers between devices, on_device(): lax.all_to_all(send, 'dom', 0, 0, tiled=True, axis_index_groups=[sorted(r...  10.9 us
    pallas_call x7, Pallas kernels, call(): pl.pallas_call(kernel, out_shape=outs, in_specs=[whole] * len(operands),...  8.41 us
    all_to_all x1, starting transfers between devices, on_device(): lax.all_to_all(send, 'dom', 0, 0, tiled=True, axis_index_groups=[sorted(r...  7.94 us
    ppermute x8, waiting for transfers between devices, swap(): return lax.ppermute(x, ('dom', 'depth'), pairs)  2.26 us
  transfers between devices with their start and end apart: 9, of which 3 were waited for; matrix products, arithmetic and copies ran while one was open for 0% of the time, Pallas kernels for 4%

profile of v3, /device:TPU:99, one launch (start us, length us, event | category | flops | bytes accessed | tf_op | source)
XLA Modules:
  0.0 42.0 jit_solution(12853487424185163784)
XLA Ops:
  0.6 3.9 %shard_map.113 = (f32[24,64,128]{2,1,0:T(8,128)}, f32[16,104,128]{2,1,0:T(8,128)}, f32[64,128]{1,0:T(8,128)}) custom-call(s32[64]{0:T(128)} %refs_0_.1, s32[64]{0:T(128)} %refs_1_.1, f32[1,64,512]{2,1,0:T(8,128)} %refs_2_.1, f32[1,64,512]{2,1,0:T(8,128)} %refs_3_.1, f32[1,64,512]{2,1,0:T(8,128)} %refs_4_.1, f32[1,64,512]{2,1,0:T(8,128)} %refs_5_.1, ...), custom_call_target="tpu_custom_call" | custom-call | tf_op jit(solution)/shard_map/pallas_call | solution.py:448
  4.5 0.0 copy-start
  4.5 0.0 copy-start.1
  4.6 7.9 %all-to-all-start = ((f32[16,104,128]{2,1,0:T(8,128)}), f32[16,104,128]{2,1,0:T(8,128)S(1)}, u32[]{:S(2)}, u32[]{:S(2)}) async-start(f32[16,104,128]{2,1,0:T(8,128)} %get-tuple-element.25), calls=%async_computation | async-start | bytes 1703936 | tf_op jit(solution)/shard_map/all_to_all | solution.py:498
  12.5 0.0 copy-done
  12.5 0.0 copy-done.1
  12.5 0.5 %shard_map.114.settled = f32[6,256,128]{2,1,0:T(8,128)S(1)} custom-call(f32[24,64,128]{2,1,0:T(8,128)S(1)} %copy-done, f32[64,128]{1,0:T(8,128)S(1)} %copy-done.1), custom_call_target="tpu_custom_call" | custom-call | tf_op jit(solution)/shard_map/pallas_call | solution.py:448
  13.0 10.9 %all-to-all-done = f32[16,104,128]{2,1,0:T(8,128)S(1)} async-done(((f32[16,104,128]{2,1,0:T(8,128)}), f32[16,104,128]{2,1,0:T(8,128)S(1)}, u32[]{:S(2)}, u32[]{:S(2)}) %all-to-all-start) | async-done | bytes 852000 | tf_op jit(solution)/shard_map/all_to_all | solution.py:498
  24.0 0.8 %shard_map.115 = (f32[256,128]{1,0:T(8,128)S(1)}, f32[6,256,128]{2,1,0:T(8,128)S(1)}, f32[256,128]{1,0:T(8,128)S(1)}, f32[256,128]{1,0:T(8,128)S(1)}, f32[64,128...) custom-call(f32[1664,128]{1,0:T(8,128)S(1)} %bitcast.4, ...), custom_call_target="tpu_custom_call" | custom-call | tf_op jit(solution)/shard_map/pallas_call | solution.py:448
  24.8 0.0 copy-start.2
  24.8 0.5 %collective-permute-start = (f32[64,128]{1,0:T(8,128)S(1)}, f32[64,128]{1,0:T(8,128)S(1)}, u32[]{:S(2)}, u32[]{:S(2)}) collective-permute-start(f32[64,128]{1,0:T(8,128)S(1)} %get-tuple-element.34), channel_id=1, source_target_pairs={{0,16},{1,17},{2,18},{3,19},{4,20},{5,21},{6,22},{7,23},{8,24},{9,... | collective-permute-start | bytes 98312 | tf_op jit(solution)/shard_map/ppermute | solution.py:467
  25.3 1.5 %collective-permute-start.1 = (f32[64,128]{1,0:T(8,128)S(1)}, f32[64,128]{1,0:T(8,128)S(1)}, u32[]{:S(2)}, u32[]{:S(2)}) collective-permute-start(f32[64,128]{1,0:T(8,128)S(1)} %get-tuple-element.35), channel_id=1, source_target_pairs={{0,1},{1,0},{2,3},{3,2},{4,5},{5,4},{6,7},{7,6},{8,9},{9,8},{10,11... | collective-permute-start | bytes 98312 | tf_op jit(solution)/shard_map/ppermute | solution.py:467
  26.8 2.2 %collective-permute-start.2 = (f32[64,128]{1,0:T(8,128)S(1)}, f32[64,128]{1,0:T(8,128)S(1)}, u32[]{:S(2)}, u32[]{:S(2)}) collective-permute-start(f32[64,128]{1,0:T(8,128)S(1)} %get-tuple-element.36), channel_id=1, source_target_pairs={{0,1},{1,0},{2,3},{3,2},{4,5},{5,4},{6,7},{7,6},{8,9},{9,8},{10,11... | collective-permute-start | bytes 98312 | tf_op jit(solution)/shard_map/ppermute | solution.py:467
  29.0 2.7 %collective-permute-start.3 = (f32[64,128]{1,0:T(8,128)S(1)}, f32[64,128]{1,0:T(8,128)S(1)}, u32[]{:S(2)}, u32[]{:S(2)}) collective-permute-start(f32[64,128]{1,0:T(8,128)S(1)} %get-tuple-element.37), channel_id=1, source_target_pairs={{0,16},{1,2},{2,1},{3,4},{4,3},{5,6},{6,5},{7,8},{8,7},{9,10},{10,... | collective-permute-start | bytes 98312 | tf_op jit(solution)/shard_map/ppermute | solution.py:467
  31.8 0.0 copy-done.2
  31.8 0.1 pad_add_fusion.refs_4_.table
  31.8 0.2 shard_map.116
  32.0 0.0 collective-permute-done.refs_0_
  32.0 0.0 collective-permute-done.1.refs_1_
  32.0 0.0 collective-permute-done.2.refs_2_
  32.0 1.5 %collective-permute-done.3.refs_3_ = f32[64,128]{1,0:T(8,128)S(1)} collective-permute-done((f32[64,128]{1,0:T(8,128)S(1)}, f32[64,128]{1,0:T(8,128)S(1)}, u32[]{:S(2)}, u32[]{:S(2)}) %collective-permute-start.3) | collective-permute-done | bytes 32800 | tf_op jit(solution)/shard_map/ppermute | solution.py:467
  33.6 0.9 %shard_map.117 = (f32[256,128]{1,0:T(8,128)S(1)}, f32[256,128]{1,0:T(8,128)S(1)}, f32[256,128]{1,0:T(8,128)S(1)}, f32[64,128]{1,0:T(8,128)S(1)}, f32[64,128]{1,0...) custom-call(f32[6,256,128]{2,1,0:T(8,128)S(1)} %get-tuple-element.28.state, ...), custom_call_target="tpu_custom_call" | custom-call | tf_op jit(solution)/shard_map/pallas_call | solution.py:448
  34.4 0.1 collective-permute-start.4
  34.5 1.4 %collective-permute-start.5 = (f32[64,128]{1,0:T(8,128)S(1)}, f32[64,128]{1,0:T(8,128)S(1)}, u32[]{:S(2)}, u32[]{:S(2)}) collective-permute-start(f32[64,128]{1,0:T(8,128)S(1)} %get-tuple-element.45), channel_id=1, source_target_pairs={{0,1},{1,0},{2,3},{3,2},{4,5},{5,4},{6,7},{7,6},{8,9},{9,8},{10,11... | collective-permute-start | bytes 98312 | tf_op jit(solution)/shard_map/ppermute | solution.py:467
  35.9 0.2 collective-permute-start.6
  36.1 3.0 %collective-permute-start.7 = (f32[64,128]{1,0:T(8,128)S(1)}, f32[64,128]{1,0:T(8,128)S(1)}, u32[]{:S(2)}, u32[]{:S(2)}) collective-permute-start(f32[64,128]{1,0:T(8,128)S(1)} %get-tuple-element.47), channel_id=1, source_target_pairs={{0,16},{1,2},{2,1},{3,4},{4,3},{5,6},{6,5},{7,8},{8,7},{9,10},{10,... | collective-permute-start | bytes 98312 | tf_op jit(solution)/shard_map/ppermute | solution.py:467
  39.2 0.9 %shard_map.118 = (f32[256,128]{1,0:T(8,128)S(1)}, f32[256,128]{1,0:T(8,128)S(1)}, f32[1,64,512]{2,1,0:T(8,128)}) custom-call(f32[256,128]{1,0:T(8,128)S(1)} %get-tuple-element.38.head_ref.head, f32[256,128]{1,0:T(8,128)S(1)} %get-tuple-element.39.cond_ref.cond), custom_call_target="tpu_custom_call" | custom-call | tf_op jit(solution)/shard_map/pallas_call | solution.py:448
  40.0 0.0 collective-permute-done.4.near_in
  40.0 0.0 collective-permute-done.5.far_in
  40.0 0.0 collective-permute-done.6.core
  40.0 0.7 %collective-permute-done.7.chip = f32[64,128]{1,0:T(8,128)S(1)} collective-permute-done((f32[64,128]{1,0:T(8,128)S(1)}, f32[64,128]{1,0:T(8,128)S(1)}, u32[]{:S(2)}, u32[]{:S(2)}) %collective-permute-start.7) | collective-permute-done | bytes 32800 | tf_op jit(solution)/shard_map/ppermute | solution.py:467
  40.8 1.3 %shard_map.119 = f32[1,64,512]{2,1,0:T(8,128)} custom-call(f32[256,128]{1,0:T(8,128)S(1)} %get-tuple-element.38.head_ref.head, f32[256,128]{1,0:T(8,128)S(1)} %get-tuple-element.39.cond_ref.cond, f32[256,128]{1,0:T(8,128)S(1)} %get-tuple-element.41.water, f32[256,128]{1,0:T(8,128)S(1)} %get-tuple-element.42.flux, f32[256,128]{1,0:T(8,128)S(1)} %get-tuple-element.43.total, ...), custom_call_target="tpu_custom_call" | custom-call | tf_op jit(solution)/shard_map/pallas_call | solution.py:448
Async XLA Ops:
  4.5 8.0 %copy-start = (f32[24,64,128]{2,1,0:T(8,128)S(1)}, f32[24,64,128]{2,1,0:T(8,128)}, u32[]{:S(2)}) copy-start(f32[24,64,128]{2,1,0:T(8,128)} %get-tuple-element.26.own) | copy-start | bytes 2359300
  4.5 8.0 %copy-start.1 = (f32[64,128]{1,0:T(8,128)S(1)}, f32[64,128]{1,0:T(8,128)}, u32[]{:S(2)}) copy-start(f32[64,128]{1,0:T(8,128)} %get-tuple-element.27.stay) | copy-start | bytes 98308
  4.6 19.4 %all-to-all-start = ((f32[16,104,128]{2,1,0:T(8,128)}), f32[16,104,128]{2,1,0:T(8,128)S(1)}, u32[]{:S(2)}, u32[]{:S(2)}) async-start(f32[16,104,128]{2,1,0:T(8,128)} %get-tuple-element.25), calls=%async_computation | async-start | bytes 1703936 | tf_op jit(solution)/shard_map/all_to_all | solution.py:498
  24.8 7.0 %copy-start.2 = (s32[64,4,4]{0,2,1:T(4,128)S(1)}, s32[64,4,4]{0,2,1:T(4,128)}, u32[]{:S(2)}) copy-start(s32[64,4,4]{0,2,1:T(4,128)} %param.19) | copy-start | bytes 12292
  24.8 7.2 %collective-permute-start = (f32[64,128]{1,0:T(8,128)S(1)}, f32[64,128]{1,0:T(8,128)S(1)}, u32[]{:S(2)}, u32[]{:S(2)}) collective-permute-start(f32[64,128]{1,0:T(8,128)S(1)} %get-tuple-element.34), channel_id=1, source_target_pairs={{0,16},{1,17},{2,18},{3,19},{4,20},{5,21},{6,22},{7,23},{8,24},{9,... | collective-permute-start | bytes 98312 | tf_op jit(solution)/shard_map/ppermute | solution.py:467
  25.3 6.7 %collective-permute-start.1 = (f32[64,128]{1,0:T(8,128)S(1)}, f32[64,128]{1,0:T(8,128)S(1)}, u32[]{:S(2)}, u32[]{:S(2)}) collective-permute-start(f32[64,128]{1,0:T(8,128)S(1)} %get-tuple-element.35), channel_id=1, source_target_pairs={{0,1},{1,0},{2,3},{3,2},{4,5},{5,4},{6,7},{7,6},{8,9},{9,8},{10,11... | collective-permute-start | bytes 98312 | tf_op jit(solution)/shard_map/ppermute | solution.py:467
  26.8 5.2 %collective-permute-start.2 = (f32[64,128]{1,0:T(8,128)S(1)}, f32[64,128]{1,0:T(8,128)S(1)}, u32[]{:S(2)}, u32[]{:S(2)}) collective-permute-start(f32[64,128]{1,0:T(8,128)S(1)} %get-tuple-element.36), channel_id=1, source_target_pairs={{0,1},{1,0},{2,3},{3,2},{4,5},{5,4},{6,7},{7,6},{8,9},{9,8},{10,11... | collective-permute-start | bytes 98312 | tf_op jit(solution)/shard_map/ppermute | solution.py:467
  29.0 4.6 %collective-permute-start.3 = (f32[64,128]{1,0:T(8,128)S(1)}, f32[64,128]{1,0:T(8,128)S(1)}, u32[]{:S(2)}, u32[]{:S(2)}) collective-permute-start(f32[64,128]{1,0:T(8,128)S(1)} %get-tuple-element.37), channel_id=1, source_target_pairs={{0,16},{1,2},{2,1},{3,4},{4,3},{5,6},{6,5},{7,8},{8,7},{9,10},{10,... | collective-permute-start | bytes 98312 | tf_op jit(solution)/shard_map/ppermute | solution.py:467
  34.4 5.6 %collective-permute-start.4 = (f32[64,128]{1,0:T(8,128)S(1)}, f32[64,128]{1,0:T(8,128)S(1)}, u32[]{:S(2)}, u32[]{:S(2)}) collective-permute-start(f32[64,128]{1,0:T(8,128)S(1)} %get-tuple-element.44), channel_id=1, source_target_pairs={{0,16},{1,17},{2,18},{3,19},{4,20},{5,21},{6,22},{7,23},{8,24},{9,... | collective-permute-start | bytes 98312 | tf_op jit(solution)/shard_map/ppermute | solution.py:467
  34.5 5.5 %collective-permute-start.5 = (f32[64,128]{1,0:T(8,128)S(1)}, f32[64,128]{1,0:T(8,128)S(1)}, u32[]{:S(2)}, u32[]{:S(2)}) collective-permute-start(f32[64,128]{1,0:T(8,128)S(1)} %get-tuple-element.45), channel_id=1, source_target_pairs={{0,1},{1,0},{2,3},{3,2},{4,5},{5,4},{6,7},{7,6},{8,9},{9,8},{10,11... | collective-permute-start | bytes 98312 | tf_op jit(solution)/shard_map/ppermute | solution.py:467
  35.9 4.1 %collective-permute-start.6 = (f32[64,128]{1,0:T(8,128)S(1)}, f32[64,128]{1,0:T(8,128)S(1)}, u32[]{:S(2)}, u32[]{:S(2)}) collective-permute-start(f32[64,128]{1,0:T(8,128)S(1)} %get-tuple-element.46), channel_id=1, source_target_pairs={{0,1},{1,0},{2,3},{3,2},{4,5},{5,4},{6,7},{7,6},{8,9},{9,8},{10,11... | collective-permute-start | bytes 98312 | tf_op jit(solution)/shard_map/ppermute | solution.py:467
  36.1 4.6 %collective-permute-start.7 = (f32[64,128]{1,0:T(8,128)S(1)}, f32[64,128]{1,0:T(8,128)S(1)}, u32[]{:S(2)}, u32[]{:S(2)}) collective-permute-start(f32[64,128]{1,0:T(8,128)S(1)} %get-tuple-element.47), channel_id=1, source_target_pairs={{0,16},{1,2},{2,1},{3,4},{4,3},{5,6},{6,5},{7,8},{8,7},{9,10},{10,... | collective-permute-start | bytes 98312 | tf_op jit(solution)/shard_map/ppermute | solution.py:467

commit v4 on v3

--- a/solution.py
+++ b/solution.py
@@ -61,27 +61,31 @@
 
 def pack_kernel(*refs):
     sources, targets, refs = refs[:9], refs[9:12], refs[12:]
-    held, (own, send, stay), refs = refs[:9], refs[9:12], refs[12:]
-    work_late, work_early, weights, flags, count, slot_early, sems_in, sems_out = refs
-    arriving = [pltpu.make_async_copy(source, ref, sems_in.at[n]) for n, (source, ref) in enumerate(zip(sources, held))]
+    held, refs = refs[:9], refs[9:]
+    own, part_late, part_early, part_place, places, stay, *refs = refs
+    work_late, work_early, weights, flags, free, taken, sems = refs
+    arriving = [pltpu.make_async_copy(source, ref, sems.at[0]) for source, ref in zip(sources, held)]
     for copy in arriving:
         copy.start()
     leaving = []
 
     def depart(source, target):
-        copy = pltpu.make_async_copy(source, target, sems_out.at[len(leaving)])
+        copy = pltpu.make_async_copy(source, target, sems.at[1])
         copy.start()
         leaving.append(copy)
 
     for bits in range(4):
         table = plane_weights(bits // 2, bits % 2)
-        for n in range(2):
+        for n in range(3):
             weights[128 * n : 128 * n + 128, 128 * bits : 128 * bits + 128] = table
     refine, destination = held[:2]
     me = lax.axis_index("dom")
     for peer in range(peers):
-        count[peer] = 0
-    arriving[0].wait()
+        free[peer] = jnp.where(peer == me, peers * room * late, seat(peer) * room * late)
+        part_place[peer] = jnp.full((8, 128), -1.0, f32)
+    places[...] = jnp.full((2 * blocks, 128), -1, jnp.int32)
+    for copy in arriving:
+        copy.wait()
     for block in range(blocks):
         flags[pl.ds(block, 1), :] = jnp.full((1, 128), refine[block], jnp.int32)
     lane = iota((blocks, 128), 1)
@@ -93,7 +97,6 @@
     up_x = bit_x == 1
 
     def get(n):
-        arriving[n].wait()
         return [held[n][0, :, 128 * c : 128 * c + 128] for c in range(4)]
 
     plain_y, plain_z = 4 * bit_y + (fine_y >> 1), 4 * bit_z + (fine_z >> 1)
@@ -132,8 +135,7 @@
         x = x - high.astype(f32)
         middle = x.astype(jnp.bfloat16)
         x = (x - middle.astype(f32)).astype(jnp.bfloat16)
-        y = jnp.dot(jnp.concatenate([high, middle], axis=1), weights[...], preferred_element_type=f32)
-        y = y + jnp.dot(x, weights[:128, :], preferred_element_type=f32)
+        y = jnp.dot(jnp.concatenate([high, middle, x], axis=1), weights[...], preferred_element_type=f32)
         result = []
         for c in range(4):
             parts = [y[blocks * c : blocks * (c + 1), 128 * n : 128 * n + 128] for n in range(4)]
@@ -148,42 +150,41 @@
                 work[pl.ds(8 * g * size + (f - first) * 4 + c, 8, stride=size), :] = values[c][8 * g : 8 * g + 8]
         depart(own.at[4 * f : 4 * f + 4], targets[0].at[4 * f : 4 * f + 4])
 
+    low = get(6)
+    keep(0, smooth(get(7)), work_early, early, 0)
+    keep(1, [x - y for x, y in zip(plain(low), smooth(get(8)))], work_early, early, 0)
     for n, f in ((2, 2), (3, 3), (4, 4)):
         keep(f, plain(get(n)), work_late, late, 2)
-    high, low = get(5), get(6)
+    high = get(5)
     keep(5, plain([x - y for x, y in zip(high, low)]), work_late, late, 2)
 
-    arriving[1].wait()
-    for peer in range(peers):
-        send[peer, rows * room :, :] = jnp.full((8, 128), -1.0, f32)
     for block in range(blocks):
         target = destination[block]
         owner = target >> 6
-        place = seat(owner)
-        used = count[owner] & (room - 1)
-        count[owner] = used + 1
-        spot = jnp.full((1, 128), target & 63, jnp.int32).astype(f32)
-        slot_early[block] = room * late + used * early
-        start = pl.ds(pl.multiple_of(used * late, 8), late)
-        send[place, start, :] = work_late[block * late : block * late + late, :]
-        send[place, pl.ds(room * rows + used, 1), :] = spot
-        stay[block : block + 1, :] = jnp.where(owner == me, spot, -1.0)
-    send[seat(me), rows * room :, :] = jnp.full((8, 128), -1.0, f32)
-    depart(send.at[:, : room * late], targets[1].at[:, : room * late])
+        row = free[owner]
+        free[owner] = row + late
+        taken[block] = row >> 1
+        place = jnp.full((1, 128), target, jnp.int32)
+        part_late[pl.ds(pl.multiple_of(row, late), late), :] = work_late[block * late : block * late + late, :]
+        places[pl.ds(row >> 4, 1), :] = place
+        stay[block : block + 1, :] = place.astype(f32)
+    for peer in range(peers):
+        part_place[peer, :room, :] = places[room * peer : room * peer + room, :].astype(f32)
+    depart(part_late.reshape(2 * peers, room * late, 128).at[:peers], targets[1].at[:, : room * late])
+    depart(part_place, targets[1].at[:, room * rows :])
     depart(stay, targets[2])
 
-    keep(0, smooth(get(7)), work_early, early, 0)
-    keep(1, [x - y for x, y in zip(plain(low), smooth(get(8)))], work_early, early, 0)
     for block in range(blocks):
-        start = pl.ds(pl.multiple_of(slot_early[block], 8), early)
-        send[seat(destination[block] >> 6), start, :] = work_early[block * early : block * early + early, :]
-    depart(send.at[:, room * late :], targets[1].at[:, room * late :])
+        row = pl.multiple_of(taken[block], early)
+        part_early[pl.ds(row, early), :] = work_early[block * early : block * early + early, :]
+    depart(part_early.reshape(2 * peers, room * early, 128).at[:peers], targets[1].at[:, room * late : room * rows])
     for copy in leaving:
         copy.wait()
 
 
 def find(places):
-    hit = places == (iota((blocks, 128), 1) & 63).astype(f32)
+    position = lax.axis_index("dom") * blocks + (iota((blocks, 128), 1) & 63)
+    hit = places.astype(jnp.int32) == position
     row = jnp.sum(jnp.where(hit, iota((blocks, 128), 0), 0), axis=0, keepdims=True)
     has = jnp.sum(jnp.where(hit, 1, 0), axis=0, keepdims=True) > 0
     return row + (iota((1, 128), 1) & 64), has
@@ -198,13 +199,13 @@
             out[f, 128 * c : 128 * c + 128, :] = lane_take(cells, index)
 
 
-def closure(head, less, alpha, shape_n, cond, span):
+def closure(head, alpha, shape_n, cond):
     expo = 1.0 - 1.0 / shape_n
     log_t = shape_n * jnp.log(alpha * jnp.maximum(-head, 0.0))
     log_s = jnp.log(1.0 + jnp.exp(log_t))
     root = jnp.exp(-0.5 * expo * log_s)
     inner = 1.0 - jnp.exp(expo * (log_t - log_s))
-    return cond * root * inner * inner, 4.0 * (less + span * root * root)
+    return cond * root * inner * inner, root * root
 
 
 def cube(x):
@@ -221,14 +222,16 @@
     ]
 
 
-def pack_faces(tiles_h, tiles_k, first):
+def pack_faces(tiles_h, tiles_k):
     group = iota((8, 8, 128), 2) >> 4
-    packed = None
+    right = left = None
     for f in range(4):
         for q, tiles in enumerate((tiles_h, tiles_k)):
-            part = turn(tiles[f], (2 * f + q) * reach - first)
-            packed = part if packed is None else jnp.where(group == 2 * f + q, part, packed)
-    return packed.reshape(64, 128)
+            g = 2 * f + q
+            part = turn(tiles[f], g * reach)
+            left = part if left is None else jnp.where(group == g, part, left)
+            right = part if right is None else jnp.where(group == (g + 3) % 8, part, right)
+    return right.reshape(64, 128), left.reshape(64, 128)
 
 
 def even(axis):
@@ -237,8 +240,7 @@
 
 def emit(head_ref, cond_ref, near, far, core, chip):
     tiles_h, tiles_k = face_tiles(cube(head_ref[...])), face_tiles(cube(cond_ref[...]))
-    right = pack_faces(tiles_h, tiles_k, blocks - reach)
-    left = pack_faces(tiles_h, tiles_k, 0)
+    right, left = pack_faces(tiles_h, tiles_k)
     near[...] = jnp.where(even("dom"), right, left)
     far[...] = jnp.where(even("dom"), left, right)
     for q, ref in enumerate((head_ref, cond_ref)):
@@ -247,14 +249,15 @@
         chip[32 * q : 32 * q + 32, :] = jnp.where(even("depth"), bottom, top)
 
 
-def arrive_kernel(recv, settled, head_out, state, cond_out, water_out, *outgoing):
+def receive(recv, settled, chosen):
     def slots(start):
         return [recv[pl.ds(start(o), peers, stride=chunk), :] for o in range(room)]
 
     places = jnp.concatenate(slots(lambda o: room * rows + o), axis=0)
     index, has = find(places)
     index = jnp.broadcast_to(index, (128, 128))
-    for f in range(fields):
+    for f in chosen:
+        halves = []
         for c in range(2):
             parts = []
             for r in (c, c + 2):
@@ -263,21 +266,29 @@
                 else:
                     parts += slots(lambda o: o * late + (f - 2) * 4 + r)
             cells = jnp.concatenate(parts, axis=0).T
-            span = slice(128 * c, 128 * c + 128)
-            state[f, span, :] = jnp.where(has, lane_take(cells, index), settled[f, span, :])
-    head_out[...] = state[0]
-    cond, water = closure(*[state[f] for f in range(fields)])
-    cond_out[...] = cond
-    water_out[...] = water
-    emit(state.at[0], cond_out, *outgoing)
+            halves.append(jnp.where(has, lane_take(cells, index), settled[f, 128 * c : 128 * c + 128, :]))
+        yield jnp.concatenate(halves, axis=0)
+
+
+def arrive_kernel(recv, settled, head_out, alpha_out, shape_out, sat_out, cond_out, wet_out, *outgoing):
+    outs = (head_out, alpha_out, shape_out, sat_out)
+    for ref, value in zip(outs, receive(recv, settled, (0, 2, 3, 4))):
+        ref[...] = value
+    cond_out[...], wet_out[...] = closure(*[ref[...] for ref in outs])
+    emit(head_out, cond_out, *outgoing)
+
+
+def later_kernel(recv, settled, wet, less_out, span_out, water_out):
+    for ref, value in zip((less_out, span_out), receive(recv, settled, (1, 5))):
+        ref[...] = value
+    water_out[...] = 4.0 * (less_out[...] + span_out[...] * wet[...])
 
 
 class Table:
     def __init__(self, near):
         position = near[...] - lax.axis_index("dom") * blocks
-        spot = jnp.where(position < 0, position + 80, jnp.where(position >= blocks, position + reach, position))
         present = near[...] >= 0
-        spot = jnp.where(present, spot, 0)
+        spot = jnp.where(present, position & 127, 0)
         lower = iota((8, 128), 1) < 64
         front = iota((8, 128), 0) < 4
 
@@ -327,7 +338,7 @@
     tiles = []
     for f, tile in enumerate(face_tiles(x)):
         g = 2 * f + q
-        after = jnp.where(lane < 80, turn(left, 64 - g * reach), turn(right, 80 - g * reach))
+        after = turn(jnp.where(lane >> 4 == g, right, left), (4 - g) * reach)
         tiles.append(jnp.where(lane < 64, tile, after))
     coarse = [quarters(tile) for tile in tiles]
     low = table.lower
@@ -349,7 +360,7 @@
     return jnp.stack(face_x), face_y[0], face_y[1]
 
 
-def inside_kernel(head_ref, cond_ref, flux_out, total_out, *head_out):
+def inside_kernel(head_ref, cond_ref, *outs):
     head, cond = cube(head_ref[...]), cube(cond_ref[...])
     lower = iota((8, 8, 128), 2) < 64
     level_k = iota((256, 128), 0) & 7
@@ -367,7 +378,7 @@
     rise = pair(cond_ref[...], up_k, head_ref[...], up_h + 1.0)
     rise = [jnp.where(level_k < 7, x, 0.0) for x in rise]
     along = pair(cond[:, :7], cond[:, 1:], head[:, :7], head[:, 1:])
-    for q, (out, sign) in enumerate(((flux_out, -1.0), (total_out, 1.0))):
+    for q, (out, sign) in enumerate(zip(outs, (-1.0, 1.0))):
         x = spread([step[q] for step in steps], [step[q] for step in steps], sign)
         x[3] = x[3] + cross[q]
         x[0] = x[0] + sign * turn(cross[q], 64)
@@ -375,11 +386,14 @@
         y = jnp.concatenate([along[q], empty], axis=1) + sign * jnp.concatenate([empty, along[q]], axis=1)
         z = rise[q] + sign * turn(rise[q], 1, 0)
         out[...] = (jnp.stack(x) + y).reshape(256, 128) + z
-    for ref in head_out:
-        leave(ref, head_ref[...])
-
-
-def balance(head_ref, cond_ref, flux_in, total_in, near_in, far_in, core, chip, near, planes):
+
+
+def last_inside_kernel(head_ref, cond_ref, flux_out, head_out):
+    inside_kernel(head_ref, cond_ref, flux_out)
+    leave(head_out, head_ref[...])
+
+
+def balance(head_ref, cond_ref, sums_in, near_in, far_in, core, chip, near, planes):
     table = Table(near)
     level = lax.axis_index("depth")
     head, cond = cube(head_ref[...]), cube(cond_ref[...])
@@ -401,11 +415,11 @@
     last = lax.axis_size("depth") - 1
     for n, (plane, k, on, lift) in enumerate(((below, 0, level > 0, -1.0), (above, 7, level < last, 1.0))):
         own_h, own_k = head_ref[pl.ds(k, 32, stride=8), :], cond_ref[pl.ds(k, 32, stride=8), :]
-        for q, value in enumerate(term(on, own_k, plane[32:], own_h, plane[:32] + lift)):
+        for q, value in enumerate(term(on, own_k, plane[32:], own_h, plane[:32] + lift)[: len(sums_in)]):
             planes[2 * n + q, pl.ds(k, 32, stride=8), :] = value
     level_k = iota((4, 8, 8, 128), 2)
     sums = []
-    for q, ref in enumerate((flux_in, total_in)):
+    for q, ref in enumerate(sums_in):
         z = jnp.where(level_k == 0, cube(planes[q]), jnp.where(level_k == 7, cube(planes[2 + q]), 0.0))
         total = cube(ref[...]) + z
         slabs = [total[0] + jnp.where(lower, x[q], 0.0), total[1], total[2], total[3] + jnp.where(lower, 0.0, x[q])]
@@ -415,15 +429,13 @@
     return sums
 
 
-def newton_kernel(state, cond, water, flux, total, *refs):
-    (near_in, far_in, core, chip, table), (head_out, cond_out, water_out, *outgoing), planes = refs[:5], refs[5:12], refs[12]
-    flux, total = balance(state.at[0], cond, flux, total, near_in, far_in, core, chip, table, planes)
+def newton_kernel(head, alpha, shape_n, sat, cond, span, water, flux, total, *refs):
+    incoming, (head_out, cond_out, wet_out, *outgoing), planes = refs[:5], refs[5:12], refs[12]
+    flux, total = balance(head, cond, (flux, total), *incoming, planes)
     resid = cube(water[...]) - flux
-    diagonal = 4.0 * cube(state[5]) * cube(state[2]) + total
-    head_out[...] = (cube(state[0]) - resid / diagonal).reshape(256, 128)
-    new_cond, new_water = closure(head_out[...], *[state[f] for f in range(1, fields)])
-    cond_out[...] = new_cond
-    water_out[...] = new_water
+    diagonal = 4.0 * cube(span[...]) * cube(alpha[...]) + total
+    head_out[...] = (cube(head[...]) - resid / diagonal).reshape(256, 128)
+    cond_out[...], wet_out[...] = closure(head_out[...], alpha[...], shape_n[...], sat[...])
     emit(head_out, cond_out, *outgoing)
 
 
@@ -434,9 +446,9 @@
         ref[0, :, 128 * c + 256 : 128 * c + 384] = turned[blocks:]
 
 
-def residual_kernel(head, cond, water, flux, total, near_in, far_in, core, chip, table, resid_out, planes):
-    flux, _ = balance(head, cond, flux, total, near_in, far_in, core, chip, table, planes)
-    leave(resid_out, water[...] - flux.reshape(256, 128))
+def residual_kernel(head, cond, wet, less, span, flux, near_in, far_in, core, chip, table, resid_out, planes):
+    (flux,) = balance(head, cond, (flux,), near_in, far_in, core, chip, table, planes)
+    leave(resid_out, 4.0 * (less[...] + span[...] * wet[...]) - flux.reshape(256, 128))
 
 
 def shape(*dims):
@@ -484,11 +496,13 @@
 def pack(head, water_prev, alpha, shape_n, theta_r, theta_s, sat_cond, refine, destination):
     outs = [shape(rows, blocks, 128), shape(peers, chunk, 128), shape(blocks, 128)]
     scratch = [pltpu.SMEM((blocks,), jnp.int32)] * 2 + [pltpu.VMEM((1, blocks, 512), f32)] * 7
-    scratch += [pltpu.VMEM(out.shape, f32) for out in outs]
+    scratch += [pltpu.VMEM((rows, blocks, 128), f32)]
+    scratch += [pltpu.VMEM((2 * blocks * size, 128), f32) for size in (late, early)]
+    scratch += [pltpu.VMEM((peers, 8, 128), f32), pltpu.VMEM((2 * blocks, 128), jnp.int32), pltpu.VMEM((blocks, 128), f32)]
     scratch += [pltpu.VMEM((blocks * late, 128), f32), pltpu.VMEM((blocks * early, 128), f32)]
-    scratch += [pltpu.VMEM((256, 512), jnp.bfloat16)]
+    scratch += [pltpu.VMEM((384, 512), jnp.bfloat16)]
     scratch += [pltpu.VMEM((blocks, 128), jnp.int32), pltpu.SMEM((peers,), jnp.int32), pltpu.SMEM((blocks,), jnp.int32)]
-    scratch += [pltpu.SemaphoreType.DMA((9,))] * 2
+    scratch += [pltpu.SemaphoreType.DMA((2,))]
     operands = (refine, destination, alpha, shape_n, sat_cond, theta_s, theta_r, head, water_prev)
     return call(pack_kernel, outs, scratch, *operands, space=pltpu.HBM, limit=64 * 1024 * 1024)
 
@@ -500,22 +514,19 @@
     near = neighbours.reshape(blocks, 16).T
     near = jnp.concatenate([near, near], axis=1)
     cells, halo = shape(256, 128), [shape(64, 128)] * 4
-    head, state, cond, water, *outgoing = call(
-        arrive_kernel,
-        [cells, shape(fields, 256, 128), cells, cells] + halo,
-        [],
-        recv.reshape(peers * chunk, 128), settled,
-    )
+    recv = recv.reshape(peers * chunk, 128)
+    head, alpha, shape_n, sat, cond, wet, *outgoing = call(arrive_kernel, [cells] * 6 + halo, [], recv, settled)
     incoming = exchange(*outgoing)
     sums = call(inside_kernel, [cells, cells], [], head, cond)
+    less, span, water = call(later_kernel, [cells] * 3, [], recv, settled, wet)
     planes = [pltpu.VMEM((4, 256, 128), f32)]
-    head, cond, water, *outgoing = call(
-        newton_kernel, [cells] * 3 + halo, planes, state, cond, water, *sums, *incoming, near
+    head, cond, wet, *outgoing = call(
+        newton_kernel, [cells] * 3 + halo, planes, head, alpha, shape_n, sat, cond, span, water, *sums, *incoming, near
     )
     incoming = exchange(*outgoing)
     final = shape(1, blocks, 512)
-    *sums, new_head = call(inside_kernel, [cells, cells, final], [], head, cond)
-    (residual,) = call(residual_kernel, [final], planes, head, cond, water, *sums, *incoming, near)
+    flux, new_head = call(last_inside_kernel, [cells, final], [], head, cond)
+    (residual,) = call(residual_kernel, [final], planes, head, cond, wet, less, span, flux, *incoming, near)
     return new_head, residual
 
 

time: 42.2 us -> 41.1 us (0.974)
  Pallas kernels: 8.41 us -> 7.5 us
    pallas_call x7 -> x8, Pallas kernels: 8.41 us -> 7.5 us  [call(): pl.pallas_call(kernel, out_shape=outs, in_specs=[whole] * len(operands),...]
where the time goes in v4:
time: 41.1 us; the launch traced here: 40.8 us
  starting transfers between devices  19.6 us (48%)
  waiting for transfers between devices  12.9 us (31%)
  Pallas kernels  7.5 us (18%)
  between operations  0.75 us (2%)
    ppermute x8, starting transfers between devices, swap(): return lax.ppermute(x, ('dom', 'depth'), pairs)  11.6 us
    all_to_all x1, waiting for transfers between devices, on_device(): lax.all_to_all(send, 'dom', 0, 0, tiled=True, axis_index_groups=[sorted(r...  10.9 us
    all_to_all x1, starting transfers between devices, on_device(): lax.all_to_all(send, 'dom', 0, 0, tiled=True, axis_index_groups=[sorted(r...  7.94 us
    pallas_call x8, Pallas kernels, call(): pl.pallas_call(kernel, out_shape=outs, in_specs=[whole] * len(operands),...  7.5 us
    ppermute x8, waiting for transfers between devices, swap(): return lax.ppermute(x, ('dom', 'depth'), pairs)  2 us
  transfers between devices with their start and end apart: 9, of which 3 were waited for; matrix products, arithmetic and copies ran while one was open for 0% of the time, Pallas kernels for 4%

profile of v4, /device:TPU:99, one launch (start us, length us, event | category | flops | bytes accessed | tf_op | source)
XLA Modules:
  0.0 40.8 jit_solution(6171288955502801009)
XLA Ops:
  0.6 3.0 %shard_map.113 = (f32[24,64,128]{2,1,0:T(8,128)}, f32[16,104,128]{2,1,0:T(8,128)}, f32[64,128]{1,0:T(8,128)}) custom-call(s32[64]{0:T(128)} %refs_0_.1, s32[64]{0:T(128)} %refs_1_.1, f32[1,64,512]{2,1,0:T(8,128)} %refs_2_.1, f32[1,64,512]{2,1,0:T(8,128)} %refs_3_.1, f32[1,64,512]{2,1,0:T(8,128)} %refs_4_.1, f32[1,64,512]{2,1,0:T(8,128)} %refs_5_.1, ...), custom_call_target="tpu_custom_call" | custom-call | tf_op jit(solution)/shard_map/pallas_call | solution.py:460
  3.7 0.0 copy-start
  3.7 0.0 copy-start.1
  3.7 7.9 %all-to-all-start = ((f32[16,104,128]{2,1,0:T(8,128)}), f32[16,104,128]{2,1,0:T(8,128)S(1)}, u32[]{:S(2)}, u32[]{:S(2)}) async-start(f32[16,104,128]{2,1,0:T(8,128)} %get-tuple-element.29), calls=%async_computation | async-start | bytes 1703936 | tf_op jit(solution)/shard_map/all_to_all | solution.py:512
  11.6 0.0 copy-done
  11.6 0.0 copy-done.1
  11.6 0.5 %shard_map.114.settled = f32[6,256,128]{2,1,0:T(8,128)S(1)} custom-call(f32[24,64,128]{2,1,0:T(8,128)S(1)} %copy-done, f32[64,128]{1,0:T(8,128)S(1)} %copy-done.1), custom_call_target="tpu_custom_call" | custom-call | tf_op jit(solution)/shard_map/pallas_call | solution.py:460
  12.2 10.9 %all-to-all-done = f32[16,104,128]{2,1,0:T(8,128)S(1)} async-done(((f32[16,104,128]{2,1,0:T(8,128)}), f32[16,104,128]{2,1,0:T(8,128)S(1)}, u32[]{:S(2)}, u32[]{:S(2)}) %all-to-all-start) | async-done | bytes 852000 | tf_op jit(solution)/shard_map/all_to_all | solution.py:512
  23.1 0.7 %shard_map.115 = (f32[256,128]{1,0:T(8,128)S(1)}, f32[256,128]{1,0:T(8,128)S(1)}, f32[256,128]{1,0:T(8,128)S(1)}, f32[256,128]{1,0:T(8,128)S(1)}, f32[256,128]{1...) custom-call(f32[1664,128]{1,0:T(8,128)S(1)} %bitcast.4, ...), custom_call_target="tpu_custom_call" | custom-call | tf_op jit(solution)/shard_map/pallas_call | solution.py:460
  23.8 0.0 copy-start.2
  23.8 0.5 %collective-permute-start = (f32[64,128]{1,0:T(8,128)S(1)}, f32[64,128]{1,0:T(8,128)S(1)}, u32[]{:S(2)}, u32[]{:S(2)}) collective-permute-start(f32[64,128]{1,0:T(8,128)S(1)} %get-tuple-element.42), channel_id=1, source_target_pairs={{0,16},{1,17},{2,18},{3,19},{4,20},{5,21},{6,22},{7,23},{8,24},{9,... | collective-permute-start | bytes 98312 | tf_op jit(solution)/shard_map/ppermute | solution.py:479
  24.3 1.5 %collective-permute-start.1 = (f32[64,128]{1,0:T(8,128)S(1)}, f32[64,128]{1,0:T(8,128)S(1)}, u32[]{:S(2)}, u32[]{:S(2)}) collective-permute-start(f32[64,128]{1,0:T(8,128)S(1)} %get-tuple-element.43), channel_id=1, source_target_pairs={{0,1},{1,0},{2,3},{3,2},{4,5},{5,4},{6,7},{7,6},{8,9},{9,8},{10,11... | collective-permute-start | bytes 98312 | tf_op jit(solution)/shard_map/ppermute | solution.py:479
  25.8 2.2 %collective-permute-start.2 = (f32[64,128]{1,0:T(8,128)S(1)}, f32[64,128]{1,0:T(8,128)S(1)}, u32[]{:S(2)}, u32[]{:S(2)}) collective-permute-start(f32[64,128]{1,0:T(8,128)S(1)} %get-tuple-element.44), channel_id=1, source_target_pairs={{0,1},{1,0},{2,3},{3,2},{4,5},{5,4},{6,7},{7,6},{8,9},{9,8},{10,11... | collective-permute-start | bytes 98312 | tf_op jit(solution)/shard_map/ppermute | solution.py:479
  28.0 2.7 %collective-permute-start.3 = (f32[64,128]{1,0:T(8,128)S(1)}, f32[64,128]{1,0:T(8,128)S(1)}, u32[]{:S(2)}, u32[]{:S(2)}) collective-permute-start(f32[64,128]{1,0:T(8,128)S(1)} %get-tuple-element.45), channel_id=1, source_target_pairs={{0,16},{1,2},{2,1},{3,4},{4,3},{5,6},{6,5},{7,8},{8,7},{9,10},{10,... | collective-permute-start | bytes 98312 | tf_op jit(solution)/shard_map/ppermute | solution.py:479
  30.7 0.0 copy-done.2
  30.7 0.1 pad_add_fusion.refs_4_.table
  30.8 0.3 shard_map.116
  31.1 0.2 shard_map.117
  31.3 0.0 collective-permute-done.refs_0_
  31.3 0.0 collective-permute-done.1.refs_1_
  31.3 0.0 collective-permute-done.2.refs_2_
  31.3 1.3 %collective-permute-done.3.refs_3_ = f32[64,128]{1,0:T(8,128)S(1)} collective-permute-done((f32[64,128]{1,0:T(8,128)S(1)}, f32[64,128]{1,0:T(8,128)S(1)}, u32[]{:S(2)}, u32[]{:S(2)}) %collective-permute-start.3) | collective-permute-done | bytes 32800 | tf_op jit(solution)/shard_map/ppermute | solution.py:479
  32.6 0.8 %shard_map.118 = (f32[256,128]{1,0:T(8,128)S(1)}, f32[256,128]{1,0:T(8,128)S(1)}, f32[256,128]{1,0:T(8,128)S(1)}, f32[64,128]{1,0:T(8,128)S(1)}, f32[64,128]{1,0...) custom-call(f32[256,128]{1,0:T(8,128)S(1)} %get-tuple-element.32.head_ref.head, ...), custom_call_target="tpu_custom_call" | custom-call | tf_op jit(solution)/shard_map/pallas_call | solution.py:460
  33.3 0.1 collective-permute-start.4
  33.4 1.4 %collective-permute-start.5 = (f32[64,128]{1,0:T(8,128)S(1)}, f32[64,128]{1,0:T(8,128)S(1)}, u32[]{:S(2)}, u32[]{:S(2)}) collective-permute-start(f32[64,128]{1,0:T(8,128)S(1)} %get-tuple-element.53), channel_id=1, source_target_pairs={{0,1},{1,0},{2,3},{3,2},{4,5},{5,4},{6,7},{7,6},{8,9},{9,8},{10,11... | collective-permute-start | bytes 98312 | tf_op jit(solution)/shard_map/ppermute | solution.py:479
  34.8 0.2 collective-permute-start.6
  35.0 3.0 %collective-permute-start.7 = (f32[64,128]{1,0:T(8,128)S(1)}, f32[64,128]{1,0:T(8,128)S(1)}, u32[]{:S(2)}, u32[]{:S(2)}) collective-permute-start(f32[64,128]{1,0:T(8,128)S(1)} %get-tuple-element.55), channel_id=1, source_target_pairs={{0,16},{1,2},{2,1},{3,4},{4,3},{5,6},{6,5},{7,8},{8,7},{9,10},{10,... | collective-permute-start | bytes 98312 | tf_op jit(solution)/shard_map/ppermute | solution.py:479
  38.0 0.9 %shard_map.119 = (f32[256,128]{1,0:T(8,128)S(1)}, f32[1,64,512]{2,1,0:T(8,128)}) custom-call(f32[256,128]{1,0:T(8,128)S(1)} %get-tuple-element.46.head_ref.head, f32[256,128]{1,0:T(8,128)S(1)} %get-tuple-element.47.cond_ref.cond), custom_call_target="tpu_custom_call" | custom-call | tf_op jit(solution)/shard_map/pallas_call | solution.py:460
  38.9 0.0 collective-permute-done.4.near_in
  38.9 0.0 collective-permute-done.5.far_in
  38.9 0.0 collective-permute-done.6.core
  38.9 0.7 %collective-permute-done.7.chip = f32[64,128]{1,0:T(8,128)S(1)} collective-permute-done((f32[64,128]{1,0:T(8,128)S(1)}, f32[64,128]{1,0:T(8,128)S(1)}, u32[]{:S(2)}, u32[]{:S(2)}) %collective-permute-start.7) | collective-permute-done | bytes 32800 | tf_op jit(solution)/shard_map/ppermute | solution.py:479
  39.6 1.2 %shard_map.120 = f32[1,64,512]{2,1,0:T(8,128)} custom-call(f32[256,128]{1,0:T(8,128)S(1)} %get-tuple-element.46.head_ref.head, f32[256,128]{1,0:T(8,128)S(1)} %get-tuple-element.47.cond_ref.cond, f32[256,128]{1,0:T(8,128)S(1)} %get-tuple-element.49.wet, f32[256,128]{1,0:T(8,128)S(1)} %get-tuple-element.50.less, f32[256,128]{1,0:T(8,128)S(1)} %get-tuple-element.38.span, ...), custom_call_target="tpu_custom_call" | custom-call | tf_op jit(solution)/shard_map/pallas_call | solution.py:460
Async XLA Ops:
  3.7 8.0 %copy-start = (f32[24,64,128]{2,1,0:T(8,128)S(1)}, f32[24,64,128]{2,1,0:T(8,128)}, u32[]{:S(2)}) copy-start(f32[24,64,128]{2,1,0:T(8,128)} %get-tuple-element.30.own) | copy-start | bytes 2359300
  3.7 8.0 %copy-start.1 = (f32[64,128]{1,0:T(8,128)S(1)}, f32[64,128]{1,0:T(8,128)}, u32[]{:S(2)}) copy-start(f32[64,128]{1,0:T(8,128)} %get-tuple-element.31.stay) | copy-start | bytes 98308
  3.7 19.4 %all-to-all-start = ((f32[16,104,128]{2,1,0:T(8,128)}), f32[16,104,128]{2,1,0:T(8,128)S(1)}, u32[]{:S(2)}, u32[]{:S(2)}) async-start(f32[16,104,128]{2,1,0:T(8,128)} %get-tuple-element.29), calls=%async_computation | async-start | bytes 1703936 | tf_op jit(solution)/shard_map/all_to_all | solution.py:512
  23.8 7.0 %copy-start.2 = (s32[64,4,4]{0,2,1:T(4,128)S(1)}, s32[64,4,4]{0,2,1:T(4,128)}, u32[]{:S(2)}) copy-start(s32[64,4,4]{0,2,1:T(4,128)} %param.19) | copy-start | bytes 12292
  23.8 7.5 %collective-permute-start = (f32[64,128]{1,0:T(8,128)S(1)}, f32[64,128]{1,0:T(8,128)S(1)}, u32[]{:S(2)}, u32[]{:S(2)}) collective-permute-start(f32[64,128]{1,0:T(8,128)S(1)} %get-tuple-element.42), channel_id=1, source_target_pairs={{0,16},{1,17},{2,18},{3,19},{4,20},{5,21},{6,22},{7,23},{8,24},{9,... | collective-permute-start | bytes 98312 | tf_op jit(solution)/shard_map/ppermute | solution.py:479
  24.3 7.0 %collective-permute-start.1 = (f32[64,128]{1,0:T(8,128)S(1)}, f32[64,128]{1,0:T(8,128)S(1)}, u32[]{:S(2)}, u32[]{:S(2)}) collective-permute-start(f32[64,128]{1,0:T(8,128)S(1)} %get-tuple-element.43), channel_id=1, source_target_pairs={{0,1},{1,0},{2,3},{3,2},{4,5},{5,4},{6,7},{7,6},{8,9},{9,8},{10,11... | collective-permute-start | bytes 98312 | tf_op jit(solution)/shard_map/ppermute | solution.py:479
  25.8 5.5 %collective-permute-start.2 = (f32[64,128]{1,0:T(8,128)S(1)}, f32[64,128]{1,0:T(8,128)S(1)}, u32[]{:S(2)}, u32[]{:S(2)}) collective-permute-start(f32[64,128]{1,0:T(8,128)S(1)} %get-tuple-element.44), channel_id=1, source_target_pairs={{0,1},{1,0},{2,3},{3,2},{4,5},{5,4},{6,7},{7,6},{8,9},{9,8},{10,11... | collective-permute-start | bytes 98312 | tf_op jit(solution)/shard_map/ppermute | solution.py:479
  28.0 4.6 %collective-permute-start.3 = (f32[64,128]{1,0:T(8,128)S(1)}, f32[64,128]{1,0:T(8,128)S(1)}, u32[]{:S(2)}, u32[]{:S(2)}) collective-permute-start(f32[64,128]{1,0:T(8,128)S(1)} %get-tuple-element.45), channel_id=1, source_target_pairs={{0,16},{1,2},{2,1},{3,4},{4,3},{5,6},{6,5},{7,8},{8,7},{9,10},{10,... | collective-permute-start | bytes 98312 | tf_op jit(solution)/shard_map/ppermute | solution.py:479
  33.3 5.6 %collective-permute-start.4 = (f32[64,128]{1,0:T(8,128)S(1)}, f32[64,128]{1,0:T(8,128)S(1)}, u32[]{:S(2)}, u32[]{:S(2)}) collective-permute-start(f32[64,128]{1,0:T(8,128)S(1)} %get-tuple-element.52), channel_id=1, source_target_pairs={{0,16},{1,17},{2,18},{3,19},{4,20},{5,21},{6,22},{7,23},{8,24},{9,... | collective-permute-start | bytes 98312 | tf_op jit(solution)/shard_map/ppermute | solution.py:479
  33.4 5.5 %collective-permute-start.5 = (f32[64,128]{1,0:T(8,128)S(1)}, f32[64,128]{1,0:T(8,128)S(1)}, u32[]{:S(2)}, u32[]{:S(2)}) collective-permute-start(f32[64,128]{1,0:T(8,128)S(1)} %get-tuple-element.53), channel_id=1, source_target_pairs={{0,1},{1,0},{2,3},{3,2},{4,5},{5,4},{6,7},{7,6},{8,9},{9,8},{10,11... | collective-permute-start | bytes 98312 | tf_op jit(solution)/shard_map/ppermute | solution.py:479
  34.8 4.1 %collective-permute-start.6 = (f32[64,128]{1,0:T(8,128)S(1)}, f32[64,128]{1,0:T(8,128)S(1)}, u32[]{:S(2)}, u32[]{:S(2)}) collective-permute-start(f32[64,128]{1,0:T(8,128)S(1)} %get-tuple-element.54), channel_id=1, source_target_pairs={{0,1},{1,0},{2,3},{3,2},{4,5},{5,4},{6,7},{7,6},{8,9},{9,8},{10,11... | collective-permute-start | bytes 98312 | tf_op jit(solution)/shard_map/ppermute | solution.py:479
  35.0 4.6 %collective-permute-start.7 = (f32[64,128]{1,0:T(8,128)S(1)}, f32[64,128]{1,0:T(8,128)S(1)}, u32[]{:S(2)}, u32[]{:S(2)}) collective-permute-start(f32[64,128]{1,0:T(8,128)S(1)} %get-tuple-element.55), channel_id=1, source_target_pairs={{0,16},{1,2},{2,1},{3,4},{4,3},{5,6},{6,5},{7,8},{8,7},{9,10},{10,... | collective-permute-start | bytes 98312 | tf_op jit(solution)/shard_map/ppermute | solution.py:479

commit v5 on v4

--- a/solution.py
+++ b/solution.py
@@ -285,20 +285,13 @@
 
 
 class Table:
-    def __init__(self, near):
-        position = near[...] - lax.axis_index("dom") * blocks
-        present = near[...] >= 0
-        spot = jnp.where(present, position & 127, 0)
+    def __init__(self, values):
         lower = iota((8, 128), 1) < 64
         front = iota((8, 128), 0) < 4
 
         def row(f, e):
-            return jnp.broadcast_to(spot[4 * f + e : 4 * f + e + 1], (8, 128))
-
-        def on(f, e):
-            return jnp.broadcast_to(present[4 * f + e : 4 * f + e + 1].astype(jnp.int32), (8, 128)) == 1
-
-        self.lower = lower
+            return jnp.broadcast_to(values[4 * f + e : 4 * f + e + 1], (8, 128))
+
         self.one_x = jnp.where(lower, row(0, 0), row(1, 0))
         self.four_x = [
             jnp.where(
@@ -308,8 +301,6 @@
             )
             for s in range(2)
         ]
-        self.hang_x = (lower & on(0, 3)) | (~lower & on(1, 3))
-        self.on_x = (lower & on(0, 0)) | (~lower & on(1, 0))
         self.one_y = [row(f, 0) for f in (2, 3)]
         self.four_y = [
             jnp.where(
@@ -319,8 +310,33 @@
             )
             for f in (2, 3)
         ]
-        self.hang_y = [on(f, 3) for f in (2, 3)]
-        self.on_y = [on(f, 0) for f in (2, 3)]
+        self.last_x = jnp.where(lower, row(0, 3), row(1, 3))
+        self.last_y = [row(f, 3) for f in (2, 3)]
+
+
+class Faces:
+    def __init__(self, near):
+        position = near[...] - lax.axis_index("dom") * blocks
+        self.position, self.present = position, near[...] >= 0
+        self.own = (position >= 0) & (position < blocks)
+        there = Table(self.present.astype(jnp.int32))
+        self.on_x, self.hang_x = there.one_x == 1, there.last_x == 1
+        self.on_y, self.hang_y = [x == 1 for x in there.one_y], [x == 1 for x in there.last_y]
+
+    def own_lanes(self):
+        return Table(jnp.where(self.present & self.own, self.position, 0))
+
+    def halo_lanes(self, q):
+        group = ((iota((16, 128), 0) >> 2) ^ 1) * 2 + q
+        right = group * reach + self.position - blocks
+        left = ((group + 3) & 7) * reach + self.position + reach
+        return Table(jnp.where(self.present & ~self.own, jnp.where(self.position < 0, left, right), 0))
+
+    def away(self):
+        table = Table((self.present & ~self.own).astype(jnp.int32))
+        x = [jnp.where(self.hang_x, four, table.one_x) == 1 for four in table.four_x]
+        y = [jnp.where(self.hang_y[n], table.four_y[n], table.one_y[n]) == 1 for n in range(2)]
+        return x, y
 
 
 def quarters(tile):
@@ -333,34 +349,51 @@
     return result
 
 
-def ghosts(x, left, right, q, table):
-    lane = iota((8, 8, 128), 2)
-    tiles = []
-    for f, tile in enumerate(face_tiles(x)):
-        g = 2 * f + q
-        after = turn(jnp.where(lane >> 4 == g, right, left), (4 - g) * reach)
-        tiles.append(jnp.where(lane < 64, tile, after))
-    coarse = [quarters(tile) for tile in tiles]
-    low = table.lower
-    face_x = []
+def ghosts(faces, table, tiles, coarse):
+    low = iota((8, 128), 1) < 64
+    alike = len(tiles) == 1
+    made = []
+
+    def both(lists, n, index):
+        if alike:
+            return lane_take(lists[0][n], index)
+        return jnp.where(low, lane_take(lists[1][n], index), lane_take(lists[0][n], index))
+
     for a in range(8):
-        one = jnp.where(low, lane_take(tiles[1][a], table.one_x), lane_take(tiles[0][a], table.one_x))
-        index = table.four_x[a // 4]
-        four = jnp.where(low, lane_take(coarse[1][a % 4], index), lane_take(coarse[0][a % 4], index))
-        face_x.append(jnp.where(table.hang_x, four, one))
-    face_y = []
-    for side, source in ((0, 3), (1, 2)):
-        made = []
+        one = both(tiles, a, table.one_x)
+        four = both(coarse, a % 4, table.four_x[a // 4])
+        made.append(jnp.where(faces.hang_x, four, one))
+    for side, source in ((0, 0 if alike else 3), (1, 0 if alike else 2)):
         for a in range(4):
             index = table.one_y[side]
             one = jnp.where(low, lane_take(tiles[source][a], index), lane_take(tiles[source][a + 4], index))
             four = lane_take(coarse[source][a], table.four_y[side])
-            made.append(jnp.where(table.hang_y[side], four, one))
-        face_y.append(jnp.stack(made))
-    return jnp.stack(face_x), face_y[0], face_y[1]
-
-
-def inside_kernel(head_ref, cond_ref, *outs):
+            made.append(jnp.where(faces.hang_y[side], four, one))
+    return made
+
+
+def own_ghosts(refs, near, out):
+    faces = Faces(near)
+    table = faces.own_lanes()
+    for q, ref in enumerate(refs):
+        tiles = face_tiles(cube(ref[...]))
+        for n, value in enumerate(ghosts(faces, table, tiles, [quarters(tile) for tile in tiles])):
+            out[q, 8 * n : 8 * n + 8, :] = value
+
+
+def all_ghosts(faces, left, right, own):
+    group = iota((8, 8, 128), 2) >> 4
+    away_x, away_y = faces.away()
+    for q in range(2):
+        tile = jnp.where(group % 2 == q, right, left)
+        made = ghosts(faces, faces.halo_lanes(q), [tile], [quarters(tile)])
+        away = [away_x[0]] * 4 + [away_x[1]] * 4 + [away_y[0]] * 4 + [away_y[1]] * 4
+        made = [jnp.where(far, x, own[q, 8 * n : 8 * n + 8, :]) for n, (far, x) in enumerate(zip(away, made))]
+        yield jnp.stack(made[:8]), jnp.stack(made[8:12]), jnp.stack(made[12:])
+
+
+def inside_kernel(head_ref, cond_ref, near, own, *outs):
+    own_ghosts((head_ref, cond_ref), near, own)
     head, cond = cube(head_ref[...]), cube(cond_ref[...])
     lower = iota((8, 8, 128), 2) < 64
     level_k = iota((256, 128), 0) & 7
@@ -388,19 +421,18 @@
         out[...] = (jnp.stack(x) + y).reshape(256, 128) + z
 
 
-def last_inside_kernel(head_ref, cond_ref, flux_out, head_out):
-    inside_kernel(head_ref, cond_ref, flux_out)
+def last_inside_kernel(head_ref, cond_ref, near, own, flux_out, head_out):
+    inside_kernel(head_ref, cond_ref, near, own, flux_out)
     leave(head_out, head_ref[...])
 
 
-def balance(head_ref, cond_ref, sums_in, near_in, far_in, core, chip, near, planes):
-    table = Table(near)
+def balance(head_ref, cond_ref, own, sums_in, near_in, far_in, core, chip, near, planes):
+    table = Faces(near)
     level = lax.axis_index("depth")
     head, cond = cube(head_ref[...]), cube(cond_ref[...])
     left = jnp.where(even("dom"), far_in[...], near_in[...]).reshape(8, 8, 128)
     right = jnp.where(even("dom"), near_in[...], far_in[...]).reshape(8, 8, 128)
-    around_h, *sides_h = ghosts(head, left, right, 0, table)
-    around_k, *sides_k = ghosts(cond, left, right, 1, table)
+    (around_h, *sides_h), (around_k, *sides_k) = all_ghosts(table, left, right, own)
     lower = iota((8, 8, 128), 2) < 64
 
     def term(on, k, other_k, h, other_h):
@@ -429,9 +461,9 @@
     return sums
 
 
-def newton_kernel(head, alpha, shape_n, sat, cond, span, water, flux, total, *refs):
+def newton_kernel(head, alpha, shape_n, sat, cond, span, water, own, flux, total, *refs):
     incoming, (head_out, cond_out, wet_out, *outgoing), planes = refs[:5], refs[5:12], refs[12]
-    flux, total = balance(head, cond, (flux, total), *incoming, planes)
+    flux, total = balance(head, cond, own, (flux, total), *incoming, planes)
     resid = cube(water[...]) - flux
     diagonal = 4.0 * cube(span[...]) * cube(alpha[...]) + total
     head_out[...] = (cube(head[...]) - resid / diagonal).reshape(256, 128)
@@ -446,8 +478,8 @@
         ref[0, :, 128 * c + 256 : 128 * c + 384] = turned[blocks:]
 
 
-def residual_kernel(head, cond, wet, less, span, flux, near_in, far_in, core, chip, table, resid_out, planes):
-    (flux,) = balance(head, cond, (flux,), near_in, far_in, core, chip, table, planes)
+def residual_kernel(head, cond, wet, less, span, own, flux, near_in, far_in, core, chip, table, resid_out, planes):
+    (flux,) = balance(head, cond, own, (flux,), near_in, far_in, core, chip, table, planes)
     leave(resid_out, 4.0 * (less[...] + span[...] * wet[...]) - flux.reshape(256, 128))
 
 
@@ -508,16 +540,17 @@
 
 
 def on_device(head, water_prev, alpha, shape_n, theta_r, theta_s, sat_cond, refine, destination, neighbours):
-    own, send, stay = pack(head, water_prev, alpha, shape_n, theta_r, theta_s, sat_cond, refine, destination)
+    held, send, stay = pack(head, water_prev, alpha, shape_n, theta_r, theta_s, sat_cond, refine, destination)
     recv = lax.all_to_all(send, "dom", 0, 0, tiled=True, axis_index_groups=[sorted(range(peers), key=seat)])
-    (settled,) = call(settle_kernel, [shape(fields, 256, 128)], [], own, stay)
+    (settled,) = call(settle_kernel, [shape(fields, 256, 128)], [], held, stay)
     near = neighbours.reshape(blocks, 16).T
     near = jnp.concatenate([near, near], axis=1)
     cells, halo = shape(256, 128), [shape(64, 128)] * 4
     recv = recv.reshape(peers * chunk, 128)
     head, alpha, shape_n, sat, cond, wet, *outgoing = call(arrive_kernel, [cells] * 6 + halo, [], recv, settled)
     incoming = exchange(*outgoing)
-    sums = call(inside_kernel, [cells, cells], [], head, cond)
+    ghost = shape(2, 128, 128)
+    sums = call(inside_kernel, [ghost, cells, cells], [], head, cond, near)
     less, span, water = call(later_kernel, [cells] * 3, [], recv, settled, wet)
     planes = [pltpu.VMEM((4, 256, 128), f32)]
     head, cond, wet, *outgoing = call(
@@ -525,8 +558,8 @@
     )
     incoming = exchange(*outgoing)
     final = shape(1, blocks, 512)
-    flux, new_head = call(last_inside_kernel, [cells, final], [], head, cond)
-    (residual,) = call(residual_kernel, [final], planes, head, cond, wet, less, span, flux, *incoming, near)
+    own, flux, new_head = call(last_inside_kernel, [ghost, cells, final], [], head, cond, near)
+    (residual,) = call(residual_kernel, [final], planes, head, cond, wet, less, span, own, flux, *incoming, near)
     return new_head, residual
 
 

time: 41.1 us -> 40.6 us (0.988)
  waiting for transfers between devices: 12.9 us -> 12.3 us
    ppermute x8, waiting for transfers between devices: 2 us -> 1.38 us  [swap(): return lax.ppermute(x, ('dom', 'depth'), pairs)]
  transfers between devices with their start and end apart: 9 -> 9, of which waited for: 3 -> 3; matrix products, arithmetic and copies ran while one was open for 0% -> 0% of each run, Pallas kernels for 4% -> 6%
where the time goes in v5:
time: 40.6 us; the launch traced here: 40.4 us
  starting transfers between devices  19.6 us (48%)
  waiting for transfers between devices  12.3 us (30%)
  Pallas kernels  7.67 us (19%)
  between operations  0.75 us (2%)
    ppermute x8, starting transfers between devices, swap(): return lax.ppermute(x, ('dom', 'depth'), pairs)  11.6 us
    all_to_all x1, waiting for transfers between devices, on_device(): lax.all_to_all(send, 'dom', 0, 0, tiled=True, axis_index_groups=[sorted(r...  10.9 us
    all_to_all x1, starting transfers between devices, on_device(): lax.all_to_all(send, 'dom', 0, 0, tiled=True, axis_index_groups=[sorted(r...  7.94 us
    pallas_call x8, Pallas kernels, call(): pl.pallas_call(kernel, out_shape=outs, in_specs=[whole] * len(operands),...  7.67 us
    ppermute x8, waiting for transfers between devices, swap(): return lax.ppermute(x, ('dom', 'depth'), pairs)  1.38 us
  transfers between devices with their start and end apart: 9, of which 3 were waited for; matrix products, arithmetic and copies ran while one was open for 0% of the time, Pallas kernels for 6%

profile of v5, /device:TPU:99, one launch (start us, length us, event | category | flops | bytes accessed | tf_op | source)
XLA Modules:
  0.0 40.4 jit_solution(8569260476697191188)
XLA Ops:
  0.6 3.0 %shard_map.113 = (f32[24,64,128]{2,1,0:T(8,128)}, f32[16,104,128]{2,1,0:T(8,128)}, f32[64,128]{1,0:T(8,128)}) custom-call(s32[64]{0:T(128)} %refs_0_.1, s32[64]{0:T(128)} %refs_1_.1, f32[1,64,512]{2,1,0:T(8,128)} %refs_2_.1, f32[1,64,512]{2,1,0:T(8,128)} %refs_3_.1, f32[1,64,512]{2,1,0:T(8,128)} %refs_4_.1, f32[1,64,512]{2,1,0:T(8,128)} %refs_5_.1, ...), custom_call_target="tpu_custom_call" | custom-call | tf_op jit(solution)/shard_map/pallas_call | solution.py:492
  3.7 0.0 copy-start
  3.7 0.0 copy-start.1
  3.7 7.9 %all-to-all-start = ((f32[16,104,128]{2,1,0:T(8,128)}), f32[16,104,128]{2,1,0:T(8,128)S(1)}, u32[]{:S(2)}, u32[]{:S(2)}) async-start(f32[16,104,128]{2,1,0:T(8,128)} %get-tuple-element.31), calls=%async_computation | async-start | bytes 1703936 | tf_op jit(solution)/shard_map/all_to_all | solution.py:544
  11.6 0.0 copy-done
  11.6 0.0 copy-done.1
  11.6 0.5 %shard_map.114.settled = f32[6,256,128]{2,1,0:T(8,128)S(1)} custom-call(f32[24,64,128]{2,1,0:T(8,128)S(1)} %copy-done, f32[64,128]{1,0:T(8,128)S(1)} %copy-done.1), custom_call_target="tpu_custom_call" | custom-call | tf_op jit(solution)/shard_map/pallas_call | solution.py:492
  12.2 10.9 %all-to-all-done = f32[16,104,128]{2,1,0:T(8,128)S(1)} async-done(((f32[16,104,128]{2,1,0:T(8,128)}), f32[16,104,128]{2,1,0:T(8,128)S(1)}, u32[]{:S(2)}, u32[]{:S(2)}) %all-to-all-start) | async-done | bytes 852000 | tf_op jit(solution)/shard_map/all_to_all | solution.py:544
  23.1 0.7 %shard_map.115 = (f32[256,128]{1,0:T(8,128)S(1)}, f32[256,128]{1,0:T(8,128)S(1)}, f32[256,128]{1,0:T(8,128)S(1)}, f32[256,128]{1,0:T(8,128)S(1)}, f32[256,128]{1...) custom-call(f32[1664,128]{1,0:T(8,128)S(1)} %bitcast.4, ...), custom_call_target="tpu_custom_call" | custom-call | tf_op jit(solution)/shard_map/pallas_call | solution.py:492
  23.8 0.0 copy-start.2
  23.8 0.5 %collective-permute-start = (f32[64,128]{1,0:T(8,128)S(1)}, f32[64,128]{1,0:T(8,128)S(1)}, u32[]{:S(2)}, u32[]{:S(2)}) collective-permute-start(f32[64,128]{1,0:T(8,128)S(1)} %get-tuple-element.45), channel_id=1, source_target_pairs={{0,16},{1,17},{2,18},{3,19},{4,20},{5,21},{6,22},{7,23},{8,24},{9,... | collective-permute-start | bytes 98312 | tf_op jit(solution)/shard_map/ppermute | solution.py:511
  24.3 1.5 %collective-permute-start.1 = (f32[64,128]{1,0:T(8,128)S(1)}, f32[64,128]{1,0:T(8,128)S(1)}, u32[]{:S(2)}, u32[]{:S(2)}) collective-permute-start(f32[64,128]{1,0:T(8,128)S(1)} %get-tuple-element.46), channel_id=1, source_target_pairs={{0,1},{1,0},{2,3},{3,2},{4,5},{5,4},{6,7},{7,6},{8,9},{9,8},{10,11... | collective-permute-start | bytes 98312 | tf_op jit(solution)/shard_map/ppermute | solution.py:511
  25.8 2.2 %collective-permute-start.2 = (f32[64,128]{1,0:T(8,128)S(1)}, f32[64,128]{1,0:T(8,128)S(1)}, u32[]{:S(2)}, u32[]{:S(2)}) collective-permute-start(f32[64,128]{1,0:T(8,128)S(1)} %get-tuple-element.47), channel_id=1, source_target_pairs={{0,1},{1,0},{2,3},{3,2},{4,5},{5,4},{6,7},{7,6},{8,9},{9,8},{10,11... | collective-permute-start | bytes 98312 | tf_op jit(solution)/shard_map/ppermute | solution.py:511
  28.0 2.7 %collective-permute-start.3 = (f32[64,128]{1,0:T(8,128)S(1)}, f32[64,128]{1,0:T(8,128)S(1)}, u32[]{:S(2)}, u32[]{:S(2)}) collective-permute-start(f32[64,128]{1,0:T(8,128)S(1)} %get-tuple-element.48), channel_id=1, source_target_pairs={{0,16},{1,2},{2,1},{3,4},{4,3},{5,6},{6,5},{7,8},{8,7},{9,10},{10,... | collective-permute-start | bytes 98312 | tf_op jit(solution)/shard_map/ppermute | solution.py:511
  30.7 0.0 copy-done.2
  30.7 0.1 pad_add_fusion.near.refs_4_.table
  30.8 0.3 shard_map.116
  31.1 0.5 %shard_map.117 = (f32[2,128,128]{2,1,0:T(8,128)S(1)}, f32[256,128]{1,0:T(8,128)S(1)}, f32[256,128]{1,0:T(8,128)S(1)}) custom-call(f32[256,128]{1,0:T(8,128)S(1)} %get-tuple-element.34.head_ref.head, f32[256,128]{1,0:T(8,128)S(1)} %get-tuple-element.38.cond_ref.cond, s32[16,128]{1,0:T(8,128)S(1)} %pad_add_fusion.near.refs_4_.table), custom_call_target="tpu_custom_call" | custom-call | tf_op jit(solution)/shard_map/pallas_call | solution.py:492
  31.6 0.0 collective-permute-done.refs_0_
  31.6 0.0 collective-permute-done.1.refs_1_
  31.6 0.0 collective-permute-done.2.refs_2_
  31.6 1.0 %collective-permute-done.3.refs_3_ = f32[64,128]{1,0:T(8,128)S(1)} collective-permute-done((f32[64,128]{1,0:T(8,128)S(1)}, f32[64,128]{1,0:T(8,128)S(1)}, u32[]{:S(2)}, u32[]{:S(2)}) %collective-permute-start.3) | collective-permute-done | bytes 32800 | tf_op jit(solution)/shard_map/ppermute | solution.py:511
  32.6 0.5 %shard_map.118 = (f32[256,128]{1,0:T(8,128)S(1)}, f32[256,128]{1,0:T(8,128)S(1)}, f32[256,128]{1,0:T(8,128)S(1)}, f32[64,128]{1,0:T(8,128)S(1)}, f32[64,128]{1,0...) custom-call(f32[256,128]{1,0:T(8,128)S(1)} %get-tuple-element.34.head_ref.head, ...), custom_call_target="tpu_custom_call" | custom-call | tf_op jit(solution)/shard_map/pallas_call | solution.py:492
  33.1 0.1 collective-permute-start.4
  33.2 1.4 %collective-permute-start.5 = (f32[64,128]{1,0:T(8,128)S(1)}, f32[64,128]{1,0:T(8,128)S(1)}, u32[]{:S(2)}, u32[]{:S(2)}) collective-permute-start(f32[64,128]{1,0:T(8,128)S(1)} %get-tuple-element.57), channel_id=1, source_target_pairs={{0,1},{1,0},{2,3},{3,2},{4,5},{5,4},{6,7},{7,6},{8,9},{9,8},{10,11... | collective-permute-start | bytes 98312 | tf_op jit(solution)/shard_map/ppermute | solution.py:511
  34.6 0.2 collective-permute-start.6
  34.8 3.0 %collective-permute-start.7 = (f32[64,128]{1,0:T(8,128)S(1)}, f32[64,128]{1,0:T(8,128)S(1)}, u32[]{:S(2)}, u32[]{:S(2)}) collective-permute-start(f32[64,128]{1,0:T(8,128)S(1)} %get-tuple-element.59), channel_id=1, source_target_pairs={{0,16},{1,2},{2,1},{3,4},{4,3},{5,6},{6,5},{7,8},{8,7},{9,10},{10,... | collective-permute-start | bytes 98312 | tf_op jit(solution)/shard_map/ppermute | solution.py:511
  37.8 1.2 %shard_map.119 = (f32[2,128,128]{2,1,0:T(8,128)S(1)}, f32[256,128]{1,0:T(8,128)S(1)}, f32[1,64,512]{2,1,0:T(8,128)}) custom-call(f32[256,128]{1,0:T(8,128)S(1)} %get-tuple-element.49.head_ref.head, f32[256,128]{1,0:T(8,128)S(1)} %get-tuple-element.50.cond_ref.cond, s32[16,128]{1,0:T(8,128)S(1)} %pad_add_fusion.near.refs_4_.table), custom_call_target="tpu_custom_call" | custom-call | tf_op jit(solution)/shard_map/pallas_call | solution.py:492
  39.0 0.0 collective-permute-done.4.near_in
  39.0 0.0 collective-permute-done.5.far_in
  39.0 0.0 collective-permute-done.6.core
  39.0 0.4 collective-permute-done.7.chip
  39.4 1.0 %shard_map.120 = f32[1,64,512]{2,1,0:T(8,128)} custom-call(f32[256,128]{1,0:T(8,128)S(1)} %get-tuple-element.49.head_ref.head, f32[256,128]{1,0:T(8,128)S(1)} %get-tuple-element.50.cond_ref.cond, f32[256,128]{1,0:T(8,128)S(1)} %get-tuple-element.52.wet, f32[256,128]{1,0:T(8,128)S(1)} %get-tuple-element.53.less, f32[256,128]{1,0:T(8,128)S(1)} %get-tuple-element.40.span, ...), custom_call_target="tpu_custom_call" | custom-call | tf_op jit(solution)/shard_map/pallas_call | solution.py:492
Async XLA Ops:
  3.7 8.0 %copy-start = (f32[24,64,128]{2,1,0:T(8,128)S(1)}, f32[24,64,128]{2,1,0:T(8,128)}, u32[]{:S(2)}) copy-start(f32[24,64,128]{2,1,0:T(8,128)} %get-tuple-element.32.own) | copy-start | bytes 2359300
  3.7 8.0 %copy-start.1 = (f32[64,128]{1,0:T(8,128)S(1)}, f32[64,128]{1,0:T(8,128)}, u32[]{:S(2)}) copy-start(f32[64,128]{1,0:T(8,128)} %get-tuple-element.33.stay) | copy-start | bytes 98308
  3.7 19.4 %all-to-all-start = ((f32[16,104,128]{2,1,0:T(8,128)}), f32[16,104,128]{2,1,0:T(8,128)S(1)}, u32[]{:S(2)}, u32[]{:S(2)}) async-start(f32[16,104,128]{2,1,0:T(8,128)} %get-tuple-element.31), calls=%async_computation | async-start | bytes 1703936 | tf_op jit(solution)/shard_map/all_to_all | solution.py:544
  23.8 7.0 %copy-start.2 = (s32[64,4,4]{0,2,1:T(4,128)S(1)}, s32[64,4,4]{0,2,1:T(4,128)}, u32[]{:S(2)}) copy-start(s32[64,4,4]{0,2,1:T(4,128)} %param.19) | copy-start | bytes 12292
  23.8 7.8 %collective-permute-start = (f32[64,128]{1,0:T(8,128)S(1)}, f32[64,128]{1,0:T(8,128)S(1)}, u32[]{:S(2)}, u32[]{:S(2)}) collective-permute-start(f32[64,128]{1,0:T(8,128)S(1)} %get-tuple-element.45), channel_id=1, source_target_pairs={{0,16},{1,17},{2,18},{3,19},{4,20},{5,21},{6,22},{7,23},{8,24},{9,... | collective-permute-start | bytes 98312 | tf_op jit(solution)/shard_map/ppermute | solution.py:511
  24.3 7.3 %collective-permute-start.1 = (f32[64,128]{1,0:T(8,128)S(1)}, f32[64,128]{1,0:T(8,128)S(1)}, u32[]{:S(2)}, u32[]{:S(2)}) collective-permute-start(f32[64,128]{1,0:T(8,128)S(1)} %get-tuple-element.46), channel_id=1, source_target_pairs={{0,1},{1,0},{2,3},{3,2},{4,5},{5,4},{6,7},{7,6},{8,9},{9,8},{10,11... | collective-permute-start | bytes 98312 | tf_op jit(solution)/shard_map/ppermute | solution.py:511
  25.8 5.8 %collective-permute-start.2 = (f32[64,128]{1,0:T(8,128)S(1)}, f32[64,128]{1,0:T(8,128)S(1)}, u32[]{:S(2)}, u32[]{:S(2)}) collective-permute-start(f32[64,128]{1,0:T(8,128)S(1)} %get-tuple-element.47), channel_id=1, source_target_pairs={{0,1},{1,0},{2,3},{3,2},{4,5},{5,4},{6,7},{7,6},{8,9},{9,8},{10,11... | collective-permute-start | bytes 98312 | tf_op jit(solution)/shard_map/ppermute | solution.py:511
  28.0 4.6 %collective-permute-start.3 = (f32[64,128]{1,0:T(8,128)S(1)}, f32[64,128]{1,0:T(8,128)S(1)}, u32[]{:S(2)}, u32[]{:S(2)}) collective-permute-start(f32[64,128]{1,0:T(8,128)S(1)} %get-tuple-element.48), channel_id=1, source_target_pairs={{0,16},{1,2},{2,1},{3,4},{4,3},{5,6},{6,5},{7,8},{8,7},{9,10},{10,... | collective-permute-start | bytes 98312 | tf_op jit(solution)/shard_map/ppermute | solution.py:511
  33.1 5.9 %collective-permute-start.4 = (f32[64,128]{1,0:T(8,128)S(1)}, f32[64,128]{1,0:T(8,128)S(1)}, u32[]{:S(2)}, u32[]{:S(2)}) collective-permute-start(f32[64,128]{1,0:T(8,128)S(1)} %get-tuple-element.56), channel_id=1, source_target_pairs={{0,16},{1,17},{2,18},{3,19},{4,20},{5,21},{6,22},{7,23},{8,24},{9,... | collective-permute-start | bytes 98312 | tf_op jit(solution)/shard_map/ppermute | solution.py:511
  33.2 5.8 %collective-permute-start.5 = (f32[64,128]{1,0:T(8,128)S(1)}, f32[64,128]{1,0:T(8,128)S(1)}, u32[]{:S(2)}, u32[]{:S(2)}) collective-permute-start(f32[64,128]{1,0:T(8,128)S(1)} %get-tuple-element.57), channel_id=1, source_target_pairs={{0,1},{1,0},{2,3},{3,2},{4,5},{5,4},{6,7},{7,6},{8,9},{9,8},{10,11... | collective-permute-start | bytes 98312 | tf_op jit(solution)/shard_map/ppermute | solution.py:511
  34.6 4.4 %collective-permute-start.6 = (f32[64,128]{1,0:T(8,128)S(1)}, f32[64,128]{1,0:T(8,128)S(1)}, u32[]{:S(2)}, u32[]{:S(2)}) collective-permute-start(f32[64,128]{1,0:T(8,128)S(1)} %get-tuple-element.58), channel_id=1, source_target_pairs={{0,1},{1,0},{2,3},{3,2},{4,5},{5,4},{6,7},{7,6},{8,9},{9,8},{10,11... | collective-permute-start | bytes 98312 | tf_op jit(solution)/shard_map/ppermute | solution.py:511
  34.8 4.6 %collective-permute-start.7 = (f32[64,128]{1,0:T(8,128)S(1)}, f32[64,128]{1,0:T(8,128)S(1)}, u32[]{:S(2)}, u32[]{:S(2)}) collective-permute-start(f32[64,128]{1,0:T(8,128)S(1)} %get-tuple-element.59), channel_id=1, source_target_pairs={{0,16},{1,2},{2,1},{3,4},{4,3},{5,6},{6,5},{7,8},{8,7},{9,10},{10,... | collective-permute-start | bytes 98312 | tf_op jit(solution)/shard_map/ppermute | solution.py:511

commit v6 on v5

--- a/solution.py
+++ b/solution.py
@@ -222,13 +222,17 @@
     ]
 
 
-def pack_faces(tiles_h, tiles_k):
+def pack_faces(head, cond):
     group = iota((8, 8, 128), 2) >> 4
     right = left = None
     for f in range(4):
-        for q, tiles in enumerate((tiles_h, tiles_k)):
+        for q, x in enumerate((head, cond)):
             g = 2 * f + q
-            part = turn(tiles[f], g * reach)
+            if f < 2:
+                part = turn(x[3 * f], 64 * f + g * reach)
+            else:
+                edge = x[:, 7 * (f - 2)]
+                part = jnp.concatenate([turn(edge, g * reach), turn(edge, 64 + g * reach)], axis=0)
             left = part if left is None else jnp.where(group == g, part, left)
             right = part if right is None else jnp.where(group == (g + 3) % 8, part, right)
     return right.reshape(64, 128), left.reshape(64, 128)
@@ -239,8 +243,7 @@
 
 
 def emit(head_ref, cond_ref, near, far, core, chip):
-    tiles_h, tiles_k = face_tiles(cube(head_ref[...])), face_tiles(cube(cond_ref[...]))
-    right, left = pack_faces(tiles_h, tiles_k)
+    right, left = pack_faces(cube(head_ref[...]), cube(cond_ref[...]))
     near[...] = jnp.where(even("dom"), right, left)
     far[...] = jnp.where(even("dom"), left, right)
     for q, ref in enumerate((head_ref, cond_ref)):

time: 40.6 us -> 40.5 us (level)
  no operation moved by 1% of the time
where the time goes in v6:
time: 40.5 us; the launch traced here: 40.3 us
  starting transfers between devices  19.6 us (48%)
  waiting for transfers between devices  12.3 us (30%)
  Pallas kernels  7.54 us (19%)
  between operations  0.75 us (2%)
    ppermute x8, starting transfers between devices, swap(): return lax.ppermute(x, ('dom', 'depth'), pairs)  11.6 us
    all_to_all x1, waiting for transfers between devices, on_device(): lax.all_to_all(send, 'dom', 0, 0, tiled=True, axis_index_groups=[sorted(r...  10.9 us
    all_to_all x1, starting transfers between devices, on_device(): lax.all_to_all(send, 'dom', 0, 0, tiled=True, axis_index_groups=[sorted(r...  7.94 us
    pallas_call x8, Pallas kernels, call(): pl.pallas_call(kernel, out_shape=outs, in_specs=[whole] * len(operands),...  7.54 us
    ppermute x8, waiting for transfers between devices, swap(): return lax.ppermute(x, ('dom', 'depth'), pairs)  1.38 us
  transfers between devices with their start and end apart: 9, of which 3 were waited for; matrix products, arithmetic and copies ran while one was open for 0% of the time, Pallas kernels for 6%

profile of v6, /device:TPU:99, one launch (start us, length us, event | category | flops | bytes accessed | tf_op | source)
XLA Modules:
  0.0 40.3 jit_solution(6606012228955035171)
XLA Ops:
  0.6 3.0 %shard_map.113 = (f32[24,64,128]{2,1,0:T(8,128)}, f32[16,104,128]{2,1,0:T(8,128)}, f32[64,128]{1,0:T(8,128)}) custom-call(s32[64]{0:T(128)} %refs_0_.1, s32[64]{0:T(128)} %refs_1_.1, f32[1,64,512]{2,1,0:T(8,128)} %refs_2_.1, f32[1,64,512]{2,1,0:T(8,128)} %refs_3_.1, f32[1,64,512]{2,1,0:T(8,128)} %refs_4_.1, f32[1,64,512]{2,1,0:T(8,128)} %refs_5_.1, ...), custom_call_target="tpu_custom_call" | custom-call | tf_op jit(solution)/shard_map/pallas_call | solution.py:495
  3.7 0.0 copy-start
  3.7 0.0 copy-start.1
  3.7 7.9 %all-to-all-start = ((f32[16,104,128]{2,1,0:T(8,128)}), f32[16,104,128]{2,1,0:T(8,128)S(1)}, u32[]{:S(2)}, u32[]{:S(2)}) async-start(f32[16,104,128]{2,1,0:T(8,128)} %get-tuple-element.31), calls=%async_computation | async-start | bytes 1703936 | tf_op jit(solution)/shard_map/all_to_all | solution.py:547
  11.6 0.0 copy-done
  11.6 0.0 copy-done.1
  11.6 0.5 %shard_map.114.settled = f32[6,256,128]{2,1,0:T(8,128)S(1)} custom-call(f32[24,64,128]{2,1,0:T(8,128)S(1)} %copy-done, f32[64,128]{1,0:T(8,128)S(1)} %copy-done.1), custom_call_target="tpu_custom_call" | custom-call | tf_op jit(solution)/shard_map/pallas_call | solution.py:495
  12.2 10.9 %all-to-all-done = f32[16,104,128]{2,1,0:T(8,128)S(1)} async-done(((f32[16,104,128]{2,1,0:T(8,128)}), f32[16,104,128]{2,1,0:T(8,128)S(1)}, u32[]{:S(2)}, u32[]{:S(2)}) %all-to-all-start) | async-done | bytes 852000 | tf_op jit(solution)/shard_map/all_to_all | solution.py:547
  23.1 0.6 %shard_map.115 = (f32[256,128]{1,0:T(8,128)S(1)}, f32[256,128]{1,0:T(8,128)S(1)}, f32[256,128]{1,0:T(8,128)S(1)}, f32[256,128]{1,0:T(8,128)S(1)}, f32[256,128]{1...) custom-call(f32[1664,128]{1,0:T(8,128)S(1)} %bitcast.4, ...), custom_call_target="tpu_custom_call" | custom-call | tf_op jit(solution)/shard_map/pallas_call | solution.py:495
  23.7 0.0 copy-start.2
  23.7 0.5 %collective-permute-start = (f32[64,128]{1,0:T(8,128)S(1)}, f32[64,128]{1,0:T(8,128)S(1)}, u32[]{:S(2)}, u32[]{:S(2)}) collective-permute-start(f32[64,128]{1,0:T(8,128)S(1)} %get-tuple-element.45), channel_id=1, source_target_pairs={{0,16},{1,17},{2,18},{3,19},{4,20},{5,21},{6,22},{7,23},{8,24},{9,... | collective-permute-start | bytes 98312 | tf_op jit(solution)/shard_map/ppermute | solution.py:514
  24.2 1.5 %collective-permute-start.1 = (f32[64,128]{1,0:T(8,128)S(1)}, f32[64,128]{1,0:T(8,128)S(1)}, u32[]{:S(2)}, u32[]{:S(2)}) collective-permute-start(f32[64,128]{1,0:T(8,128)S(1)} %get-tuple-element.46), channel_id=1, source_target_pairs={{0,1},{1,0},{2,3},{3,2},{4,5},{5,4},{6,7},{7,6},{8,9},{9,8},{10,11... | collective-permute-start | bytes 98312 | tf_op jit(solution)/shard_map/ppermute | solution.py:514
  25.7 2.2 %collective-permute-start.2 = (f32[64,128]{1,0:T(8,128)S(1)}, f32[64,128]{1,0:T(8,128)S(1)}, u32[]{:S(2)}, u32[]{:S(2)}) collective-permute-start(f32[64,128]{1,0:T(8,128)S(1)} %get-tuple-element.47), channel_id=1, source_target_pairs={{0,1},{1,0},{2,3},{3,2},{4,5},{5,4},{6,7},{7,6},{8,9},{9,8},{10,11... | collective-permute-start | bytes 98312 | tf_op jit(solution)/shard_map/ppermute | solution.py:514
  27.9 2.7 %collective-permute-start.3 = (f32[64,128]{1,0:T(8,128)S(1)}, f32[64,128]{1,0:T(8,128)S(1)}, u32[]{:S(2)}, u32[]{:S(2)}) collective-permute-start(f32[64,128]{1,0:T(8,128)S(1)} %get-tuple-element.48), channel_id=1, source_target_pairs={{0,16},{1,2},{2,1},{3,4},{4,3},{5,6},{6,5},{7,8},{8,7},{9,10},{10,... | collective-permute-start | bytes 98312 | tf_op jit(solution)/shard_map/ppermute | solution.py:514
  30.7 0.0 copy-done.2
  30.7 0.1 pad_add_fusion.near.refs_4_.table
  30.7 0.3 shard_map.116
  31.0 0.5 %shard_map.117 = (f32[2,128,128]{2,1,0:T(8,128)S(1)}, f32[256,128]{1,0:T(8,128)S(1)}, f32[256,128]{1,0:T(8,128)S(1)}) custom-call(f32[256,128]{1,0:T(8,128)S(1)} %get-tuple-element.34.head_ref.head, f32[256,128]{1,0:T(8,128)S(1)} %get-tuple-element.38.cond_ref.cond, s32[16,128]{1,0:T(8,128)S(1)} %pad_add_fusion.near.refs_4_.table), custom_call_target="tpu_custom_call" | custom-call | tf_op jit(solution)/shard_map/pallas_call | solution.py:495
  31.5 0.0 collective-permute-done.refs_0_
  31.5 0.0 collective-permute-done.1.refs_1_
  31.5 0.0 collective-permute-done.2.refs_2_
  31.5 1.0 %collective-permute-done.3.refs_3_ = f32[64,128]{1,0:T(8,128)S(1)} collective-permute-done((f32[64,128]{1,0:T(8,128)S(1)}, f32[64,128]{1,0:T(8,128)S(1)}, u32[]{:S(2)}, u32[]{:S(2)}) %collective-permute-start.3) | collective-permute-done | bytes 32800 | tf_op jit(solution)/shard_map/ppermute | solution.py:514
  32.5 0.5 %shard_map.118 = (f32[256,128]{1,0:T(8,128)S(1)}, f32[256,128]{1,0:T(8,128)S(1)}, f32[256,128]{1,0:T(8,128)S(1)}, f32[64,128]{1,0:T(8,128)S(1)}, f32[64,128]{1,0...) custom-call(f32[256,128]{1,0:T(8,128)S(1)} %get-tuple-element.34.head_ref.head, ...), custom_call_target="tpu_custom_call" | custom-call | tf_op jit(solution)/shard_map/pallas_call | solution.py:495
  33.0 0.1 collective-permute-start.4
  33.1 1.4 %collective-permute-start.5 = (f32[64,128]{1,0:T(8,128)S(1)}, f32[64,128]{1,0:T(8,128)S(1)}, u32[]{:S(2)}, u32[]{:S(2)}) collective-permute-start(f32[64,128]{1,0:T(8,128)S(1)} %get-tuple-element.57), channel_id=1, source_target_pairs={{0,1},{1,0},{2,3},{3,2},{4,5},{5,4},{6,7},{7,6},{8,9},{9,8},{10,11... | collective-permute-start | bytes 98312 | tf_op jit(solution)/shard_map/ppermute | solution.py:514
  34.5 0.2 collective-permute-start.6
  34.6 3.0 %collective-permute-start.7 = (f32[64,128]{1,0:T(8,128)S(1)}, f32[64,128]{1,0:T(8,128)S(1)}, u32[]{:S(2)}, u32[]{:S(2)}) collective-permute-start(f32[64,128]{1,0:T(8,128)S(1)} %get-tuple-element.59), channel_id=1, source_target_pairs={{0,16},{1,2},{2,1},{3,4},{4,3},{5,6},{6,5},{7,8},{8,7},{9,10},{10,... | collective-permute-start | bytes 98312 | tf_op jit(solution)/shard_map/ppermute | solution.py:514
  37.7 1.2 %shard_map.119 = (f32[2,128,128]{2,1,0:T(8,128)S(1)}, f32[256,128]{1,0:T(8,128)S(1)}, f32[1,64,512]{2,1,0:T(8,128)}) custom-call(f32[256,128]{1,0:T(8,128)S(1)} %get-tuple-element.49.head_ref.head, f32[256,128]{1,0:T(8,128)S(1)} %get-tuple-element.50.cond_ref.cond, s32[16,128]{1,0:T(8,128)S(1)} %pad_add_fusion.near.refs_4_.table), custom_call_target="tpu_custom_call" | custom-call | tf_op jit(solution)/shard_map/pallas_call | solution.py:495
  38.9 0.0 collective-permute-done.4.near_in
  38.9 0.0 collective-permute-done.5.far_in
  38.9 0.0 collective-permute-done.6.core
  38.9 0.4 collective-permute-done.7.chip
  39.3 1.0 %shard_map.120 = f32[1,64,512]{2,1,0:T(8,128)} custom-call(f32[256,128]{1,0:T(8,128)S(1)} %get-tuple-element.49.head_ref.head, f32[256,128]{1,0:T(8,128)S(1)} %get-tuple-element.50.cond_ref.cond, f32[256,128]{1,0:T(8,128)S(1)} %get-tuple-element.52.wet, f32[256,128]{1,0:T(8,128)S(1)} %get-tuple-element.53.less, f32[256,128]{1,0:T(8,128)S(1)} %get-tuple-element.40.span, ...), custom_call_target="tpu_custom_call" | custom-call | tf_op jit(solution)/shard_map/pallas_call | solution.py:495
Async XLA Ops:
  3.7 8.0 %copy-start = (f32[24,64,128]{2,1,0:T(8,128)S(1)}, f32[24,64,128]{2,1,0:T(8,128)}, u32[]{:S(2)}) copy-start(f32[24,64,128]{2,1,0:T(8,128)} %get-tuple-element.32.own) | copy-start | bytes 2359300
  3.7 8.0 %copy-start.1 = (f32[64,128]{1,0:T(8,128)S(1)}, f32[64,128]{1,0:T(8,128)}, u32[]{:S(2)}) copy-start(f32[64,128]{1,0:T(8,128)} %get-tuple-element.33.stay) | copy-start | bytes 98308
  3.7 19.4 %all-to-all-start = ((f32[16,104,128]{2,1,0:T(8,128)}), f32[16,104,128]{2,1,0:T(8,128)S(1)}, u32[]{:S(2)}, u32[]{:S(2)}) async-start(f32[16,104,128]{2,1,0:T(8,128)} %get-tuple-element.31), calls=%async_computation | async-start | bytes 1703936 | tf_op jit(solution)/shard_map/all_to_all | solution.py:547
  23.7 7.0 %copy-start.2 = (s32[64,4,4]{0,2,1:T(4,128)S(1)}, s32[64,4,4]{0,2,1:T(4,128)}, u32[]{:S(2)}) copy-start(s32[64,4,4]{0,2,1:T(4,128)} %param.19) | copy-start | bytes 12292
  23.7 7.8 %collective-permute-start = (f32[64,128]{1,0:T(8,128)S(1)}, f32[64,128]{1,0:T(8,128)S(1)}, u32[]{:S(2)}, u32[]{:S(2)}) collective-permute-start(f32[64,128]{1,0:T(8,128)S(1)} %get-tuple-element.45), channel_id=1, source_target_pairs={{0,16},{1,17},{2,18},{3,19},{4,20},{5,21},{6,22},{7,23},{8,24},{9,... | collective-permute-start | bytes 98312 | tf_op jit(solution)/shard_map/ppermute | solution.py:514
  24.2 7.3 %collective-permute-start.1 = (f32[64,128]{1,0:T(8,128)S(1)}, f32[64,128]{1,0:T(8,128)S(1)}, u32[]{:S(2)}, u32[]{:S(2)}) collective-permute-start(f32[64,128]{1,0:T(8,128)S(1)} %get-tuple-element.46), channel_id=1, source_target_pairs={{0,1},{1,0},{2,3},{3,2},{4,5},{5,4},{6,7},{7,6},{8,9},{9,8},{10,11... | collective-permute-start | bytes 98312 | tf_op jit(solution)/shard_map/ppermute | solution.py:514
  25.7 5.8 %collective-permute-start.2 = (f32[64,128]{1,0:T(8,128)S(1)}, f32[64,128]{1,0:T(8,128)S(1)}, u32[]{:S(2)}, u32[]{:S(2)}) collective-permute-start(f32[64,128]{1,0:T(8,128)S(1)} %get-tuple-element.47), channel_id=1, source_target_pairs={{0,1},{1,0},{2,3},{3,2},{4,5},{5,4},{6,7},{7,6},{8,9},{9,8},{10,11... | collective-permute-start | bytes 98312 | tf_op jit(solution)/shard_map/ppermute | solution.py:514
  27.9 4.6 %collective-permute-start.3 = (f32[64,128]{1,0:T(8,128)S(1)}, f32[64,128]{1,0:T(8,128)S(1)}, u32[]{:S(2)}, u32[]{:S(2)}) collective-permute-start(f32[64,128]{1,0:T(8,128)S(1)} %get-tuple-element.48), channel_id=1, source_target_pairs={{0,16},{1,2},{2,1},{3,4},{4,3},{5,6},{6,5},{7,8},{8,7},{9,10},{10,... | collective-permute-start | bytes 98312 | tf_op jit(solution)/shard_map/ppermute | solution.py:514
  33.0 5.9 %collective-permute-start.4 = (f32[64,128]{1,0:T(8,128)S(1)}, f32[64,128]{1,0:T(8,128)S(1)}, u32[]{:S(2)}, u32[]{:S(2)}) collective-permute-start(f32[64,128]{1,0:T(8,128)S(1)} %get-tuple-element.56), channel_id=1, source_target_pairs={{0,16},{1,17},{2,18},{3,19},{4,20},{5,21},{6,22},{7,23},{8,24},{9,... | collective-permute-start | bytes 98312 | tf_op jit(solution)/shard_map/ppermute | solution.py:514
  33.1 5.8 %collective-permute-start.5 = (f32[64,128]{1,0:T(8,128)S(1)}, f32[64,128]{1,0:T(8,128)S(1)}, u32[]{:S(2)}, u32[]{:S(2)}) collective-permute-start(f32[64,128]{1,0:T(8,128)S(1)} %get-tuple-element.57), channel_id=1, source_target_pairs={{0,1},{1,0},{2,3},{3,2},{4,5},{5,4},{6,7},{7,6},{8,9},{9,8},{10,11... | collective-permute-start | bytes 98312 | tf_op jit(solution)/shard_map/ppermute | solution.py:514
  34.5 4.4 %collective-permute-start.6 = (f32[64,128]{1,0:T(8,128)S(1)}, f32[64,128]{1,0:T(8,128)S(1)}, u32[]{:S(2)}, u32[]{:S(2)}) collective-permute-start(f32[64,128]{1,0:T(8,128)S(1)} %get-tuple-element.58), channel_id=1, source_target_pairs={{0,1},{1,0},{2,3},{3,2},{4,5},{5,4},{6,7},{7,6},{8,9},{9,8},{10,11... | collective-permute-start | bytes 98312 | tf_op jit(solution)/shard_map/ppermute | solution.py:514
  34.6 4.6 %collective-permute-start.7 = (f32[64,128]{1,0:T(8,128)S(1)}, f32[64,128]{1,0:T(8,128)S(1)}, u32[]{:S(2)}, u32[]{:S(2)}) collective-permute-start(f32[64,128]{1,0:T(8,128)S(1)} %get-tuple-element.59), channel_id=1, source_target_pairs={{0,16},{1,2},{2,1},{3,4},{4,3},{5,6},{6,5},{7,8},{8,7},{9,10},{10,... | collective-permute-start | bytes 98312 | tf_op jit(solution)/shard_map/ppermute | solution.py:514

commit v7 on v6

--- a/solution.py
+++ b/solution.py
@@ -281,10 +281,11 @@
     emit(head_out, cond_out, *outgoing)
 
 
-def later_kernel(recv, settled, wet, less_out, span_out, water_out):
+def later_kernel(recv, settled, wet, alpha, less_out, span_out, water_out, slope_out):
     for ref, value in zip((less_out, span_out), receive(recv, settled, (1, 5))):
         ref[...] = value
     water_out[...] = 4.0 * (less_out[...] + span_out[...] * wet[...])
+    slope_out[...] = 4.0 * span_out[...] * alpha[...]
 
 
 class Table:
@@ -464,11 +465,11 @@
     return sums
 
 
-def newton_kernel(head, alpha, shape_n, sat, cond, span, water, own, flux, total, *refs):
+def newton_kernel(head, alpha, shape_n, sat, cond, slope, water, own, flux, total, *refs):
     incoming, (head_out, cond_out, wet_out, *outgoing), planes = refs[:5], refs[5:12], refs[12]
     flux, total = balance(head, cond, own, (flux, total), *incoming, planes)
     resid = cube(water[...]) - flux
-    diagonal = 4.0 * cube(span[...]) * cube(alpha[...]) + total
+    diagonal = cube(slope[...]) + total
     head_out[...] = (cube(head[...]) - resid / diagonal).reshape(256, 128)
     cond_out[...], wet_out[...] = closure(head_out[...], alpha[...], shape_n[...], sat[...])
     emit(head_out, cond_out, *outgoing)
@@ -554,10 +555,10 @@
     incoming = exchange(*outgoing)
     ghost = shape(2, 128, 128)
     sums = call(inside_kernel, [ghost, cells, cells], [], head, cond, near)
-    less, span, water = call(later_kernel, [cells] * 3, [], recv, settled, wet)
+    less, span, water, slope = call(later_kernel, [cells] * 4, [], recv, settled, wet, alpha)
     planes = [pltpu.VMEM((4, 256, 128), f32)]
     head, cond, wet, *outgoing = call(
-        newton_kernel, [cells] * 3 + halo, planes, head, alpha, shape_n, sat, cond, span, water, *sums, *incoming, near
+        newton_kernel, [cells] * 3 + halo, planes, head, alpha, shape_n, sat, cond, slope, water, *sums, *incoming, near
     )
     incoming = exchange(*outgoing)
     final = shape(1, blocks, 512)

time: 40.5 us -> 40.5 us (level)
  no operation moved by 1% of the time
where the time goes in v7:
time: 40.5 us; the launch traced here: 40.3 us
  starting transfers between devices  19.6 us (48%)
  waiting for transfers between devices  12.3 us (30%)
  Pallas kernels  7.54 us (19%)
  between operations  0.75 us (2%)
    ppermute x8, starting transfers between devices, swap(): return lax.ppermute(x, ('dom', 'depth'), pairs)  11.6 us
    all_to_all x1, waiting for transfers between devices, on_device(): lax.all_to_all(send, 'dom', 0, 0, tiled=True, axis_index_groups=[sorted(r...  10.9 us
    all_to_all x1, starting transfers between devices, on_device(): lax.all_to_all(send, 'dom', 0, 0, tiled=True, axis_index_groups=[sorted(r...  7.94 us
    pallas_call x8, Pallas kernels, call(): pl.pallas_call(kernel, out_shape=outs, in_specs=[whole] * len(operands),...  7.54 us
    ppermute x8, waiting for transfers between devices, swap(): return lax.ppermute(x, ('dom', 'depth'), pairs)  1.38 us
  transfers between devices with their start and end apart: 9, of which 3 were waited for; matrix products, arithmetic and copies ran while one was open for 0% of the time, Pallas kernels for 6%

profile of v7, /device:TPU:99, one launch (start us, length us, event | category | flops | bytes accessed | tf_op | source)
XLA Modules:
  0.0 40.3 jit_solution(1261678813641518179)
XLA Ops:
  0.6 3.0 %shard_map.113 = (f32[24,64,128]{2,1,0:T(8,128)}, f32[16,104,128]{2,1,0:T(8,128)}, f32[64,128]{1,0:T(8,128)}) custom-call(s32[64]{0:T(128)} %refs_0_.1, s32[64]{0:T(128)} %refs_1_.1, f32[1,64,512]{2,1,0:T(8,128)} %refs_2_.1, f32[1,64,512]{2,1,0:T(8,128)} %refs_3_.1, f32[1,64,512]{2,1,0:T(8,128)} %refs_4_.1, f32[1,64,512]{2,1,0:T(8,128)} %refs_5_.1, ...), custom_call_target="tpu_custom_call" | custom-call | tf_op jit(solution)/shard_map/pallas_call | solution.py:496
  3.7 0.0 copy-start
  3.7 0.0 copy-start.1
  3.7 7.9 %all-to-all-start = ((f32[16,104,128]{2,1,0:T(8,128)}), f32[16,104,128]{2,1,0:T(8,128)S(1)}, u32[]{:S(2)}, u32[]{:S(2)}) async-start(f32[16,104,128]{2,1,0:T(8,128)} %get-tuple-element.32), calls=%async_computation | async-start | bytes 1703936 | tf_op jit(solution)/shard_map/all_to_all | solution.py:548
  11.6 0.0 copy-done
  11.6 0.0 copy-done.1
  11.6 0.5 %shard_map.114.settled = f32[6,256,128]{2,1,0:T(8,128)S(1)} custom-call(f32[24,64,128]{2,1,0:T(8,128)S(1)} %copy-done, f32[64,128]{1,0:T(8,128)S(1)} %copy-done.1), custom_call_target="tpu_custom_call" | custom-call | tf_op jit(solution)/shard_map/pallas_call | solution.py:496
  12.2 10.9 %all-to-all-done = f32[16,104,128]{2,1,0:T(8,128)S(1)} async-done(((f32[16,104,128]{2,1,0:T(8,128)}), f32[16,104,128]{2,1,0:T(8,128)S(1)}, u32[]{:S(2)}, u32[]{:S(2)}) %all-to-all-start) | async-done | bytes 852000 | tf_op jit(solution)/shard_map/all_to_all | solution.py:548
  23.1 0.6 %shard_map.115 = (f32[256,128]{1,0:T(8,128)S(1)}, f32[256,128]{1,0:T(8,128)S(1)}, f32[256,128]{1,0:T(8,128)S(1)}, f32[256,128]{1,0:T(8,128)S(1)}, f32[256,128]{1...) custom-call(f32[1664,128]{1,0:T(8,128)S(1)} %bitcast.4, ...), custom_call_target="tpu_custom_call" | custom-call | tf_op jit(solution)/shard_map/pallas_call | solution.py:496
  23.7 0.0 copy-start.2
  23.7 0.5 %collective-permute-start = (f32[64,128]{1,0:T(8,128)S(1)}, f32[64,128]{1,0:T(8,128)S(1)}, u32[]{:S(2)}, u32[]{:S(2)}) collective-permute-start(f32[64,128]{1,0:T(8,128)S(1)} %get-tuple-element.46), channel_id=1, source_target_pairs={{0,16},{1,17},{2,18},{3,19},{4,20},{5,21},{6,22},{7,23},{8,24},{9,... | collective-permute-start | bytes 98312 | tf_op jit(solution)/shard_map/ppermute | solution.py:515
  24.2 1.5 %collective-permute-start.1 = (f32[64,128]{1,0:T(8,128)S(1)}, f32[64,128]{1,0:T(8,128)S(1)}, u32[]{:S(2)}, u32[]{:S(2)}) collective-permute-start(f32[64,128]{1,0:T(8,128)S(1)} %get-tuple-element.47), channel_id=1, source_target_pairs={{0,1},{1,0},{2,3},{3,2},{4,5},{5,4},{6,7},{7,6},{8,9},{9,8},{10,11... | collective-permute-start | bytes 98312 | tf_op jit(solution)/shard_map/ppermute | solution.py:515
  25.7 2.2 %collective-permute-start.2 = (f32[64,128]{1,0:T(8,128)S(1)}, f32[64,128]{1,0:T(8,128)S(1)}, u32[]{:S(2)}, u32[]{:S(2)}) collective-permute-start(f32[64,128]{1,0:T(8,128)S(1)} %get-tuple-element.48), channel_id=1, source_target_pairs={{0,1},{1,0},{2,3},{3,2},{4,5},{5,4},{6,7},{7,6},{8,9},{9,8},{10,11... | collective-permute-start | bytes 98312 | tf_op jit(solution)/shard_map/ppermute | solution.py:515
  27.9 2.7 %collective-permute-start.3 = (f32[64,128]{1,0:T(8,128)S(1)}, f32[64,128]{1,0:T(8,128)S(1)}, u32[]{:S(2)}, u32[]{:S(2)}) collective-permute-start(f32[64,128]{1,0:T(8,128)S(1)} %get-tuple-element.49), channel_id=1, source_target_pairs={{0,16},{1,2},{2,1},{3,4},{4,3},{5,6},{6,5},{7,8},{8,7},{9,10},{10,... | collective-permute-start | bytes 98312 | tf_op jit(solution)/shard_map/ppermute | solution.py:515
  30.7 0.0 copy-done.2
  30.7 0.1 pad_add_fusion.near.refs_4_.table
  30.7 0.3 shard_map.116
  31.0 0.5 %shard_map.117 = (f32[2,128,128]{2,1,0:T(8,128)S(1)}, f32[256,128]{1,0:T(8,128)S(1)}, f32[256,128]{1,0:T(8,128)S(1)}) custom-call(f32[256,128]{1,0:T(8,128)S(1)} %get-tuple-element.35.head_ref.head, f32[256,128]{1,0:T(8,128)S(1)} %get-tuple-element.39.cond_ref.cond, s32[16,128]{1,0:T(8,128)S(1)} %pad_add_fusion.near.refs_4_.table), custom_call_target="tpu_custom_call" | custom-call | tf_op jit(solution)/shard_map/pallas_call | solution.py:496
  31.5 0.0 collective-permute-done.refs_0_
  31.5 0.0 collective-permute-done.1.refs_1_
  31.5 0.0 collective-permute-done.2.refs_2_
  31.5 1.0 %collective-permute-done.3.refs_3_ = f32[64,128]{1,0:T(8,128)S(1)} collective-permute-done((f32[64,128]{1,0:T(8,128)S(1)}, f32[64,128]{1,0:T(8,128)S(1)}, u32[]{:S(2)}, u32[]{:S(2)}) %collective-permute-start.3) | collective-permute-done | bytes 32800 | tf_op jit(solution)/shard_map/ppermute | solution.py:515
  32.5 0.5 %shard_map.118 = (f32[256,128]{1,0:T(8,128)S(1)}, f32[256,128]{1,0:T(8,128)S(1)}, f32[256,128]{1,0:T(8,128)S(1)}, f32[64,128]{1,0:T(8,128)S(1)}, f32[64,128]{1,0...) custom-call(f32[256,128]{1,0:T(8,128)S(1)} %get-tuple-element.35.head_ref.head, ...), custom_call_target="tpu_custom_call" | custom-call | tf_op jit(solution)/shard_map/pallas_call | solution.py:496
  33.0 0.1 collective-permute-start.4
  33.1 1.4 %collective-permute-start.5 = (f32[64,128]{1,0:T(8,128)S(1)}, f32[64,128]{1,0:T(8,128)S(1)}, u32[]{:S(2)}, u32[]{:S(2)}) collective-permute-start(f32[64,128]{1,0:T(8,128)S(1)} %get-tuple-element.59), channel_id=1, source_target_pairs={{0,1},{1,0},{2,3},{3,2},{4,5},{5,4},{6,7},{7,6},{8,9},{9,8},{10,11... | collective-permute-start | bytes 98312 | tf_op jit(solution)/shard_map/ppermute | solution.py:515
  34.5 0.2 collective-permute-start.6
  34.6 3.0 %collective-permute-start.7 = (f32[64,128]{1,0:T(8,128)S(1)}, f32[64,128]{1,0:T(8,128)S(1)}, u32[]{:S(2)}, u32[]{:S(2)}) collective-permute-start(f32[64,128]{1,0:T(8,128)S(1)} %get-tuple-element.61), channel_id=1, source_target_pairs={{0,16},{1,2},{2,1},{3,4},{4,3},{5,6},{6,5},{7,8},{8,7},{9,10},{10,... | collective-permute-start | bytes 98312 | tf_op jit(solution)/shard_map/ppermute | solution.py:515
  37.7 1.2 %shard_map.119 = (f32[2,128,128]{2,1,0:T(8,128)S(1)}, f32[256,128]{1,0:T(8,128)S(1)}, f32[1,64,512]{2,1,0:T(8,128)}) custom-call(f32[256,128]{1,0:T(8,128)S(1)} %get-tuple-element.50.head_ref.head, f32[256,128]{1,0:T(8,128)S(1)} %get-tuple-element.51.cond_ref.cond, s32[16,128]{1,0:T(8,128)S(1)} %pad_add_fusion.near.refs_4_.table), custom_call_target="tpu_custom_call" | custom-call | tf_op jit(solution)/shard_map/pallas_call | solution.py:496
  38.9 0.0 collective-permute-done.4.near_in
  38.9 0.0 collective-permute-done.5.far_in
  38.9 0.0 collective-permute-done.6.core
  38.9 0.4 collective-permute-done.7.chip
  39.3 1.0 %shard_map.120 = f32[1,64,512]{2,1,0:T(8,128)} custom-call(f32[256,128]{1,0:T(8,128)S(1)} %get-tuple-element.50.head_ref.head, f32[256,128]{1,0:T(8,128)S(1)} %get-tuple-element.51.cond_ref.cond, f32[256,128]{1,0:T(8,128)S(1)} %get-tuple-element.53.wet, f32[256,128]{1,0:T(8,128)S(1)} %get-tuple-element.54.less, f32[256,128]{1,0:T(8,128)S(1)} %get-tuple-element.55.span, ...), custom_call_target="tpu_custom_call" | custom-call | tf_op jit(solution)/shard_map/pallas_call | solution.py:496
Async XLA Ops:
  3.7 8.0 %copy-start = (f32[24,64,128]{2,1,0:T(8,128)S(1)}, f32[24,64,128]{2,1,0:T(8,128)}, u32[]{:S(2)}) copy-start(f32[24,64,128]{2,1,0:T(8,128)} %get-tuple-element.33.own) | copy-start | bytes 2359300
  3.7 8.0 %copy-start.1 = (f32[64,128]{1,0:T(8,128)S(1)}, f32[64,128]{1,0:T(8,128)}, u32[]{:S(2)}) copy-start(f32[64,128]{1,0:T(8,128)} %get-tuple-element.34.stay) | copy-start | bytes 98308
  3.7 19.4 %all-to-all-start = ((f32[16,104,128]{2,1,0:T(8,128)}), f32[16,104,128]{2,1,0:T(8,128)S(1)}, u32[]{:S(2)}, u32[]{:S(2)}) async-start(f32[16,104,128]{2,1,0:T(8,128)} %get-tuple-element.32), calls=%async_computation | async-start | bytes 1703936 | tf_op jit(solution)/shard_map/all_to_all | solution.py:548
  23.7 7.0 %copy-start.2 = (s32[64,4,4]{0,2,1:T(4,128)S(1)}, s32[64,4,4]{0,2,1:T(4,128)}, u32[]{:S(2)}) copy-start(s32[64,4,4]{0,2,1:T(4,128)} %param.19) | copy-start | bytes 12292
  23.7 7.8 %collective-permute-start = (f32[64,128]{1,0:T(8,128)S(1)}, f32[64,128]{1,0:T(8,128)S(1)}, u32[]{:S(2)}, u32[]{:S(2)}) collective-permute-start(f32[64,128]{1,0:T(8,128)S(1)} %get-tuple-element.46), channel_id=1, source_target_pairs={{0,16},{1,17},{2,18},{3,19},{4,20},{5,21},{6,22},{7,23},{8,24},{9,... | collective-permute-start | bytes 98312 | tf_op jit(solution)/shard_map/ppermute | solution.py:515
  24.2 7.3 %collective-permute-start.1 = (f32[64,128]{1,0:T(8,128)S(1)}, f32[64,128]{1,0:T(8,128)S(1)}, u32[]{:S(2)}, u32[]{:S(2)}) collective-permute-start(f32[64,128]{1,0:T(8,128)S(1)} %get-tuple-element.47), channel_id=1, source_target_pairs={{0,1},{1,0},{2,3},{3,2},{4,5},{5,4},{6,7},{7,6},{8,9},{9,8},{10,11... | collective-permute-start | bytes 98312 | tf_op jit(solution)/shard_map/ppermute | solution.py:515
  25.7 5.8 %collective-permute-start.2 = (f32[64,128]{1,0:T(8,128)S(1)}, f32[64,128]{1,0:T(8,128)S(1)}, u32[]{:S(2)}, u32[]{:S(2)}) collective-permute-start(f32[64,128]{1,0:T(8,128)S(1)} %get-tuple-element.48), channel_id=1, source_target_pairs={{0,1},{1,0},{2,3},{3,2},{4,5},{5,4},{6,7},{7,6},{8,9},{9,8},{10,11... | collective-permute-start | bytes 98312 | tf_op jit(solution)/shard_map/ppermute | solution.py:515
  27.9 4.6 %collective-permute-start.3 = (f32[64,128]{1,0:T(8,128)S(1)}, f32[64,128]{1,0:T(8,128)S(1)}, u32[]{:S(2)}, u32[]{:S(2)}) collective-permute-start(f32[64,128]{1,0:T(8,128)S(1)} %get-tuple-element.49), channel_id=1, source_target_pairs={{0,16},{1,2},{2,1},{3,4},{4,3},{5,6},{6,5},{7,8},{8,7},{9,10},{10,... | collective-permute-start | bytes 98312 | tf_op jit(solution)/shard_map/ppermute | solution.py:515
  33.0 5.9 %collective-permute-start.4 = (f32[64,128]{1,0:T(8,128)S(1)}, f32[64,128]{1,0:T(8,128)S(1)}, u32[]{:S(2)}, u32[]{:S(2)}) collective-permute-start(f32[64,128]{1,0:T(8,128)S(1)} %get-tuple-element.58), channel_id=1, source_target_pairs={{0,16},{1,17},{2,18},{3,19},{4,20},{5,21},{6,22},{7,23},{8,24},{9,... | collective-permute-start | bytes 98312 | tf_op jit(solution)/shard_map/ppermute | solution.py:515
  33.1 5.8 %collective-permute-start.5 = (f32[64,128]{1,0:T(8,128)S(1)}, f32[64,128]{1,0:T(8,128)S(1)}, u32[]{:S(2)}, u32[]{:S(2)}) collective-permute-start(f32[64,128]{1,0:T(8,128)S(1)} %get-tuple-element.59), channel_id=1, source_target_pairs={{0,1},{1,0},{2,3},{3,2},{4,5},{5,4},{6,7},{7,6},{8,9},{9,8},{10,11... | collective-permute-start | bytes 98312 | tf_op jit(solution)/shard_map/ppermute | solution.py:515
  34.5 4.4 %collective-permute-start.6 = (f32[64,128]{1,0:T(8,128)S(1)}, f32[64,128]{1,0:T(8,128)S(1)}, u32[]{:S(2)}, u32[]{:S(2)}) collective-permute-start(f32[64,128]{1,0:T(8,128)S(1)} %get-tuple-element.60), channel_id=1, source_target_pairs={{0,1},{1,0},{2,3},{3,2},{4,5},{5,4},{6,7},{7,6},{8,9},{9,8},{10,11... | collective-permute-start | bytes 98312 | tf_op jit(solution)/shard_map/ppermute | solution.py:515
  34.6 4.6 %collective-permute-start.7 = (f32[64,128]{1,0:T(8,128)S(1)}, f32[64,128]{1,0:T(8,128)S(1)}, u32[]{:S(2)}, u32[]{:S(2)}) collective-permute-start(f32[64,128]{1,0:T(8,128)S(1)} %get-tuple-element.61), channel_id=1, source_target_pairs={{0,16},{1,2},{2,1},{3,4},{4,3},{5,6},{6,5},{7,8},{8,7},{9,10},{10,... | collective-permute-start | bytes 98312 | tf_op jit(solution)/shard_map/ppermute | solution.py:515
